TPU v7x, 32 devices: a whole 2x2x4 slice. The times are simulated.
32 devices in a mesh: groups: 2 (over x), seq: 16 (over z, y, core).
Axes of the slice: x: 2, y: 2, z: 4, core: 2. Of those that a mesh axis runs over, the one named last changes fastest.
Arguments:
- queries: bfloat16 [4096, 2560], P(('groups', 'seq')), parts along dimension 0, may hold values from -25 to 25
- keys: bfloat16 [4096, 512], P(('groups', 'seq')), parts along dimension 0, may hold values from -4 to 4
- values: bfloat16 [4096, 512], P(('groups', 'seq')), parts along dimension 0, may hold values from -6 to 6
- out_grad: bfloat16 [4096, 2560], P(('groups', 'seq')), parts along dimension 0, may hold values from -6 to 6
Outputs:
- query_grad: bfloat16 [4096, 2560], P(('groups', 'seq')), parts along dimension 0
- key_grad: bfloat16 [4096, 512], P(('groups', 'seq')), parts along dimension 0
- value_grad: bfloat16 [4096, 512], P(('groups', 'seq')), parts along dimension 0
There are 2 independent parts, one for each index of `groups`. A program takes and returns all parts, laid end to end along the dimension named above; each array names one. Nothing has to cross between parts.
All inputs are finite; a program needn't handle non-finite values.
Results may differ from a plain program's by a relative error of at most 0.005.
Values may be sent and summed in bfloat16 or wider, within the bound.
No kernel may reach another device: no remote copies, remote signals or barrier semaphores. Data moves between devices by JAX's collectives and lax.ppermute only.
A program may use at most 256 MiB of HBM per device.

v0:
```python
from functools import reduce

import jax
import jax.numpy as jnp
from jax import lax
from jax.sharding import PartitionSpec as P

DH = 128
KVH = 4
QPG = 5


def add_pair(first_term, second_term):
    return first_term + second_term


def per_device(queries, keys, values, out_grad):
    devices = lax.axis_size("seq")
    subgroup = devices // KVH
    tokens_here = queries.shape[0]
    run_count = tokens_here // subgroup
    device = lax.axis_index("seq")
    stride_phase = device % subgroup

    def to_heads(array):
        shaped = array.reshape(run_count, subgroup, KVH, QPG * DH).transpose(2, 1, 0, 3)
        return shaped.reshape(KVH * subgroup * run_count, QPG * DH)

    query_rows, grad_rows = (
        lax.all_to_all(to_heads(queries), "seq", split_axis=0, concat_axis=0, tiled=True),
        lax.all_to_all(to_heads(out_grad), "seq", split_axis=0, concat_axis=0, tiled=True),
    )

    def spread(array):
        heads = array.reshape(tokens_here, KVH, DH).transpose(1, 0, 2)[:, None]
        copies = jnp.broadcast_to(heads, (KVH, subgroup, tokens_here, DH))
        return copies.reshape(KVH * subgroup * tokens_here, DH)

    key_head, value_head = (
        lax.all_to_all(spread(keys), "seq", split_axis=0, concat_axis=0, tiled=True),
        lax.all_to_all(spread(values), "seq", split_axis=0, concat_axis=0, tiled=True),
    )
    key_count = key_head.shape[0]
    query_count = query_rows.shape[0]
    blocks = 16
    tile_rows = query_count // blocks
    width = key_count // blocks
    scaling = DH ** (-0.5)
    query_tiles = query_rows.reshape(query_count, QPG, DH)
    grad_tiles = grad_rows.reshape(query_count, QPG, DH)
    score_pieces = [[] for column in range(blocks)]
    prob_pieces = [[] for column in range(blocks)]
    for block in range(blocks):
        first = block * tile_rows
        reach = width * (block + 1)
        query_tile = query_tiles[first : first + tile_rows]
        grad_tile = grad_tiles[first : first + tile_rows]
        scores = (
            jnp.einsum(
                "nhd,kd->hnk", query_tile, key_head[:reach], preferred_element_type=jnp.float32
            )
            * scaling
        )
        grad_probs = jnp.einsum(
            "nhd,kd->hnk", grad_tile, value_head[:reach], preferred_element_type=jnp.float32
        )
        key_place = jnp.arange(reach, dtype=jnp.int32)
        query_place = subgroup * (first + jnp.arange(tile_rows, dtype=jnp.int32)) + stride_phase
        causal = key_place[None, None, :] <= query_place[None, :, None]
        row_max = jnp.max(jnp.where(causal, scores, -jnp.inf), axis=2, keepdims=True)
        weights = jnp.where(causal, jnp.exp(scores - row_max), 0.0)
        total = jnp.sum(weights, axis=2, keepdims=True)
        weighted = jnp.sum(weights * grad_probs, axis=2, keepdims=True)
        row_delta = weighted / total
        for column in range(block + 1):
            lower = column * width
            part_probs = weights[:, :, lower : lower + width] / total
            prob_pieces[column].append(part_probs.astype(jnp.bfloat16))
            part_grads = (
                part_probs * (grad_probs[:, :, lower : lower + width] - row_delta) * scaling
            )
            score_pieces[column].append(part_grads.astype(jnp.bfloat16))
    query_sums = [[] for block in range(blocks)]
    key_blocks = []
    value_blocks = []
    for column in range(blocks):
        start = column * tile_rows
        grads_here = jnp.concatenate(score_pieces[column], axis=1)
        probs_here = jnp.concatenate(prob_pieces[column], axis=1)
        key_block = key_head[column * width : (column + 1) * width]
        key_blocks.append(
            jnp.einsum(
                "hnk,nhd->kd", grads_here, query_tiles[start:], preferred_element_type=jnp.float32
            )
        )
        value_blocks.append(
            jnp.einsum(
                "hnk,nhd->kd", probs_here, grad_tiles[start:], preferred_element_type=jnp.float32
            )
        )
        query_piece = jnp.einsum(
            "hnk,kd->nhd", grads_here, key_block, preferred_element_type=jnp.float32
        )
        for block in range(column, blocks):
            offset = (block - column) * tile_rows
            query_sums[block].append(query_piece[offset : offset + tile_rows])
    query_parts = [
        reduce(add_pair, query_sums[block]).astype(jnp.bfloat16).reshape(tile_rows, QPG * DH)
        for block in range(blocks)
    ]
    query_local = jnp.concatenate(query_parts, axis=0)
    key_accum = jnp.concatenate(key_blocks, axis=0)
    value_accum = jnp.concatenate(value_blocks, axis=0)
    returned = lax.all_to_all(query_local, "seq", split_axis=0, concat_axis=0, tiled=True)
    query_grad = (
        returned.reshape(KVH, subgroup, run_count, QPG * DH)
        .transpose(2, 1, 0, 3)
        .reshape(tokens_here, KVH * QPG * DH)
    )
    key_parts, value_parts = (
        lax.all_to_all(key_accum, "seq", split_axis=0, concat_axis=0, tiled=True),
        lax.all_to_all(value_accum, "seq", split_axis=0, concat_axis=0, tiled=True),
    )

    def fold_parts(array):
        summed = array.reshape(KVH, subgroup, tokens_here, DH).sum(axis=1)
        return summed.transpose(1, 0, 2).reshape(tokens_here, KVH * DH).astype(jnp.bfloat16)

    return (query_grad, fold_parts(key_parts), fold_parts(value_parts))


def solution(mesh):
    return jax.shard_map(
        per_device,
        mesh=mesh,
        in_specs=(
            P(("groups", "seq"), None),
            P(("groups", "seq"), None),
            P(("groups", "seq"), None),
            P(("groups", "seq"), None),
        ),
        out_specs=(
            P(("groups", "seq"), None),
            P(("groups", "seq"), None),
            P(("groups", "seq"), None),
        ),
        check_vma=False,
    )
```

profile of v0, /device:TPU:9, one launch (start us, length us, event | category | flops | bytes accessed | tf_op | source)
XLA Modules:
  0.0 292.2 jit_solution(14032343443544697038)
XLA Ops:
  0.6 1.0 reshape.935
  2.5 6.6 %all-to-all-start.2 = ((bf16[16,128,128]{2,1,0:T(8,128)(2,1)}), bf16[16,128,128]{2,1,0:T(8,128)(2,1)S(1)}, u32[]{:S(2)}, u32[]{:S(2)}) async-start(bf16[16,128,128]{2,1,0:T(8,128)(2,1)} %bitcast.8), calls=%async_computation.2 | async-start | bytes 1048576 | tf_op jit(solution)/shard_map/all_to_all | solution.py:41
  14.2 9.1 %all-to-all-done.2 = bf16[16,128,128]{2,1,0:T(8,128)(2,1)S(1)} async-done(((bf16[16,128,128]{2,1,0:T(8,128)(2,1)}), bf16[16,128,128]{2,1,0:T(8,128)(2,1)S(1)}, u32[]{:S(2)}, u32[]{:S(2)}) %all-to-all-start.2) | async-done | bytes 524320 | tf_op jit(solution)/shard_map/all_to_all | solution.py:41
  23.3 1.0 broadcast_in_dim.381
  24.3 4.4 %all-to-all-start = ((bf16[16,128,128]{2,1,0:T(8,128)(2,1)}), bf16[16,128,128]{2,1,0:T(8,128)(2,1)S(1)}, u32[]{:S(2)}, u32[]{:S(2)}) async-start(bf16[16,128,128]{2,1,0:T(8,128)(2,1)} %bitcast.1), calls=%async_computation | async-start | bytes 1048576 | tf_op jit(solution)/shard_map/all_to_all | solution.py:40
  29.5 1.0 copy.297
  30.6 1.0 copy.294
  31.8 11.0 %all-to-all-done = bf16[16,128,128]{2,1,0:T(8,128)(2,1)S(1)} async-done(((bf16[16,128,128]{2,1,0:T(8,128)(2,1)}), bf16[16,128,128]{2,1,0:T(8,128)(2,1)S(1)}, u32[]{:S(2)}, u32[]{:S(2)}) %all-to-all-start) | async-done | bytes 524320 | tf_op jit(solution)/shard_map/all_to_all | solution.py:40
  42.9 4.4 %all-to-all-start.3 = ((bf16[16,32,640]{2,1,0:T(8,128)(2,1)}), bf16[16,32,640]{2,1,0:T(8,128)(2,1)S(1)}, u32[]{:S(2)}, u32[]{:S(2)}) async-start(bf16[16,32,640]{2,1,0:T(8,128)(2,1)} %bitcast.12), calls=%async_computation.3 | async-start | bytes 1310720 | tf_op jit(solution)/shard_map/all_to_all | solution.py:31
  48.2 16.0 %all-to-all-done.3 = bf16[16,32,640]{2,1,0:T(8,128)(2,1)S(1)} async-done(((bf16[16,32,640]{2,1,0:T(8,128)(2,1)}), bf16[16,32,640]{2,1,0:T(8,128)(2,1)S(1)}, u32[]{:S(2)}, u32[]{:S(2)}) %all-to-all-start.3) | async-done | bytes 655392 | tf_op jit(solution)/shard_map/all_to_all | solution.py:31
  64.2 4.7 %all-to-all-start.1 = ((bf16[16,32,640]{2,1,0:T(8,128)(2,1)}), bf16[16,32,640]{2,1,0:T(8,128)(2,1)S(1)}, u32[]{:S(2)}, u32[]{:S(2)}) async-start(bf16[16,32,640]{2,1,0:T(8,128)(2,1)} %bitcast.5), calls=%async_computation.1 | async-start | bytes 1310720 | tf_op jit(solution)/shard_map/all_to_all | solution.py:30
  69.3 16.3 %all-to-all-done.1 = bf16[16,32,640]{2,1,0:T(8,128)(2,1)S(1)} async-done(((bf16[16,32,640]{2,1,0:T(8,128)(2,1)}), bf16[16,32,640]{2,1,0:T(8,128)(2,1)S(1)}, u32[]{:S(2)}, u32[]{:S(2)}) %all-to-all-start.1) | async-done | bytes 655392 | tf_op jit(solution)/shard_map/all_to_all | solution.py:30
  99.7 1.2 fusion.37
  118.5 1.0 fusion.712
  140.5 4.5 %all-to-all-start.4 = ((bf16[16,32,640]{2,1,0:T(8,128)(2,1)}), bf16[16,32,640]{2,1,0:T(8,128)(2,1)S(1)}, u32[]{:S(2)}, u32[]{:S(2)}) async-start(bf16[16,32,640]{2,1,0:T(8,128)(2,1)} %bitcast.585), calls=%async_computation.4 | async-start | bytes 1310720 | tf_op jit(solution)/shard_map/all_to_all | solution.py:114
  145.0 1.7 reshape.955
  146.7 2.4 fusion.113
  150.0 2.5 slice.2469
  153.4 2.5 slice.2471
  156.7 2.4 slice.2473
  159.9 2.4 slice.2475
  163.1 2.5 slice.2477
  166.4 2.3 slice.2479
  169.5 2.2 slice.2481
  172.5 2.2 slice.2483
  175.4 2.1 slice.2485
  177.5 1.1 slice.2487
  178.6 1.0 slice.2489
  182.2 1.6 slice.2497
  183.9 1.6 slice.2499
  185.5 2.5 fusion.112
  188.0 2.2 fusion.111
  190.2 1.0 fusion.110
  191.2 1.0 fusion.109
  192.2 0.9 fusion.108
  193.1 2.0 fusion.107
  195.2 0.9 fusion.106
  201.6 1.8 reshape.957
  203.4 2.4 fusion.100
  205.8 2.2 fusion.99
  207.9 1.0 fusion.98
  209.8 0.9 constant_dynamic-update-slice_fusion.266
  215.8 1.5 slice.2501
  217.3 1.7 slice.2503
  219.0 1.4 slice.2505
  220.4 1.3 slice.2507
  221.8 1.2 slice.2509
  223.9 2.3 fusion.97
  226.2 2.1 fusion.96
  228.3 0.9 fusion.95
  229.2 0.9 fusion.94
  230.1 6.1 %all-to-all-start.5 = ((f32[16,128,128]{2,1,0:T(8,128)}), f32[16,128,128]{2,1,0:T(8,128)}, u32[]{:S(2)}, u32[]{:S(2)}) async-start(f32[16,128,128]{2,1,0:T(8,128)} %bitcast.169), calls=%async_computation.5 | async-start | bytes 2097152 | tf_op jit(solution)/shard_map/all_to_all | solution.py:121
  236.3 1.9 fusion.93
  239.0 1.3 slice.2511
  241.1 2.1 slice.2513
  243.1 1.0 slice.2515
  244.2 1.0 slice.2517
  247.1 2.0 fusion.92
  249.0 2.0 fusion.116
  251.1 1.9 fusion.115
  257.4 3.9 %all-to-all-done.5 = f32[16,128,128]{2,1,0:T(8,128)} async-done(((f32[16,128,128]{2,1,0:T(8,128)}), f32[16,128,128]{2,1,0:T(8,128)}, u32[]{:S(2)}, u32[]{:S(2)}) %all-to-all-start.5) | async-done | bytes 1048608 | tf_op jit(solution)/shard_map/all_to_all | solution.py:121
  261.2 5.0 %all-to-all-start.6 = ((f32[16,128,128]{2,1,0:T(8,128)}), f32[16,128,128]{2,1,0:T(8,128)S(1)}, u32[]{:S(2)}, u32[]{:S(2)}) async-start(f32[16,128,128]{2,1,0:T(8,128)} %bitcast.189), calls=%async_computation.6 | async-start | bytes 2097152 | tf_op jit(solution)/shard_map/all_to_all | solution.py:122
  267.6 1.3 bitcast_reduce_fusion.1
  269.8 21.2 %all-to-all-done.6 = f32[16,128,128]{2,1,0:T(8,128)S(1)} async-done(((f32[16,128,128]{2,1,0:T(8,128)}), f32[16,128,128]{2,1,0:T(8,128)S(1)}, u32[]{:S(2)}, u32[]{:S(2)}) %all-to-all-start.6) | async-done | bytes 1048608 | tf_op jit(solution)/shard_map/all_to_all | solution.py:122
  (585 shorter events, 92.8 us)
Async XLA Ops:
  0.6 8.6 %copy-start.89 = (bf16[128,512]{1,0:T(8,128)(2,1)S(1)}, bf16[128,512]{1,0:T(8,128)(2,1)}, u32[]{:S(2)}) copy-start(bf16[128,512]{1,0:T(8,128)(2,1)} %param.5) | copy-start | bytes 393220
  2.5 20.8 %all-to-all-start.2 = ((bf16[16,128,128]{2,1,0:T(8,128)(2,1)}), bf16[16,128,128]{2,1,0:T(8,128)(2,1)S(1)}, u32[]{:S(2)}, u32[]{:S(2)}) async-start(bf16[16,128,128]{2,1,0:T(8,128)(2,1)} %bitcast.8), calls=%async_computation.2 | async-start | bytes 1048576 | tf_op jit(solution)/shard_map/all_to_all | solution.py:41
  9.2 20.1 %copy-start.32 = (bf16[128,2560]{1,0:T(8,128)(2,1)S(1)}, bf16[128,2560]{1,0:T(8,128)(2,1)}, u32[]{:S(2)}) copy-start(bf16[128,2560]{1,0:T(8,128)(2,1)} %param.7) | copy-start | bytes 1966084
  23.3 45.8 %copy-start.2 = (bf16[16,128,128]{2,1,0:T(8,128)(2,1)}, bf16[16,128,128]{2,1,0:T(8,128)(2,1)S(1)}, u32[]{:S(2)}) copy-start(bf16[16,128,128]{2,1,0:T(8,128)(2,1)S(1)} %all-to-all-done.2) | copy-start | bytes 1572868
  24.3 18.6 %all-to-all-start = ((bf16[16,128,128]{2,1,0:T(8,128)(2,1)}), bf16[16,128,128]{2,1,0:T(8,128)(2,1)S(1)}, u32[]{:S(2)}, u32[]{:S(2)}) async-start(bf16[16,128,128]{2,1,0:T(8,128)(2,1)} %bitcast.1), calls=%async_computation | async-start | bytes 1048576 | tf_op jit(solution)/shard_map/all_to_all | solution.py:40
  42.9 26.3 %copy-start = (bf16[16,128,128]{2,1,0:T(8,128)(2,1)}, bf16[16,128,128]{2,1,0:T(8,128)(2,1)S(1)}, u32[]{:S(2)}) copy-start(bf16[16,128,128]{2,1,0:T(8,128)(2,1)S(1)} %all-to-all-done) | copy-start | bytes 1572868
  42.9 21.3 %all-to-all-start.3 = ((bf16[16,32,640]{2,1,0:T(8,128)(2,1)}), bf16[16,32,640]{2,1,0:T(8,128)(2,1)S(1)}, u32[]{:S(2)}, u32[]{:S(2)}) async-start(bf16[16,32,640]{2,1,0:T(8,128)(2,1)} %bitcast.12), calls=%async_computation.3 | async-start | bytes 1310720 | tf_op jit(solution)/shard_map/all_to_all | solution.py:31
  64.2 21.4 %all-to-all-start.1 = ((bf16[16,32,640]{2,1,0:T(8,128)(2,1)}), bf16[16,32,640]{2,1,0:T(8,128)(2,1)S(1)}, u32[]{:S(2)}, u32[]{:S(2)}) async-start(bf16[16,32,640]{2,1,0:T(8,128)(2,1)} %bitcast.5), calls=%async_computation.1 | async-start | bytes 1310720 | tf_op jit(solution)/shard_map/all_to_all | solution.py:30
  90.5 8.8 %slice-start.14 = ((bf16[16,128,128]{2,1,0:T(8,128)(2,1)}), bf16[11,128,128]{2,1,0:T(8,128)(2,1)S(1)}, s32[]{:S(2)}) async-start(bf16[16,128,128]{2,1,0:T(8,128)(2,1)} %copy-done.2), calls=%async_computation.21 | async-start | bytes 720896 | tf_op jit(solution)/shard_map/slice | solution.py:65
  95.7 3.9 %slice-start = ((bf16[16,128,128]{2,1,0:T(8,128)(2,1)}), bf16[11,128,128]{2,1,0:T(8,128)(2,1)S(1)}, s32[]{:S(2)}) async-start(bf16[16,128,128]{2,1,0:T(8,128)(2,1)} %copy-done), calls=%async_computation.7 | async-start | bytes 720896 | tf_op jit(solution)/shard_map/slice | solution.py:60
  99.3 20.5 %copy-start.53 = (bf16[32,5,128]{2,1,0:T(8,128)(2,1)}, bf16[32,5,128]{2,1,0:T(8,128)(2,1)S(1)}, u32[]{:S(2)}) copy-start(bf16[32,5,128]{2,1,0:T(8,128)(2,1)S(1)} %slice.2058) | copy-start | bytes 122884
  112.5 19.1 %copy-start.8 = (f32[5,32,1536]{2,1,0:T(8,128)}, f32[5,32,1536]{2,1,0:T(8,128)S(1)}, u32[]{:S(2)}) copy-start(f32[5,32,1536]{2,1,0:T(8,128)S(1)} %get-tuple-element.388) | copy-start | bytes 2949124
  114.6 19.9 %copy-start.10 = (f32[5,32,1664]{2,1,0:T(8,128)}, f32[5,32,1664]{2,1,0:T(8,128)S(1)}, u32[]{:S(2)}) copy-start(f32[5,32,1664]{2,1,0:T(8,128)S(1)} %get-tuple-element.389) | copy-start | bytes 3194884
  116.7 17.9 %copy-start.6 = (f32[5,32,1792]{2,1,0:T(8,128)}, f32[5,32,1792]{2,1,0:T(8,128)S(1)}, u32[]{:S(2)}) copy-start(f32[5,32,1792]{2,1,0:T(8,128)S(1)} %get-tuple-element.390) | copy-start | bytes 3440644
  119.5 15.4 %copy-start.4 = (f32[5,32,1920]{2,1,0:T(8,128)}, f32[5,32,1920]{2,1,0:T(8,128)S(1)}, u32[]{:S(2)}) copy-start(f32[5,32,1920]{2,1,0:T(8,128)S(1)} %get-tuple-element.391) | copy-start | bytes 3686404
  121.6 16.6 %copy-start.112 = (bf16[5,32,128]{2,1,0:T(8,128)(2,1)}, bf16[5,32,128]{2,1,0:T(8,128)(2,1)S(1)}, u32[]{:S(2)}) copy-start(bf16[5,32,128]{2,1,0:T(8,128)(2,1)S(1)} %get-tuple-element.161) | copy-start | bytes 122884
  121.6 17.0 %copy-start.85 = (bf16[5,32,128]{2,1,0:T(8,128)(2,1)}, bf16[5,32,128]{2,1,0:T(8,128)(2,1)S(1)}, u32[]{:S(2)}) copy-start(bf16[5,32,128]{2,1,0:T(8,128)(2,1)S(1)} %get-tuple-element.162) | copy-start | bytes 122884
  121.6 17.3 %copy-start.83 = (bf16[5,32,128]{2,1,0:T(8,128)(2,1)}, bf16[5,32,128]{2,1,0:T(8,128)(2,1)S(1)}, u32[]{:S(2)}) copy-start(bf16[5,32,128]{2,1,0:T(8,128)(2,1)S(1)} %get-tuple-element.163) | copy-start | bytes 122884
  121.6 17.9 %copy-start.49 = (bf16[5,32,128]{2,1,0:T(8,128)(2,1)}, bf16[5,32,128]{2,1,0:T(8,128)(2,1)S(1)}, u32[]{:S(2)}) copy-start(bf16[5,32,128]{2,1,0:T(8,128)(2,1)S(1)} %get-tuple-element.164) | copy-start | bytes 122884
  122.4 15.8 %copy-start.100 = (bf16[5,32,128]{2,1,0:T(8,128)(2,1)}, bf16[5,32,128]{2,1,0:T(8,128)(2,1)S(1)}, u32[]{:S(2)}) copy-start(bf16[5,32,128]{2,1,0:T(8,128)(2,1)S(1)} %get-tuple-element.182) | copy-start | bytes 122884
  122.4 16.2 %copy-start.79 = (bf16[5,32,128]{2,1,0:T(8,128)(2,1)}, bf16[5,32,128]{2,1,0:T(8,128)(2,1)S(1)}, u32[]{:S(2)}) copy-start(bf16[5,32,128]{2,1,0:T(8,128)(2,1)S(1)} %get-tuple-element.183) | copy-start | bytes 122884
  122.4 16.6 %copy-start.77 = (bf16[5,32,128]{2,1,0:T(8,128)(2,1)}, bf16[5,32,128]{2,1,0:T(8,128)(2,1)S(1)}, u32[]{:S(2)}) copy-start(bf16[5,32,128]{2,1,0:T(8,128)(2,1)S(1)} %get-tuple-element.184) | copy-start | bytes 122884
  123.2 15.1 %copy-start.107 = (bf16[5,32,128]{2,1,0:T(8,128)(2,1)}, bf16[5,32,128]{2,1,0:T(8,128)(2,1)S(1)}, u32[]{:S(2)}) copy-start(bf16[5,32,128]{2,1,0:T(8,128)(2,1)S(1)} %get-tuple-element.207) | copy-start | bytes 122884
  123.2 15.5 %copy-start.81 = (bf16[5,32,128]{2,1,0:T(8,128)(2,1)}, bf16[5,32,128]{2,1,0:T(8,128)(2,1)S(1)}, u32[]{:S(2)}) copy-start(bf16[5,32,128]{2,1,0:T(8,128)(2,1)S(1)} %get-tuple-element.208) | copy-start | bytes 122884
  123.9 14.4 %copy-start.103 = (bf16[5,32,128]{2,1,0:T(8,128)(2,1)}, bf16[5,32,128]{2,1,0:T(8,128)(2,1)S(1)}, u32[]{:S(2)}) copy-start(bf16[5,32,128]{2,1,0:T(8,128)(2,1)S(1)} %get-tuple-element.224) | copy-start | bytes 122884
  133.3 3.7 %copy-start.36 = (bf16[5,416,128]{2,1,0:T(8,128)(2,1)}, bf16[5,416,128]{2,1,0:T(8,128)(2,1)S(1)}, u32[]{:S(2)}) copy-start(bf16[5,416,128]{2,1,0:T(8,128)(2,1)S(1)} %get-tuple-element.62) | copy-start | bytes 1597444
  140.5 89.6 %all-to-all-start.4 = ((bf16[16,32,640]{2,1,0:T(8,128)(2,1)}), bf16[16,32,640]{2,1,0:T(8,128)(2,1)S(1)}, u32[]{:S(2)}, u32[]{:S(2)}) async-start(bf16[16,32,640]{2,1,0:T(8,128)(2,1)} %bitcast.585), calls=%async_computation.4 | async-start | bytes 1310720 | tf_op jit(solution)/shard_map/all_to_all | solution.py:114
  185.5 4.7 %copy-start.25 = (bf16[416,5,128]{2,1,0:T(8,128)(2,1)S(1)}, bf16[416,5,128]{2,1,0:T(8,128)(2,1)}, u32[]{:S(2)}) copy-start(bf16[416,5,128]{2,1,0:T(8,128)(2,1)} %slice.2473) | copy-start | bytes 1597444
  185.5 4.7 %copy-start.37 = (bf16[5,416,128]{2,1,0:T(8,128)(2,1)S(1)}, bf16[5,416,128]{2,1,0:T(8,128)(2,1)}, u32[]{:S(2)}) copy-start(bf16[5,416,128]{2,1,0:T(8,128)(2,1)} %copy-done.36) | copy-start | bytes 1597444
  191.2 4.0 %copy-start.38 = (bf16[288,5,128]{2,1,0:T(8,128)(2,1)S(1)}, bf16[288,5,128]{2,1,0:T(8,128)(2,1)}, u32[]{:S(2)}) copy-start(bf16[288,5,128]{2,1,0:T(8,128)(2,1)} %slice.2481) | copy-start | bytes 1105924
  191.2 4.0 %copy-start.45 = (bf16[5,288,128]{2,1,0:T(8,128)(2,1)S(1)}, bf16[5,288,128]{2,1,0:T(8,128)(2,1)}, u32[]{:S(2)}) copy-start(bf16[5,288,128]{2,1,0:T(8,128)(2,1)} %copy-done.44) | copy-start | bytes 1105924
  192.2 4.0 %copy-start.17 = (bf16[5,256,128]{2,1,0:T(8,128)(2,1)S(1)}, bf16[5,256,128]{2,1,0:T(8,128)(2,1)}, u32[]{:S(2)}) copy-start(bf16[5,256,128]{2,1,0:T(8,128)(2,1)} %copy-done.16) | copy-start | bytes 983044
  192.2 4.0 %copy-start.18 = (bf16[256,5,128]{2,1,0:T(8,128)(2,1)S(1)}, bf16[256,5,128]{2,1,0:T(8,128)(2,1)}, u32[]{:S(2)}) copy-start(bf16[256,5,128]{2,1,0:T(8,128)(2,1)} %slice.2483) | copy-start | bytes 983044
  193.1 4.0 %copy-start.20 = (bf16[5,224,128]{2,1,0:T(8,128)(2,1)S(1)}, bf16[5,224,128]{2,1,0:T(8,128)(2,1)}, u32[]{:S(2)}) copy-start(bf16[5,224,128]{2,1,0:T(8,128)(2,1)} %copy-done.19) | copy-start | bytes 860164
  193.1 4.0 %copy-start.21 = (bf16[224,5,128]{2,1,0:T(8,128)(2,1)S(1)}, bf16[224,5,128]{2,1,0:T(8,128)(2,1)}, u32[]{:S(2)}) copy-start(bf16[224,5,128]{2,1,0:T(8,128)(2,1)} %slice.2485) | copy-start | bytes 860164
  195.2 3.8 %copy-start.55 = (bf16[160,5,128]{2,1,0:T(8,128)(2,1)S(1)}, bf16[160,5,128]{2,1,0:T(8,128)(2,1)}, u32[]{:S(2)}) copy-start(bf16[160,5,128]{2,1,0:T(8,128)(2,1)} %slice.2489) | copy-start | bytes 614404
  195.2 3.8 %copy-start.58 = (bf16[5,160,128]{2,1,0:T(8,128)(2,1)S(1)}, bf16[5,160,128]{2,1,0:T(8,128)(2,1)}, u32[]{:S(2)}) copy-start(bf16[5,160,128]{2,1,0:T(8,128)(2,1)} %copy-done.57) | copy-start | bytes 614404
  196.1 3.7 %copy-start.59 = (bf16[128,5,128]{2,1,0:T(8,128)(2,1)S(1)}, bf16[128,5,128]{2,1,0:T(8,128)(2,1)}, u32[]{:S(2)}) copy-start(bf16[128,5,128]{2,1,0:T(8,128)(2,1)} %slice.2491) | copy-start | bytes 491524
  196.1 3.7 %copy-start.101 = (bf16[5,32,128]{2,1,0:T(8,128)(2,1)S(1)}, bf16[5,32,128]{2,1,0:T(8,128)(2,1)}, u32[]{:S(2)}) copy-start(bf16[5,32,128]{2,1,0:T(8,128)(2,1)} %copy-done.100) | copy-start | bytes 122884
  196.1 3.7 %copy-start.104 = (bf16[5,32,128]{2,1,0:T(8,128)(2,1)S(1)}, bf16[5,32,128]{2,1,0:T(8,128)(2,1)}, u32[]{:S(2)}) copy-start(bf16[5,32,128]{2,1,0:T(8,128)(2,1)} %copy-done.103) | copy-start | bytes 122884
  196.2 3.7 %copy-start.108 = (bf16[5,32,128]{2,1,0:T(8,128)(2,1)S(1)}, bf16[5,32,128]{2,1,0:T(8,128)(2,1)}, u32[]{:S(2)}) copy-start(bf16[5,32,128]{2,1,0:T(8,128)(2,1)} %copy-done.107) | copy-start | bytes 122884
  196.2 3.7 %copy-start.113 = (bf16[5,32,128]{2,1,0:T(8,128)(2,1)S(1)}, bf16[5,32,128]{2,1,0:T(8,128)(2,1)}, u32[]{:S(2)}) copy-start(bf16[5,32,128]{2,1,0:T(8,128)(2,1)} %copy-done.112) | copy-start | bytes 122884
  203.4 4.6 %copy-start.23 = (bf16[448,5,128]{2,1,0:T(8,128)(2,1)S(1)}, bf16[448,5,128]{2,1,0:T(8,128)(2,1)}, u32[]{:S(2)}) copy-start(bf16[448,5,128]{2,1,0:T(8,128)(2,1)} %slice.2499) | copy-start | bytes 1720324
  203.4 4.6 %copy-start.127 = (bf16[5,448,128]{2,1,0:T(8,128)(2,1)S(1)}, bf16[5,448,128]{2,1,0:T(8,128)(2,1)}, u32[]{:S(2)}) copy-start(bf16[5,448,128]{2,1,0:T(8,128)(2,1)} %copy-done.126) | copy-start | bytes 1720324
  223.0 5.2 %copy-start.29 = (bf16[352,5,128]{2,1,0:T(8,128)(2,1)S(1)}, bf16[352,5,128]{2,1,0:T(8,128)(2,1)}, u32[]{:S(2)}) copy-start(bf16[352,5,128]{2,1,0:T(8,128)(2,1)} %slice.2505) | copy-start | bytes 1351684
  223.0 5.2 %copy-start.124 = (bf16[5,352,128]{2,1,0:T(8,128)(2,1)S(1)}, bf16[5,352,128]{2,1,0:T(8,128)(2,1)}, u32[]{:S(2)}) copy-start(bf16[5,352,128]{2,1,0:T(8,128)(2,1)} %get-tuple-element.171) | copy-start | bytes 1351684
  230.1 6.2 %copy-start.39 = (bf16[288,5,128]{2,1,0:T(8,128)(2,1)S(1)}, bf16[288,5,128]{2,1,0:T(8,128)(2,1)}, u32[]{:S(2)}) copy-start(bf16[288,5,128]{2,1,0:T(8,128)(2,1)} %slice.2509) | copy-start | bytes 1105924
  230.1 31.1 %all-to-all-start.5 = ((f32[16,128,128]{2,1,0:T(8,128)}), f32[16,128,128]{2,1,0:T(8,128)}, u32[]{:S(2)}, u32[]{:S(2)}) async-start(f32[16,128,128]{2,1,0:T(8,128)} %bitcast.169), calls=%async_computation.5 | async-start | bytes 2097152 | tf_op jit(solution)/shard_map/all_to_all | solution.py:121
  246.3 4.8 %copy-start.48 = (bf16[192,5,128]{2,1,0:T(8,128)(2,1)S(1)}, bf16[192,5,128]{2,1,0:T(8,128)(2,1)}, u32[]{:S(2)}) copy-start(bf16[192,5,128]{2,1,0:T(8,128)(2,1)} %slice.2515) | copy-start | bytes 737284
  247.0 5.9 %copy-start.56 = (bf16[160,5,128]{2,1,0:T(8,128)(2,1)S(1)}, bf16[160,5,128]{2,1,0:T(8,128)(2,1)}, u32[]{:S(2)}) copy-start(bf16[160,5,128]{2,1,0:T(8,128)(2,1)} %slice.2517) | copy-start | bytes 614404
  247.0 5.9 %copy-start.117 = (bf16[5,160,128]{2,1,0:T(8,128)(2,1)S(1)}, bf16[5,160,128]{2,1,0:T(8,128)(2,1)}, u32[]{:S(2)}) copy-start(bf16[5,160,128]{2,1,0:T(8,128)(2,1)} %copy-done.116) | copy-start | bytes 614404
  247.0 6.8 %copy-start.60 = (bf16[128,5,128]{2,1,0:T(8,128)(2,1)S(1)}, bf16[128,5,128]{2,1,0:T(8,128)(2,1)}, u32[]{:S(2)}) copy-start(bf16[128,5,128]{2,1,0:T(8,128)(2,1)} %slice.2519) | copy-start | bytes 491524
  247.0 6.8 %copy-start.99 = (bf16[5,32,128]{2,1,0:T(8,128)(2,1)S(1)}, bf16[5,32,128]{2,1,0:T(8,128)(2,1)}, u32[]{:S(2)}) copy-start(bf16[5,32,128]{2,1,0:T(8,128)(2,1)} %get-tuple-element.181) | copy-start | bytes 122884
  247.1 6.8 %copy-start.102 = (bf16[5,32,128]{2,1,0:T(8,128)(2,1)S(1)}, bf16[5,32,128]{2,1,0:T(8,128)(2,1)}, u32[]{:S(2)}) copy-start(bf16[5,32,128]{2,1,0:T(8,128)(2,1)} %get-tuple-element.223) | copy-start | bytes 122884
  247.1 6.8 %copy-start.106 = (bf16[5,32,128]{2,1,0:T(8,128)(2,1)S(1)}, bf16[5,32,128]{2,1,0:T(8,128)(2,1)}, u32[]{:S(2)}) copy-start(bf16[5,32,128]{2,1,0:T(8,128)(2,1)} %get-tuple-element.206) | copy-start | bytes 122884
  247.1 6.8 %copy-start.111 = (bf16[5,32,128]{2,1,0:T(8,128)(2,1)S(1)}, bf16[5,32,128]{2,1,0:T(8,128)(2,1)}, u32[]{:S(2)}) copy-start(bf16[5,32,128]{2,1,0:T(8,128)(2,1)} %get-tuple-element.160) | copy-start | bytes 122884
  249.0 5.7 %copy-start.98 = (bf16[5,32,128]{2,1,0:T(8,128)(2,1)S(1)}, bf16[5,32,128]{2,1,0:T(8,128)(2,1)}, u32[]{:S(2)}) copy-start(bf16[5,32,128]{2,1,0:T(8,128)(2,1)} %get-tuple-element.180) | copy-start | bytes 122884
  249.0 5.7 %copy-start.105 = (bf16[5,32,128]{2,1,0:T(8,128)(2,1)S(1)}, bf16[5,32,128]{2,1,0:T(8,128)(2,1)}, u32[]{:S(2)}) copy-start(bf16[5,32,128]{2,1,0:T(8,128)(2,1)} %get-tuple-element.205) | copy-start | bytes 122884
  249.0 5.7 %copy-start.110 = (bf16[5,32,128]{2,1,0:T(8,128)(2,1)S(1)}, bf16[5,32,128]{2,1,0:T(8,128)(2,1)}, u32[]{:S(2)}) copy-start(bf16[5,32,128]{2,1,0:T(8,128)(2,1)} %get-tuple-element.159) | copy-start | bytes 122884
  251.1 4.5 %copy-start.91 = (bf16[64,5,128]{2,1,0:T(8,128)(2,1)S(1)}, bf16[64,5,128]{2,1,0:T(8,128)(2,1)}, u32[]{:S(2)}) copy-start(bf16[64,5,128]{2,1,0:T(8,128)(2,1)} %slice.2523) | copy-start | bytes 245764
  251.1 4.5 %copy-start.97 = (bf16[5,32,128]{2,1,0:T(8,128)(2,1)S(1)}, bf16[5,32,128]{2,1,0:T(8,128)(2,1)}, u32[]{:S(2)}) copy-start(bf16[5,32,128]{2,1,0:T(8,128)(2,1)} %get-tuple-element.179) | copy-start | bytes 122884
  251.1 4.5 %copy-start.109 = (bf16[5,32,128]{2,1,0:T(8,128)(2,1)S(1)}, bf16[5,32,128]{2,1,0:T(8,128)(2,1)}, u32[]{:S(2)}) copy-start(bf16[5,32,128]{2,1,0:T(8,128)(2,1)} %get-tuple-element.158) | copy-start | bytes 122884
  251.1 5.4 %copy-start.74 = (bf16[32,5,128]{2,1,0:T(8,128)(2,1)S(1)}, bf16[32,5,128]{2,1,0:T(8,128)(2,1)}, u32[]{:S(2)}) copy-start(bf16[32,5,128]{2,1,0:T(8,128)(2,1)} %slice.2061) | copy-start | bytes 122884
  261.2 29.8 %all-to-all-start.6 = ((f32[16,128,128]{2,1,0:T(8,128)}), f32[16,128,128]{2,1,0:T(8,128)S(1)}, u32[]{:S(2)}, u32[]{:S(2)}) async-start(f32[16,128,128]{2,1,0:T(8,128)} %bitcast.189), calls=%async_computation.6 | async-start | bytes 2097152 | tf_op jit(solution)/shard_map/all_to_all | solution.py:122
  (102 other events, 177.2 us)
where the time goes:
time: 297 us; the launch traced here: 292 us
  local copies, waits for them, and re-layouts  88.3 us (30%)
  waiting for transfers between devices  77.5 us (26%)
  matrix products  56.3 us (19%)
  starting transfers between devices  35.8 us (12%)
  other arithmetic  31.1 us (10%)
  between operations  3.19 us (1%)
    slice x28, local copies, waits for them, and re-layouts, per_device(): query_tiles[start:]  33 us
    dot_general x16, matrix products, per_device(): jnp.einsum('hnk,nhd->kd', probs_here, grad_tiles[start:], preferred_eleme...  23.9 us
    all_to_all x1, waiting for transfers between devices, per_device(): lax.all_to_all(value_accum, 'seq', split_axis=0, concat_axis=0, tiled=True)  21.2 us
    dot_general x16, matrix products, per_device(): jnp.einsum('hnk,nhd->kd', grads_here, query_tiles[start:], preferred_elem...  19.9 us
    slice x28, local copies, waits for them, and re-layouts, per_device(): grad_tiles[start:]  19.4 us
    all_to_all x1, waiting for transfers between devices, per_device(): lax.all_to_all(to_heads(queries), 'seq', split_axis=0, concat_axis=0, til...  16.3 us
    all_to_all x1, waiting for transfers between devices, per_device(): lax.all_to_all(to_heads(out_grad), 'seq', split_axis=0, concat_axis=0, ti...  16 us
    unnamed x47, other arithmetic  12.2 us
  transfers between devices with their start and end apart: 7, of which 6 were waited for; matrix products, arithmetic and copies ran while one was open for 40% of the time, Pallas kernels for 0%

commit v1 on v0

v1 whole, which is shorter than its diff:
```python
from functools import partial

import jax
import jax.numpy as jnp
from jax import lax
from jax.experimental import pallas as pl
from jax.experimental.pallas import tpu as pltpu
from jax.sharding import PartitionSpec as P

DH = 128
KVH = 4
QPG = 5
SCALING = DH ** (-0.5)
LOG2E = 1.4426950408889634
CONTRACT_LAST = (((1,), (1,)), ((), ()))
VMEM_BYTES = 40 * 1024 * 1024


def token_places(rank, tokens, dim):
    shape = (tokens, 1) if dim == 0 else (1, tokens)
    own = lax.broadcasted_iota(jnp.int32, shape, dim)
    return jnp.concatenate([own + tokens * (rank ^ d) for d in range(KVH)], axis=dim)


def stacked(refs):
    return jnp.concatenate([ref[...] for ref in refs], axis=0)


def keys_values(refs):
    return (
        jnp.concatenate([ref[:, :DH] for ref in refs], axis=0),
        jnp.concatenate([ref[:, DH:] for ref in refs], axis=0),
    )


def scaled_scores(key_rows, query_rows):
    raw = lax.dot_general(key_rows, query_rows, CONTRACT_LAST, preferred_element_type=jnp.float32)
    return raw * (SCALING * LOG2E)


def stats_kernel(offset, info, kv_a, kv_b, q0, q1, q2, q3, g0, g1, g2, g3, old, new):
    tokens = q0.shape[0]

    def update():
        key_rows, value_rows = keys_values((kv_a, kv_b))
        scores = scaled_scores(key_rows, stacked((q0, q1, q2, q3)))
        grad_probs = lax.dot_general(
            value_rows, stacked((g0, g1, g2, g3)), CONTRACT_LAST, preferred_element_type=jnp.float32
        )
        if offset == 0:
            rank = info[1]
            causal = token_places(rank, tokens, 0) <= token_places(rank, tokens, 1)
            scores = jnp.where(causal, scores, -jnp.inf)
        top = jnp.max(scores, axis=0, keepdims=True)
        if offset:
            old_top = old[0, 0:1]
            top = jnp.maximum(old_top, top)
        weights = jnp.exp2(scores - top)
        total = jnp.sum(weights, axis=0, keepdims=True)
        weighted = jnp.sum(weights * grad_probs, axis=0, keepdims=True)
        if offset:
            shrink = jnp.exp2(old_top - top)
            total = total + shrink * old[0, 1:2]
            weighted = weighted + shrink * old[0, 2:3]
        new[0, 0:1] = top
        new[0, 1:2] = total
        new[0, 2:3] = weighted

    if offset == 0:
        update()
    else:
        new[0] = old[0]
        pl.when(info[0] >= offset)(update)


def grads_kernel(
    offset, first, info, kv_a, kv_b, q0, q1, q2, q3, g0, g1, g2, g3, stats, *rest
):
    tokens = q0.shape[0]
    last = offset == 0
    rest = list(rest)
    dq_old = None if first else rest.pop(0)
    dkv_a, dkv_b = rest[:2]
    dq_refs = rest[2:]
    head = pl.program_id(0)

    @pl.when(head == 0)
    def _():
        dkv_a[...] = jnp.zeros_like(dkv_a)
        dkv_b[...] = jnp.zeros_like(dkv_b)

    def work():
        key_rows, value_rows = keys_values((kv_a, kv_b))
        query_rows = stacked((q0, q1, q2, q3))
        grad_rows = stacked((g0, g1, g2, g3))
        total = stats[0, 1:2]
        log_total = stats[0, 0:1] + jnp.log2(total)
        row_delta = stats[0, 2:3] / total
        probs = jnp.exp2(scaled_scores(key_rows, query_rows) - log_total)
        if last:
            rank = info[1]
            causal = token_places(rank, tokens, 0) <= token_places(rank, tokens, 1)
            probs = jnp.where(causal, probs, 0.0)
        grad_probs = lax.dot_general(
            value_rows, grad_rows, CONTRACT_LAST, preferred_element_type=jnp.float32
        )
        grad_scores = (probs * (grad_probs - row_delta) * SCALING).astype(jnp.bfloat16)
        dv = jnp.dot(probs.astype(jnp.bfloat16), grad_rows, preferred_element_type=jnp.float32)
        dk = jnp.dot(grad_scores, query_rows, preferred_element_type=jnp.float32)
        half = 2 * tokens
        dkv_a[:, :DH] += dk[:half]
        dkv_b[:, :DH] += dk[half:]
        dkv_a[:, DH:] += dv[:half]
        dkv_b[:, DH:] += dv[half:]
        dq = jnp.dot(key_rows.T, grad_scores, preferred_element_type=jnp.float32)
        if dq_old is not None:
            dq = dq + dq_old[0]
        if last:
            rows = dq.T.astype(jnp.bfloat16)
            for d in range(KVH):
                dq_refs[d][...] = rows[d * tokens : (d + 1) * tokens]
        else:
            dq_refs[0][0] = dq

    if last:
        work()
    else:
        pl.when(info[0] >= offset)(work)

        @pl.when(info[0] < offset)
        def _():
            dq_refs[0][0] = jnp.zeros_like(dq_refs[0][0]) if dq_old is None else dq_old[0]


def piece_specs(tokens):
    queries = [pl.BlockSpec((tokens, DH), lambda h, info: (0, h)) for d in range(KVH)]
    grads = [pl.BlockSpec((tokens, DH), lambda h, info: (0, h + QPG)) for d in range(KVH)]
    return queries + grads


def whole(shape):
    return pl.BlockSpec(shape, lambda h, info: (0,) * len(shape))


def per_head(shape):
    return pl.BlockSpec((1,) + shape, lambda h, info: (h, 0, 0))


def params():
    return pltpu.CompilerParams(
        vmem_limit_bytes=VMEM_BYTES, dimension_semantics=("arbitrary",)
    )


def cost(products, span):
    return pl.CostEstimate(
        flops=products * QPG * 2 * span * span * DH,
        bytes_accessed=4 * QPG * span * DH * 2,
        transcendentals=QPG * span * span,
    )


def stats_call(offset, info, kv, pieces, old):
    tokens = pieces[0].shape[0]
    span = KVH * tokens
    shape = jax.ShapeDtypeStruct((QPG, 8, span), jnp.float32)
    return pl.pallas_call(
        partial(stats_kernel, offset),
        grid_spec=pltpu.PrefetchScalarGridSpec(
            num_scalar_prefetch=1,
            grid=(QPG,),
            in_specs=[whole(kv[0].shape), whole(kv[1].shape)]
            + piece_specs(tokens)
            + [per_head((8, span))],
            out_specs=per_head((8, span)),
        ),
        out_shape=shape,
        compiler_params=params(),
        cost_estimate=cost(2, span),
    )(info, *kv, *pieces, *pieces, old)


def grads_call(offset, info, kv, pieces, stats, dq_old):
    tokens = pieces[0].shape[0]
    span = KVH * tokens
    first = dq_old is None
    half = jax.ShapeDtypeStruct((2 * tokens, 2 * DH), jnp.float32)
    if offset:
        dq_shapes = [jax.ShapeDtypeStruct((QPG, DH, span), jnp.float32)]
        dq_specs = [per_head((DH, span))]
    else:
        dq_shapes = [jax.ShapeDtypeStruct((tokens, QPG * DH), jnp.bfloat16)] * KVH
        dq_specs = [pl.BlockSpec((tokens, DH), lambda h, info: (0, h))] * KVH
    return pl.pallas_call(
        partial(grads_kernel, offset, first),
        grid_spec=pltpu.PrefetchScalarGridSpec(
            num_scalar_prefetch=1,
            grid=(QPG,),
            in_specs=[whole(kv[0].shape), whole(kv[1].shape)]
            + piece_specs(tokens)
            + [per_head((8, span))]
            + ([] if first else [per_head((DH, span))]),
            out_specs=[whole(half.shape), whole(half.shape)] + dq_specs,
        ),
        out_shape=[half, half] + dq_shapes,
        compiler_params=params(),
        cost_estimate=cost(5, span),
    )(info, *kv, *pieces, *pieces, stats, *([] if first else [dq_old]))


def place_kernel(info, *refs):
    rank = info[1]
    sources, targets = refs[: 2 * KVH], refs[2 * KVH :]
    query_grad, key_grad, value_grad = targets
    for d in range(KVH):
        head = rank ^ d
        wide = pl.ds(pl.multiple_of(head * (QPG * DH), DH), QPG * DH)
        narrow = pl.ds(pl.multiple_of(head * DH, DH), DH)
        query_grad[:, wide] = sources[d][...]
        key_grad[:, narrow] = sources[KVH + d][:, :DH]
        value_grad[:, narrow] = sources[KVH + d][:, DH:]


def place_call(info, dq, dkv):
    tokens = dq[0].shape[0]
    shapes = [
        jax.ShapeDtypeStruct((tokens, KVH * QPG * DH), jnp.bfloat16),
        jax.ShapeDtypeStruct((tokens, KVH * DH), jnp.bfloat16),
        jax.ShapeDtypeStruct((tokens, KVH * DH), jnp.bfloat16),
    ]
    vmem = pl.BlockSpec(memory_space=pltpu.VMEM)
    return pl.pallas_call(
        place_kernel,
        in_specs=[pl.BlockSpec(memory_space=pltpu.SMEM)] + [vmem] * (2 * KVH),
        out_specs=[vmem] * 3,
        out_shape=shapes,
        compiler_params=pltpu.CompilerParams(vmem_limit_bytes=VMEM_BYTES),
    )(info, *dq, *dkv)


def per_device(queries, keys, values, out_grad):
    devices = lax.axis_size("seq")
    planes = devices // KVH
    tokens = queries.shape[0]
    device = lax.axis_index("seq")
    rank = device % KVH
    info = jnp.stack([device // KVH, rank]).astype(jnp.int32)
    up = [(i, i + KVH) for i in range(devices - KVH)]
    down = [(i + KVH, i) for i in range(devices - KVH)]

    def swap(array, d):
        if d == 0:
            return array
        return lax.ppermute(array, "seq", [(i, i ^ d) for i in range(devices)])

    def columns(array, head, width):
        return lax.dynamic_slice_in_dim(array, head * width, width, axis=1)

    kv_pieces = []
    for d in range(KVH):
        head = rank ^ d
        piece = jnp.concatenate([columns(keys, head, DH), columns(values, head, DH)], axis=1)
        kv_pieces.append(swap(piece, d))
    pieces = []
    for d in range(KVH):
        head = rank ^ d
        piece = jnp.concatenate(
            [columns(queries, head, QPG * DH), columns(out_grad, head, QPG * DH)], axis=1
        )
        pieces.append(swap(piece, d))
    chain = [
        (
            jnp.concatenate(kv_pieces[:2], axis=0),
            jnp.concatenate(kv_pieces[2:], axis=0),
        )
    ]
    for step in range(1, planes):
        chain.append(tuple(lax.ppermute(half, "seq", up) for half in chain[-1]))
    stats = jnp.zeros((QPG, 8, KVH * tokens), jnp.float32)
    for offset in range(planes):
        stats = stats_call(offset, info, chain[offset], pieces, stats)
    dq = None
    arrived = None
    for offset in reversed(range(planes)):
        results = grads_call(offset, info, chain[offset], pieces, stats, dq)
        partials = results[:2]
        if offset:
            dq = results[2]
        else:
            dq_pieces = results[2:]
        if arrived is not None:
            partials = [mine + half for mine, half in zip(partials, arrived)]
        sums = [half.astype(jnp.bfloat16) for half in partials]
        if offset:
            arrived = [lax.ppermute(half, "seq", down).astype(jnp.float32) for half in sums]
    dq_back = [swap(dq_pieces[d], d) for d in range(KVH)]
    dkv_back = [
        swap(sums[d // 2][(d % 2) * tokens : (d % 2 + 1) * tokens], d) for d in range(KVH)
    ]
    return tuple(place_call(info, dq_back, dkv_back))


def solution(mesh):
    spec = P(("groups", "seq"), None)
    return jax.shard_map(
        per_device,
        mesh=mesh,
        in_specs=(spec,) * 4,
        out_specs=(spec,) * 3,
        check_vma=False,
    )
```

time: 297 us -> 92 us (0.31); the launches traced: 292 us -> 91.3 us
  local copies, waits for them, and re-layouts: 88.3 us -> 2.31 us
  waiting for transfers between devices: 77.5 us -> 19.8 us
  matrix products: 56.3 us -> 0 us
  other arithmetic: 31.1 us -> 0.45 us
  Pallas kernels: 0 us -> 24.7 us
  starting transfers between devices: 35.8 us -> 43 us
    all_to_all x7 -> x0, waiting for transfers between devices: 77.5 us -> none  [the longest x1 21.2 us: per_device(): lax.all_to_all(value_accum, 'seq', split_axis=0, concat_axis=0, tiled=True)]
    slice x146 -> x2, local copies, waits for them, and re-layouts: 70.8 us -> 0.02 us  [per_device(): sums[d // 2][d % 2 * tokens:(d % 2 + 1) * tokens]]
    dot_general x80 -> x0, matrix products: 56.3 us -> none  [the longest x16 23.9 us: per_device(): jnp.einsum('hnk,nhd->kd', probs_here, grad_tiles[start:], preferred_eleme...]
    ppermute x0 -> x24, starting transfers between devices: none -> 43 us  [the longest x6 16.1 us: per_device(): chain.append(tuple((lax.ppermute(half, 'seq', up) for half in chain[-1])))]
    all_to_all x7 -> x0, starting transfers between devices: 35.8 us -> none  [the longest x1 6.61 us: per_device(): lax.all_to_all(spread(values), 'seq', split_axis=0, concat_axis=0, tiled=...]
    pallas_call x0 -> x9, Pallas kernels: none -> 24.7 us  [the longest x4 13.9 us: grads_call(): pl.pallas_call(partial(grads_kernel, offset, first), grid_spec=pltpu.Pref...]
    ppermute x0 -> x24, waiting for transfers between devices: none -> 19.8 us  [the longest x6 14.7 us: per_device(): lax.ppermute(half, 'seq', down).astype(jnp.float32)]
    unnamed x47 -> x0, other arithmetic: 12.2 us -> none
  transfers between devices with their start and end apart: 7 -> 24, of which waited for: 6 -> 9; matrix products, arithmetic and copies ran while one was open for 40% -> 2% of each run, Pallas kernels for 0% -> 23%
where the time goes in v1:
time: 92 us; the launch traced here: 91.3 us
  starting transfers between devices  43 us (47%)
  Pallas kernels  24.7 us (27%)
  waiting for transfers between devices  19.8 us (22%)
  local copies, waits for them, and re-layouts  2.31 us (3%)
  between operations  1.05 us (1%)
    ppermute x6, starting transfers between devices, per_device(): chain.append(tuple((lax.ppermute(half, 'seq', up) for half in chain[-1])))  16.1 us
    ppermute x12, starting transfers between devices, swap(): return lax.ppermute(array, 'seq', [(i, i ^ d) for i in range(devices)])  15.4 us
    ppermute x6, waiting for transfers between devices, per_device(): lax.ppermute(half, 'seq', down).astype(jnp.float32)  14.7 us
    pallas_call x4, Pallas kernels, grads_call(): pl.pallas_call(partial(grads_kernel, offset, first), grid_spec=pltpu.Pref...  13.9 us
    ppermute x6, starting transfers between devices, per_device(): lax.ppermute(half, 'seq', down).astype(jnp.float32)  11.5 us
    pallas_call x4, Pallas kernels, stats_call(): pl.pallas_call(partial(stats_kernel, offset), grid_spec=pltpu.PrefetchSca...  9.25 us
    ppermute x12, waiting for transfers between devices, swap(): return lax.ppermute(array, 'seq', [(i, i ^ d) for i in range(devices)])  3.52 us
    dynamic_slice x2, local copies, waits for them, and re-layouts, columns(): return lax.dynamic_slice_in_dim(array, head * width, width, axis=1)  2.26 us
  transfers between devices with their start and end apart: 24, of which 9 were waited for; matrix products, arithmetic and copies ran while one was open for 2% of the time, Pallas kernels for 23%

profile of v1, /device:TPU:9, one launch (start us, length us, event | category | flops | bytes accessed | tf_op | source)
XLA Modules:
  0.0 91.3 jit_solution(1148521699088835606)
XLA Ops:
  0.6 0.0 copy-start
  0.7 1.0 %constant_dynamic-slice_fusion.8 = (bf16[128,128]{1,0:T(8,128)(2,1)S(1)}, bf16[128,128]{1,0:T(8,128)(2,1)S(1)}, bf16[128,128]{1,0:T(8,128)(2,1)S(1)}, bf16[128,1...) fusion(bf16[128,512]{1,0:T(8,128)(2,1)} %param.6, ...), kind=kLoop, calls=%fused_computation.24 | loop fusion | bytes 524304 | tf_op jit(solution)/shard_map/dynamic_slice | solution.py:257
  1.7 1.3 %collective-permute-start.1 = (bf16[128,256]{1,0:T(8,128)(2,1)S(1)}, bf16[128,256]{1,0:T(8,128)(2,1)S(1)}, u32[]{:S(2)}, u32[]{:S(2)}) collective-permute-start(bf16[128,256]{1,0:T(8,128)(2,1)S(1)} %pad_maximum_fusion.6), channel_id=1, source_target_pairs={{0,2},{1,3},{2,0},{3,1},{4,6},{5,7},{6,4},{7,5},{8,10},{9,11},{10,... | collective-permute-start | bytes 196616 | tf_op jit(solution)/shard_map/ppermute | solution.py:254
  3.0 1.0 %collective-permute-start = (bf16[128,256]{1,0:T(8,128)(2,1)S(1)}, bf16[128,256]{1,0:T(8,128)(2,1)S(1)}, u32[]{:S(2)}, u32[]{:S(2)}) collective-permute-start(bf16[128,256]{1,0:T(8,128)(2,1)S(1)} %pad_maximum_fusion.5), channel_id=1, source_target_pairs={{0,1},{1,0},{2,3},{3,2},{4,5},{5,4},{6,7},{7,6},{8,9},{9,8},{10,11... | collective-permute-start | bytes 196616 | tf_op jit(solution)/shard_map/ppermute | solution.py:254
  4.0 0.2 collective-permute-start.2
  4.2 0.0 copy-done
  4.2 1.3 %constant_dynamic-slice_fusion = (bf16[128,640]{1,0:T(8,128)(2,1)S(1)}, bf16[128,640]{1,0:T(8,128)(2,1)S(1)}, bf16[128,640]{1,0:T(8,128)(2,1)S(1)}, bf16[128,640...) fusion(bf16[128,2560]{1,0:T(8,128)(2,1)S(1)} %copy-done, ...), kind=kLoop, calls=%fused_computation.16 | loop fusion | bytes 2621456 | tf_op jit(solution)/shard_map/dynamic_slice | solution.py:257
  5.6 1.3 %collective-permute-start.4 = (bf16[128,1280]{1,0:T(8,128)(2,1)S(1)}, bf16[128,1280]{1,0:T(8,128)(2,1)S(1)}, u32[]{:S(2)}, u32[]{:S(2)}) collective-permute-start(bf16[128,1280]{1,0:T(8,128)(2,1)S(1)} %pad_maximum_fusion.2), channel_id=1, source_target_pairs={{0,2},{1,3},{2,0},{3,1},{4,6},{5,7},{6,4},{7,5},{8,10},{9,11},{10,... | collective-permute-start | bytes 983048 | tf_op jit(solution)/shard_map/ppermute | solution.py:254
  6.9 0.8 collective-permute-start.3
  7.7 0.0 collective-permute-done.1
  7.7 0.1 collective-permute-done.2
  7.8 3.2 %collective-permute-start.9 = (bf16[256,256]{1,0:T(8,128)(2,1)S(1)}, bf16[256,256]{1,0:T(8,128)(2,1)S(1)}, u32[]{:S(2)}, u32[]{:S(2)}) collective-permute-start(bf16[256,256]{1,0:T(8,128)(2,1)S(1)} %constant_dynamic-update-slice_fusion.kv_b), channel_id=1, source_target_pairs={{0,4},{1,5},{2,6},{3,7},{4,8},{5,9},{6,10},{7,11},{8,12},{9,13},{1... | collective-permute-start | bytes 393224 | tf_op jit(solution)/shard_map/ppermute | solution.py:278
  11.0 0.0 collective-permute-done
  11.0 3.2 %collective-permute-start.6 = (bf16[256,256]{1,0:T(8,128)(2,1)S(1)}, bf16[256,256]{1,0:T(8,128)(2,1)S(1)}, u32[]{:S(2)}, u32[]{:S(2)}) collective-permute-start(bf16[256,256]{1,0:T(8,128)(2,1)S(1)} %pad_maximum_fusion.4.kv_a), channel_id=1, source_target_pairs={{0,4},{1,5},{2,6},{3,7},{4,8},{5,9},{6,10},{7,11},{8,12},{9,13},{1... | collective-permute-start | bytes 393224 | tf_op jit(solution)/shard_map/ppermute | solution.py:278
  14.3 1.4 %collective-permute-start.5 = (bf16[128,1280]{1,0:T(8,128)(2,1)S(1)}, bf16[128,1280]{1,0:T(8,128)(2,1)S(1)}, u32[]{:S(2)}, u32[]{:S(2)}) collective-permute-start(bf16[128,1280]{1,0:T(8,128)(2,1)S(1)} %pad_maximum_fusion.3), channel_id=1, source_target_pairs={{0,3},{1,2},{2,1},{3,0},{4,7},{5,6},{6,5},{7,4},{8,11},{9,10},{10,... | collective-permute-start | bytes 983048 | tf_op jit(solution)/shard_map/ppermute | solution.py:254
  15.7 0.0 collective-permute-done.9.kv_b
  15.7 2.2 %collective-permute-start.10 = (bf16[256,256]{1,0:T(8,128)(2,1)S(1)}, bf16[256,256]{1,0:T(8,128)(2,1)S(1)}, u32[]{:S(2)}, u32[]{:S(2)}) collective-permute-start(bf16[256,256]{1,0:T(8,128)(2,1)S(1)} %collective-permute-done.9.kv_b), channel_id=1, source_target_pairs={{0,4},{1,5},{2,6},{3,7},{4,8},{5,9},{6,10},{7,11},{8,12},{9,13},{1... | collective-permute-start | bytes 393224 | tf_op jit(solution)/shard_map/ppermute | solution.py:278
  17.9 0.0 collective-permute-done.6.kv_a
  18.0 3.2 %collective-permute-start.7 = (bf16[256,256]{1,0:T(8,128)(2,1)S(1)}, bf16[256,256]{1,0:T(8,128)(2,1)S(1)}, u32[]{:S(2)}, u32[]{:S(2)}) collective-permute-start(bf16[256,256]{1,0:T(8,128)(2,1)S(1)} %collective-permute-done.6.kv_a), channel_id=1, source_target_pairs={{0,4},{1,5},{2,6},{3,7},{4,8},{5,9},{6,10},{7,11},{8,12},{9,13},{1... | collective-permute-start | bytes 393224 | tf_op jit(solution)/shard_map/ppermute | solution.py:278
  21.2 0.1 pad_add_fusion.info
  21.3 1.5 %collective-permute-done.10.kv_b = bf16[256,256]{1,0:T(8,128)(2,1)S(1)} collective-permute-done((bf16[256,256]{1,0:T(8,128)(2,1)S(1)}, bf16[256,256]{1,0:T(8,128)(2,1)S(1)}, u32[]{:S(2)}, u32[]{:S(2)}) %collective-permute-start.10) | collective-permute-done | bytes 131104 | tf_op jit(solution)/shard_map/ppermute | solution.py:278
  22.8 1.9 %collective-permute-start.11 = (bf16[256,256]{1,0:T(8,128)(2,1)S(1)}, bf16[256,256]{1,0:T(8,128)(2,1)S(1)}, u32[]{:S(2)}, u32[]{:S(2)}) collective-permute-start(bf16[256,256]{1,0:T(8,128)(2,1)S(1)} %collective-permute-done.10.kv_b), channel_id=1, source_target_pairs={{0,4},{1,5},{2,6},{3,7},{4,8},{5,9},{6,10},{7,11},{8,12},{9,13},{1... | collective-permute-start | bytes 393224 | tf_op jit(solution)/shard_map/ppermute | solution.py:278
  24.7 0.1 collective-permute-done.7.kv_a
  24.8 2.3 %collective-permute-start.8 = (bf16[256,256]{1,0:T(8,128)(2,1)S(1)}, bf16[256,256]{1,0:T(8,128)(2,1)S(1)}, u32[]{:S(2)}, u32[]{:S(2)}) collective-permute-start(bf16[256,256]{1,0:T(8,128)(2,1)S(1)} %collective-permute-done.7.kv_a), channel_id=1, source_target_pairs={{0,4},{1,5},{2,6},{3,7},{4,8},{5,9},{6,10},{7,11},{8,12},{9,13},{1... | collective-permute-start | bytes 393224 | tf_op jit(solution)/shard_map/ppermute | solution.py:278
  27.2 0.0 collective-permute-done.4.q2.g2
  27.2 0.0 collective-permute-done.3.q1.g1
  27.2 0.0 collective-permute-done.5.q3.g3
  27.2 3.5 %shard_map.67.old = f32[5,8,512]{2,1,0:T(8,128)S(1)} custom-call(s32[2]{0:T(128)S(1)} %pad_add_fusion.info, bf16[256,256]{1,0:T(8,128)(2,1)S(1)} %pad_maximum_fusion.4.kv_a, bf16[256,256]{1,0:T(8,128)(2,1)S(1)} %constant_dynamic-update-slice_fusion.kv_b, bf16[128,1280]{1,0:T(8,128)(2,1)S(1)} %pad_maximum_fusion.q0.g0, ...), custom_call_target="tpu_custom_call" | custom-call | flops 671088640 | bytes 2621440 | tf_op jit(solution)/shard_map/pallas_call | solution.py:167
  30.7 3.7 %shard_map.68.old = f32[5,8,512]{2,1,0:T(8,128)S(1)} custom-call(s32[2]{0:T(128)S(1)} %pad_add_fusion.info, bf16[256,256]{1,0:T(8,128)(2,1)S(1)} %collective-permute-done.6.kv_a, bf16[256,256]{1,0:T(8,128)(2,1)S(1)} %collective-permute-done.9.kv_b, bf16[128,1280]{1,0:T(8,128)(2,1)S(1)} %pad_maximum_fusion.q0.g0, ...), custom_call_target="tpu_custom_call" | custom-call | flops 671088640 | bytes 2621440 | tf_op jit(solution)/shard_map/pallas_call | solution.py:167
  34.5 1.0 %shard_map.69.old = f32[5,8,512]{2,1,0:T(8,128)S(1)} custom-call(s32[2]{0:T(128)S(1)} %pad_add_fusion.info, bf16[256,256]{1,0:T(8,128)(2,1)S(1)} %collective-permute-done.7.kv_a, bf16[256,256]{1,0:T(8,128)(2,1)S(1)} %collective-permute-done.10.kv_b, bf16[128,1280]{1,0:T(8,128)(2,1)S(1)} %pad_maximum_fusion.q0.g0, ...), custom_call_target="tpu_custom_call" | custom-call | flops 671088640 | bytes 2621440 | tf_op jit(solution)/shard_map/pallas_call | solution.py:167
  35.5 0.0 collective-permute-done.11.kv_b
  35.5 0.0 collective-permute-done.8.kv_a
  35.5 1.0 %shard_map.70.stats = f32[5,8,512]{2,1,0:T(8,128)S(1)} custom-call(s32[2]{0:T(128)S(1)} %pad_add_fusion.info, bf16[256,256]{1,0:T(8,128)(2,1)S(1)} %collective-permute-done.8.kv_a, bf16[256,256]{1,0:T(8,128)(2,1)S(1)} %collective-permute-done.11.kv_b, bf16[128,1280]{1,0:T(8,128)(2,1)S(1)} %pad_maximum_fusion.q0.g0, ...), custom_call_target="tpu_custom_call" | custom-call | flops 671088640 | bytes 2621440 | tf_op jit(solution)/shard_map/pallas_call | solution.py:167
  36.5 1.3 %shard_map.71 = (f32[256,256]{1,0:T(8,128)S(1)}, f32[256,256]{1,0:T(8,128)S(1)}, f32[5,128,512]{2,1,0:T(8,128)S(1)}) custom-call(s32[2]{0:T(128)S(1)} %pad_add_fusion.info, bf16[256,256]{1,0:T(8,128)(2,1)S(1)} %collective-permute-done.8.kv_a, bf16[256,256]{1,0:T(8,128)(2,1)S(1)} %collective-permute-done.11.kv_b, ...), custom_call_target="tpu_custom_call" | custom-call | flops 1677721600 | bytes 2621440 | tf_op jit(solution)/shard_map/pallas_call | solution.py:194
  37.9 1.9 %collective-permute-start.19 = (bf16[256,256]{1,0:T(8,128)(2,1)S(1)}, bf16[256,256]{1,0:T(8,128)(2,1)S(1)}, u32[]{:S(2)}, u32[]{:S(2)}) collective-permute-start(bf16[256,256]{1,0:T(8,128)(2,1)S(1)} %convert_element_type.49), channel_id=1, source_target_pairs={{4,0},{5,1},{6,2},{7,3},{8,4},{9,5},{10,6},{11,7},{12,8},{13,9},{1... | collective-permute-start | bytes 393224 | tf_op jit(solution)/shard_map/ppermute | solution.py:295
  39.8 1.9 %collective-permute-start.15 = (bf16[256,256]{1,0:T(8,128)(2,1)S(1)}, bf16[256,256]{1,0:T(8,128)(2,1)S(1)}, u32[]{:S(2)}, u32[]{:S(2)}) collective-permute-start(bf16[256,256]{1,0:T(8,128)(2,1)S(1)} %convert_element_type.42), channel_id=1, source_target_pairs={{4,0},{5,1},{6,2},{7,3},{8,4},{9,5},{10,6},{11,7},{12,8},{13,9},{1... | collective-permute-start | bytes 393224 | tf_op jit(solution)/shard_map/ppermute | solution.py:295
  41.7 1.3 %shard_map.72 = (f32[256,256]{1,0:T(8,128)S(1)}, f32[256,256]{1,0:T(8,128)S(1)}, f32[5,128,512]{2,1,0:T(8,128)S(1)}) custom-call(s32[2]{0:T(128)S(1)} %pad_add_fusion.info, bf16[256,256]{1,0:T(8,128)(2,1)S(1)} %collective-permute-done.7.kv_a, bf16[256,256]{1,0:T(8,128)(2,1)S(1)} %collective-permute-done.10.kv_b, ...), custom_call_target="tpu_custom_call" | custom-call | flops 1677721600 | bytes 2621440 | tf_op jit(solution)/shard_map/pallas_call | solution.py:194
  43.0 5.2 %shard_map.73 = (f32[256,256]{1,0:T(8,128)S(1)}, f32[256,256]{1,0:T(8,128)S(1)}, f32[5,128,512]{2,1,0:T(8,128)S(1)}) custom-call(s32[2]{0:T(128)S(1)} %pad_add_fusion.info, bf16[256,256]{1,0:T(8,128)(2,1)S(1)} %collective-permute-done.6.kv_a, bf16[256,256]{1,0:T(8,128)(2,1)S(1)} %collective-permute-done.9.kv_b, bf16[128,1280]{1,0:T(8,128)(2,1)S(1)} %pad_maximum_fusion.q0.g0, ...), custom_call_target="tpu_custom_call" | custom-call | flops 1677721600 | bytes 2621440 | tf_op jit(solution)/shard_map/pallas_call | solution.py:194
  48.2 6.1 %shard_map.74 = (f32[256,256]{1,0:T(8,128)S(1)}, f32[256,256]{1,0:T(8,128)S(1)}, bf16[128,640]{1,0:T(8,128)(2,1)S(1)}, bf16[128,640]{1,0:T(8,128)(2,1)S(1)}, bf1...) custom-call(s32[2]{0:T(128)S(1)} %pad_add_fusion.info, bf16[256,256]{1,0:T(8,128)(2,1)S(1)} %pad_maximum_fusion.4.kv_a, ...), custom_call_target="tpu_custom_call" | custom-call | flops 1677721600 | bytes 2621440 | tf_op jit(solution)/shard_map/pallas_call | solution.py:194
  54.4 3.1 %collective-permute-start.12 = (bf16[128,640]{1,0:T(8,128)(2,1)S(1)}, bf16[128,640]{1,0:T(8,128)(2,1)S(1)}, u32[]{:S(2)}, u32[]{:S(2)}) collective-permute-start(bf16[128,640]{1,0:T(8,128)(2,1)S(1)} %get-tuple-element.22), channel_id=1, source_target_pairs={{0,1},{1,0},{2,3},{3,2},{4,5},{5,4},{6,7},{7,6},{8,9},{9,8},{10,11... | collective-permute-start | bytes 491528 | tf_op jit(solution)/shard_map/ppermute | solution.py:254
  57.5 0.9 %collective-permute-start.13 = (bf16[128,640]{1,0:T(8,128)(2,1)S(1)}, bf16[128,640]{1,0:T(8,128)(2,1)S(1)}, u32[]{:S(2)}, u32[]{:S(2)}) collective-permute-start(bf16[128,640]{1,0:T(8,128)(2,1)S(1)} %get-tuple-element.23), channel_id=1, source_target_pairs={{0,2},{1,3},{2,0},{3,1},{4,6},{5,7},{6,4},{7,5},{8,10},{9,11},{10,... | collective-permute-start | bytes 491528 | tf_op jit(solution)/shard_map/ppermute | solution.py:254
  58.4 0.8 collective-permute-start.14
  59.2 0.0 collective-permute-done.15
  59.2 1.9 %collective-permute-start.16 = (bf16[256,256]{1,0:T(8,128)(2,1)S(1)}, bf16[256,256]{1,0:T(8,128)(2,1)S(1)}, u32[]{:S(2)}, u32[]{:S(2)}) collective-permute-start(bf16[256,256]{1,0:T(8,128)(2,1)S(1)} %add_convert_fusion.5), channel_id=1, source_target_pairs={{4,0},{5,1},{6,2},{7,3},{8,4},{9,5},{10,6},{11,7},{12,8},{13,9},{1... | collective-permute-start | bytes 393224 | tf_op jit(solution)/shard_map/ppermute | solution.py:295
  61.1 0.0 collective-permute-done.19
  61.2 1.9 %collective-permute-start.20 = (bf16[256,256]{1,0:T(8,128)(2,1)S(1)}, bf16[256,256]{1,0:T(8,128)(2,1)S(1)}, u32[]{:S(2)}, u32[]{:S(2)}) collective-permute-start(bf16[256,256]{1,0:T(8,128)(2,1)S(1)} %add_convert_fusion.2), channel_id=1, source_target_pairs={{4,0},{5,1},{6,2},{7,3},{8,4},{9,5},{10,6},{11,7},{12,8},{13,9},{1... | collective-permute-start | bytes 393224 | tf_op jit(solution)/shard_map/ppermute | solution.py:295
  63.1 8.6 %collective-permute-done.16 = bf16[256,256]{1,0:T(8,128)(2,1)S(1)} collective-permute-done((bf16[256,256]{1,0:T(8,128)(2,1)S(1)}, bf16[256,256]{1,0:T(8,128)(2,1)S(1)}, u32[]{:S(2)}, u32[]{:S(2)}) %collective-permute-start.16) | collective-permute-done | bytes 131104 | tf_op jit(solution)/shard_map/ppermute | solution.py:295
  71.8 1.9 %collective-permute-start.17 = (bf16[256,256]{1,0:T(8,128)(2,1)S(1)}, bf16[256,256]{1,0:T(8,128)(2,1)S(1)}, u32[]{:S(2)}, u32[]{:S(2)}) collective-permute-start(bf16[256,256]{1,0:T(8,128)(2,1)S(1)} %add_convert_fusion.4), channel_id=1, source_target_pairs={{4,0},{5,1},{6,2},{7,3},{8,4},{9,5},{10,6},{11,7},{12,8},{13,9},{1... | collective-permute-start | bytes 393224 | tf_op jit(solution)/shard_map/ppermute | solution.py:295
  73.7 0.8 collective-permute-done.20
  74.6 1.9 %collective-permute-start.21 = (bf16[256,256]{1,0:T(8,128)(2,1)S(1)}, bf16[256,256]{1,0:T(8,128)(2,1)S(1)}, u32[]{:S(2)}, u32[]{:S(2)}) collective-permute-start(bf16[256,256]{1,0:T(8,128)(2,1)S(1)} %add_convert_fusion.1), channel_id=1, source_target_pairs={{4,0},{5,1},{6,2},{7,3},{8,4},{9,5},{10,6},{11,7},{12,8},{13,9},{1... | collective-permute-start | bytes 393224 | tf_op jit(solution)/shard_map/ppermute | solution.py:295
  76.5 3.8 %collective-permute-done.17 = bf16[256,256]{1,0:T(8,128)(2,1)S(1)} collective-permute-done((bf16[256,256]{1,0:T(8,128)(2,1)S(1)}, bf16[256,256]{1,0:T(8,128)(2,1)S(1)}, u32[]{:S(2)}, u32[]{:S(2)}) %collective-permute-start.17) | collective-permute-done | bytes 131104 | tf_op jit(solution)/shard_map/ppermute | solution.py:295
  80.4 1.8 %collective-permute-start.18 = (bf16[128,256]{1,0:T(8,128)(2,1)S(1)}, bf16[128,256]{1,0:T(8,128)(2,1)S(1)}, u32[]{:S(2)}, u32[]{:S(2)}) collective-permute-start(bf16[128,256]{1,0:T(8,128)(2,1)S(1)} %get-tuple-element.43), channel_id=1, source_target_pairs={{0,1},{1,0},{2,3},{3,2},{4,5},{5,4},{6,7},{7,6},{8,9},{9,8},{10,11... | collective-permute-start | bytes 196616 | tf_op jit(solution)/shard_map/ppermute | solution.py:254
  82.1 1.4 %collective-permute-done.21 = bf16[256,256]{1,0:T(8,128)(2,1)S(1)} collective-permute-done((bf16[256,256]{1,0:T(8,128)(2,1)S(1)}, bf16[256,256]{1,0:T(8,128)(2,1)S(1)}, u32[]{:S(2)}, u32[]{:S(2)}) %collective-permute-start.21) | collective-permute-done | bytes 131104 | tf_op jit(solution)/shard_map/ppermute | solution.py:295
  83.6 2.1 %collective-permute-start.23 = (bf16[128,256]{1,0:T(8,128)(2,1)S(1)}, bf16[128,256]{1,0:T(8,128)(2,1)S(1)}, u32[]{:S(2)}, u32[]{:S(2)}) collective-permute-start(bf16[128,256]{1,0:T(8,128)(2,1)S(1)} %get-tuple-element.41), channel_id=1, source_target_pairs={{0,3},{1,2},{2,1},{3,0},{4,7},{5,6},{6,5},{7,4},{8,11},{9,10},{10,... | collective-permute-start | bytes 196616 | tf_op jit(solution)/shard_map/ppermute | solution.py:254
  85.7 0.0 collective-permute-done.12.refs_1_
  85.7 0.6 collective-permute-start.22
  86.3 0.0 collective-permute-done.13.refs_2_
  86.3 0.0 collective-permute-done.14.refs_3_
  86.3 0.0 collective-permute-done.18.refs_5_
  86.3 2.0 %collective-permute-done.23.refs_7_ = bf16[128,256]{1,0:T(8,128)(2,1)S(1)} collective-permute-done((bf16[128,256]{1,0:T(8,128)(2,1)S(1)}, bf16[128,256]{1,0:T(8,128)(2,1)S(1)}, u32[]{:S(2)}, u32[]{:S(2)}) %collective-permute-start.23) | collective-permute-done | bytes 65568 | tf_op jit(solution)/shard_map/ppermute | solution.py:254
  88.3 1.4 %collective-permute-done.22.refs_6_ = bf16[128,256]{1,0:T(8,128)(2,1)S(1)} collective-permute-done((bf16[128,256]{1,0:T(8,128)(2,1)S(1)}, bf16[128,256]{1,0:T(8,128)(2,1)S(1)}, u32[]{:S(2)}, u32[]{:S(2)}) %collective-permute-start.22) | collective-permute-done | bytes 65568 | tf_op jit(solution)/shard_map/ppermute | solution.py:254
  89.7 1.5 %shard_map.75 = (bf16[128,2560]{1,0:T(8,128)(2,1)}, bf16[128,512]{1,0:T(8,128)(2,1)}, bf16[128,512]{1,0:T(8,128)(2,1)}) custom-call(s32[2]{0:T(128)S(1)} %pad_add_fusion.info, bf16[128,640]{1,0:T(8,128)(2,1)S(1)} %get-tuple-element.21.refs_0_, bf16[128,640]{1,0:T(8,128)(2,1)S(1)} %collective-permute-done.12.refs_1_, ...), custom_call_target="tpu_custom_call" | custom-call | tf_op jit(solution)/shard_map/pallas_call | solution.py:232
  (21 shorter events, 0.4 us)
Async XLA Ops:
  0.6 3.6 %copy-start = (bf16[128,2560]{1,0:T(8,128)(2,1)S(1)}, bf16[128,2560]{1,0:T(8,128)(2,1)}, u32[]{:S(2)}) copy-start(bf16[128,2560]{1,0:T(8,128)(2,1)} %param.7) | copy-start | bytes 1966084
  1.7 6.1 %collective-permute-start.1 = (bf16[128,256]{1,0:T(8,128)(2,1)S(1)}, bf16[128,256]{1,0:T(8,128)(2,1)S(1)}, u32[]{:S(2)}, u32[]{:S(2)}) collective-permute-start(bf16[128,256]{1,0:T(8,128)(2,1)S(1)} %pad_maximum_fusion.6), channel_id=1, source_target_pairs={{0,2},{1,3},{2,0},{3,1},{4,6},{5,7},{6,4},{7,5},{8,10},{9,11},{10,... | collective-permute-start | bytes 196616 | tf_op jit(solution)/shard_map/ppermute | solution.py:254
  3.0 8.0 %collective-permute-start = (bf16[128,256]{1,0:T(8,128)(2,1)S(1)}, bf16[128,256]{1,0:T(8,128)(2,1)S(1)}, u32[]{:S(2)}, u32[]{:S(2)}) collective-permute-start(bf16[128,256]{1,0:T(8,128)(2,1)S(1)} %pad_maximum_fusion.5), channel_id=1, source_target_pairs={{0,1},{1,0},{2,3},{3,2},{4,5},{5,4},{6,7},{7,6},{8,9},{9,8},{10,11... | collective-permute-start | bytes 196616 | tf_op jit(solution)/shard_map/ppermute | solution.py:254
  4.0 3.8 %collective-permute-start.2 = (bf16[128,256]{1,0:T(8,128)(2,1)S(1)}, bf16[128,256]{1,0:T(8,128)(2,1)S(1)}, u32[]{:S(2)}, u32[]{:S(2)}) collective-permute-start(bf16[128,256]{1,0:T(8,128)(2,1)S(1)} %pad_maximum_fusion.7), channel_id=1, source_target_pairs={{0,3},{1,2},{2,1},{3,0},{4,7},{5,6},{6,5},{7,4},{8,11},{9,10},{10,... | collective-permute-start | bytes 196616 | tf_op jit(solution)/shard_map/ppermute | solution.py:254
  5.6 21.6 %collective-permute-start.4 = (bf16[128,1280]{1,0:T(8,128)(2,1)S(1)}, bf16[128,1280]{1,0:T(8,128)(2,1)S(1)}, u32[]{:S(2)}, u32[]{:S(2)}) collective-permute-start(bf16[128,1280]{1,0:T(8,128)(2,1)S(1)} %pad_maximum_fusion.2), channel_id=1, source_target_pairs={{0,2},{1,3},{2,0},{3,1},{4,6},{5,7},{6,4},{7,5},{8,10},{9,11},{10,... | collective-permute-start | bytes 983048 | tf_op jit(solution)/shard_map/ppermute | solution.py:254
  6.9 20.3 %collective-permute-start.3 = (bf16[128,1280]{1,0:T(8,128)(2,1)S(1)}, bf16[128,1280]{1,0:T(8,128)(2,1)S(1)}, u32[]{:S(2)}, u32[]{:S(2)}) collective-permute-start(bf16[128,1280]{1,0:T(8,128)(2,1)S(1)} %pad_maximum_fusion.1), channel_id=1, source_target_pairs={{0,1},{1,0},{2,3},{3,2},{4,5},{5,4},{6,7},{7,6},{8,9},{9,8},{10,11... | collective-permute-start | bytes 983048 | tf_op jit(solution)/shard_map/ppermute | solution.py:254
  7.8 7.9 %collective-permute-start.9 = (bf16[256,256]{1,0:T(8,128)(2,1)S(1)}, bf16[256,256]{1,0:T(8,128)(2,1)S(1)}, u32[]{:S(2)}, u32[]{:S(2)}) collective-permute-start(bf16[256,256]{1,0:T(8,128)(2,1)S(1)} %constant_dynamic-update-slice_fusion.kv_b), channel_id=1, source_target_pairs={{0,4},{1,5},{2,6},{3,7},{4,8},{5,9},{6,10},{7,11},{8,12},{9,13},{1... | collective-permute-start | bytes 393224 | tf_op jit(solution)/shard_map/ppermute | solution.py:278
  11.0 6.9 %collective-permute-start.6 = (bf16[256,256]{1,0:T(8,128)(2,1)S(1)}, bf16[256,256]{1,0:T(8,128)(2,1)S(1)}, u32[]{:S(2)}, u32[]{:S(2)}) collective-permute-start(bf16[256,256]{1,0:T(8,128)(2,1)S(1)} %pad_maximum_fusion.4.kv_a), channel_id=1, source_target_pairs={{0,4},{1,5},{2,6},{3,7},{4,8},{5,9},{6,10},{7,11},{8,12},{9,13},{1... | collective-permute-start | bytes 393224 | tf_op jit(solution)/shard_map/ppermute | solution.py:278
  14.3 12.9 %collective-permute-start.5 = (bf16[128,1280]{1,0:T(8,128)(2,1)S(1)}, bf16[128,1280]{1,0:T(8,128)(2,1)S(1)}, u32[]{:S(2)}, u32[]{:S(2)}) collective-permute-start(bf16[128,1280]{1,0:T(8,128)(2,1)S(1)} %pad_maximum_fusion.3), channel_id=1, source_target_pairs={{0,3},{1,2},{2,1},{3,0},{4,7},{5,6},{6,5},{7,4},{8,11},{9,10},{10,... | collective-permute-start | bytes 983048 | tf_op jit(solution)/shard_map/ppermute | solution.py:254
  15.7 7.1 %collective-permute-start.10 = (bf16[256,256]{1,0:T(8,128)(2,1)S(1)}, bf16[256,256]{1,0:T(8,128)(2,1)S(1)}, u32[]{:S(2)}, u32[]{:S(2)}) collective-permute-start(bf16[256,256]{1,0:T(8,128)(2,1)S(1)} %collective-permute-done.9.kv_b), channel_id=1, source_target_pairs={{0,4},{1,5},{2,6},{3,7},{4,8},{5,9},{6,10},{7,11},{8,12},{9,13},{1... | collective-permute-start | bytes 393224 | tf_op jit(solution)/shard_map/ppermute | solution.py:278
  18.0 6.9 %collective-permute-start.7 = (bf16[256,256]{1,0:T(8,128)(2,1)S(1)}, bf16[256,256]{1,0:T(8,128)(2,1)S(1)}, u32[]{:S(2)}, u32[]{:S(2)}) collective-permute-start(bf16[256,256]{1,0:T(8,128)(2,1)S(1)} %collective-permute-done.6.kv_a), channel_id=1, source_target_pairs={{0,4},{1,5},{2,6},{3,7},{4,8},{5,9},{6,10},{7,11},{8,12},{9,13},{1... | collective-permute-start | bytes 393224 | tf_op jit(solution)/shard_map/ppermute | solution.py:278
  22.8 12.7 %collective-permute-start.11 = (bf16[256,256]{1,0:T(8,128)(2,1)S(1)}, bf16[256,256]{1,0:T(8,128)(2,1)S(1)}, u32[]{:S(2)}, u32[]{:S(2)}) collective-permute-start(bf16[256,256]{1,0:T(8,128)(2,1)S(1)} %collective-permute-done.10.kv_b), channel_id=1, source_target_pairs={{0,4},{1,5},{2,6},{3,7},{4,8},{5,9},{6,10},{7,11},{8,12},{9,13},{1... | collective-permute-start | bytes 393224 | tf_op jit(solution)/shard_map/ppermute | solution.py:278
  24.8 10.7 %collective-permute-start.8 = (bf16[256,256]{1,0:T(8,128)(2,1)S(1)}, bf16[256,256]{1,0:T(8,128)(2,1)S(1)}, u32[]{:S(2)}, u32[]{:S(2)}) collective-permute-start(bf16[256,256]{1,0:T(8,128)(2,1)S(1)} %collective-permute-done.7.kv_a), channel_id=1, source_target_pairs={{0,4},{1,5},{2,6},{3,7},{4,8},{5,9},{6,10},{7,11},{8,12},{9,13},{1... | collective-permute-start | bytes 393224 | tf_op jit(solution)/shard_map/ppermute | solution.py:278
  37.9 23.3 %collective-permute-start.19 = (bf16[256,256]{1,0:T(8,128)(2,1)S(1)}, bf16[256,256]{1,0:T(8,128)(2,1)S(1)}, u32[]{:S(2)}, u32[]{:S(2)}) collective-permute-start(bf16[256,256]{1,0:T(8,128)(2,1)S(1)} %convert_element_type.49), channel_id=1, source_target_pairs={{4,0},{5,1},{6,2},{7,3},{8,4},{9,5},{10,6},{11,7},{12,8},{13,9},{1... | collective-permute-start | bytes 393224 | tf_op jit(solution)/shard_map/ppermute | solution.py:295
  39.8 19.4 %collective-permute-start.15 = (bf16[256,256]{1,0:T(8,128)(2,1)S(1)}, bf16[256,256]{1,0:T(8,128)(2,1)S(1)}, u32[]{:S(2)}, u32[]{:S(2)}) collective-permute-start(bf16[256,256]{1,0:T(8,128)(2,1)S(1)} %convert_element_type.42), channel_id=1, source_target_pairs={{4,0},{5,1},{6,2},{7,3},{8,4},{9,5},{10,6},{11,7},{12,8},{13,9},{1... | collective-permute-start | bytes 393224 | tf_op jit(solution)/shard_map/ppermute | solution.py:295
  54.4 31.3 %collective-permute-start.12 = (bf16[128,640]{1,0:T(8,128)(2,1)S(1)}, bf16[128,640]{1,0:T(8,128)(2,1)S(1)}, u32[]{:S(2)}, u32[]{:S(2)}) collective-permute-start(bf16[128,640]{1,0:T(8,128)(2,1)S(1)} %get-tuple-element.22), channel_id=1, source_target_pairs={{0,1},{1,0},{2,3},{3,2},{4,5},{5,4},{6,7},{7,6},{8,9},{9,8},{10,11... | collective-permute-start | bytes 491528 | tf_op jit(solution)/shard_map/ppermute | solution.py:254
  57.5 28.8 %collective-permute-start.13 = (bf16[128,640]{1,0:T(8,128)(2,1)S(1)}, bf16[128,640]{1,0:T(8,128)(2,1)S(1)}, u32[]{:S(2)}, u32[]{:S(2)}) collective-permute-start(bf16[128,640]{1,0:T(8,128)(2,1)S(1)} %get-tuple-element.23), channel_id=1, source_target_pairs={{0,2},{1,3},{2,0},{3,1},{4,6},{5,7},{6,4},{7,5},{8,10},{9,11},{10,... | collective-permute-start | bytes 491528 | tf_op jit(solution)/shard_map/ppermute | solution.py:254
  58.4 27.9 %collective-permute-start.14 = (bf16[128,640]{1,0:T(8,128)(2,1)S(1)}, bf16[128,640]{1,0:T(8,128)(2,1)S(1)}, u32[]{:S(2)}, u32[]{:S(2)}) collective-permute-start(bf16[128,640]{1,0:T(8,128)(2,1)S(1)} %get-tuple-element.24), channel_id=1, source_target_pairs={{0,3},{1,2},{2,1},{3,0},{4,7},{5,6},{6,5},{7,4},{8,11},{9,10},{10,... | collective-permute-start | bytes 491528 | tf_op jit(solution)/shard_map/ppermute | solution.py:254
  59.2 12.5 %collective-permute-start.16 = (bf16[256,256]{1,0:T(8,128)(2,1)S(1)}, bf16[256,256]{1,0:T(8,128)(2,1)S(1)}, u32[]{:S(2)}, u32[]{:S(2)}) collective-permute-start(bf16[256,256]{1,0:T(8,128)(2,1)S(1)} %add_convert_fusion.5), channel_id=1, source_target_pairs={{4,0},{5,1},{6,2},{7,3},{8,4},{9,5},{10,6},{11,7},{12,8},{13,9},{1... | collective-permute-start | bytes 393224 | tf_op jit(solution)/shard_map/ppermute | solution.py:295
  61.2 13.3 %collective-permute-start.20 = (bf16[256,256]{1,0:T(8,128)(2,1)S(1)}, bf16[256,256]{1,0:T(8,128)(2,1)S(1)}, u32[]{:S(2)}, u32[]{:S(2)}) collective-permute-start(bf16[256,256]{1,0:T(8,128)(2,1)S(1)} %add_convert_fusion.2), channel_id=1, source_target_pairs={{4,0},{5,1},{6,2},{7,3},{8,4},{9,5},{10,6},{11,7},{12,8},{13,9},{1... | collective-permute-start | bytes 393224 | tf_op jit(solution)/shard_map/ppermute | solution.py:295
  71.8 8.6 %collective-permute-start.17 = (bf16[256,256]{1,0:T(8,128)(2,1)S(1)}, bf16[256,256]{1,0:T(8,128)(2,1)S(1)}, u32[]{:S(2)}, u32[]{:S(2)}) collective-permute-start(bf16[256,256]{1,0:T(8,128)(2,1)S(1)} %add_convert_fusion.4), channel_id=1, source_target_pairs={{4,0},{5,1},{6,2},{7,3},{8,4},{9,5},{10,6},{11,7},{12,8},{13,9},{1... | collective-permute-start | bytes 393224 | tf_op jit(solution)/shard_map/ppermute | solution.py:295
  74.6 9.0 %collective-permute-start.21 = (bf16[256,256]{1,0:T(8,128)(2,1)S(1)}, bf16[256,256]{1,0:T(8,128)(2,1)S(1)}, u32[]{:S(2)}, u32[]{:S(2)}) collective-permute-start(bf16[256,256]{1,0:T(8,128)(2,1)S(1)} %add_convert_fusion.1), channel_id=1, source_target_pairs={{4,0},{5,1},{6,2},{7,3},{8,4},{9,5},{10,6},{11,7},{12,8},{13,9},{1... | collective-permute-start | bytes 393224 | tf_op jit(solution)/shard_map/ppermute | solution.py:295
  80.4 5.9 %collective-permute-start.18 = (bf16[128,256]{1,0:T(8,128)(2,1)S(1)}, bf16[128,256]{1,0:T(8,128)(2,1)S(1)}, u32[]{:S(2)}, u32[]{:S(2)}) collective-permute-start(bf16[128,256]{1,0:T(8,128)(2,1)S(1)} %get-tuple-element.43), channel_id=1, source_target_pairs={{0,1},{1,0},{2,3},{3,2},{4,5},{5,4},{6,7},{7,6},{8,9},{9,8},{10,11... | collective-permute-start | bytes 196616 | tf_op jit(solution)/shard_map/ppermute | solution.py:254
  83.6 4.8 %collective-permute-start.23 = (bf16[128,256]{1,0:T(8,128)(2,1)S(1)}, bf16[128,256]{1,0:T(8,128)(2,1)S(1)}, u32[]{:S(2)}, u32[]{:S(2)}) collective-permute-start(bf16[128,256]{1,0:T(8,128)(2,1)S(1)} %get-tuple-element.41), channel_id=1, source_target_pairs={{0,3},{1,2},{2,1},{3,0},{4,7},{5,6},{6,5},{7,4},{8,11},{9,10},{10,... | collective-permute-start | bytes 196616 | tf_op jit(solution)/shard_map/ppermute | solution.py:254
  85.7 4.1 %collective-permute-start.22 = (bf16[128,256]{1,0:T(8,128)(2,1)S(1)}, bf16[128,256]{1,0:T(8,128)(2,1)S(1)}, u32[]{:S(2)}, u32[]{:S(2)}) collective-permute-start(bf16[128,256]{1,0:T(8,128)(2,1)S(1)} %get-tuple-element.42), channel_id=1, source_target_pairs={{0,2},{1,3},{2,0},{3,1},{4,6},{5,7},{6,4},{7,5},{8,10},{9,11},{10,... | collective-permute-start | bytes 196616 | tf_op jit(solution)/shard_map/ppermute | solution.py:254

commit v2 on v1

v2 whole, which is shorter than its diff:
```python
from functools import partial

import jax
import jax.numpy as jnp
from jax import lax
from jax.experimental import pallas as pl
from jax.experimental.pallas import tpu as pltpu
from jax.sharding import PartitionSpec as P

DH = 128
KVH = 4
QPG = 5
SCALING = DH ** (-0.5)
LOG2E = 1.4426950408889634
CONTRACT_LAST = (((1,), (1,)), ((), ()))
VMEM_BYTES = 28 * 1024 * 1024
EXTRA = 8


def token_places(rank, tokens, dim):
    shape = (tokens, 1) if dim == 0 else (1, tokens)
    own = lax.broadcasted_iota(jnp.int32, shape, dim)
    return jnp.concatenate([own + tokens * (rank ^ d) for d in range(KVH)], axis=dim)


def causal_mask(info, tokens):
    return token_places(info[1], tokens, 0) <= token_places(info[1], tokens, 1)


def stacked(refs, head):
    return jnp.concatenate([ref[:, head * DH : (head + 1) * DH] for ref in refs], axis=0)


def keys_values(refs):
    return (
        jnp.concatenate([ref[:, :DH] for ref in refs], axis=0),
        jnp.concatenate([ref[:, DH:] for ref in refs], axis=0),
    )


def scaled_scores(key_rows, query_rows):
    raw = lax.dot_general(key_rows, query_rows, CONTRACT_LAST, preferred_element_type=jnp.float32)
    return raw * (SCALING * LOG2E)


def forward_kernel(offset, last, info, *refs):
    refs = list(refs)
    kv = [refs.pop(0) for _ in range(2)]
    q = [refs.pop(0) for _ in range(KVH)]
    g = [refs.pop(0) for _ in range(KVH)] if last else None
    if offset:
        old_stats, old_sums = refs.pop(0), refs.pop(0)
    if last:
        finals, stats, sums = refs
    else:
        stats, sums = refs
    tokens = q[0].shape[0]

    def update():
        key_rows, value_rows = keys_values(kv)
        span = key_rows.shape[0]
        left = jnp.concatenate([value_rows.T, jnp.ones((EXTRA, span), jnp.bfloat16)], axis=0)
        mask = None if offset else causal_mask(info, tokens)
        for h in range(QPG):
            scores = scaled_scores(key_rows, stacked(q, h))
            if offset == 0:
                scores = jnp.where(mask, scores, -jnp.inf)
            top = jnp.max(scores, axis=0, keepdims=True)
            if offset:
                old_top = old_stats[h, 0:1]
                top = jnp.maximum(old_top, top)
                shrink = jnp.exp2(old_top - top)
            weights = jnp.exp2(scores - top)
            total = jnp.sum(weights, axis=0, keepdims=True)
            added = jnp.dot(left, weights.astype(jnp.bfloat16), preferred_element_type=jnp.float32)
            if offset:
                total = total + shrink * old_stats[h, 1:2]
                added = added + shrink * old_sums[h]
            stats[h, 0:1] = top
            stats[h, 1:2] = total
            sums[h] = added

    if offset == 0:
        update()
    else:
        pl.when(info[0] >= offset)(update)

        @pl.when(info[0] < offset)
        def _():
            stats[...] = old_stats[...]
            sums[...] = old_sums[...]

    if last:
        for h in range(QPG):
            grads = stacked(g, h).T.astype(jnp.float32)
            weighted = jnp.sum(sums[h, :DH] * grads, axis=0, keepdims=True)
            finals[h, 0:1] = stats[h, 0:1] + jnp.log2(stats[h, 1:2])
            finals[h, 1:2] = weighted / sums[h, DH : DH + 1]


def backward_kernel(offset, first, info, *refs):
    refs = list(refs)
    kv = [refs.pop(0) for _ in range(2)]
    q = [refs.pop(0) for _ in range(KVH)]
    g = [refs.pop(0) for _ in range(KVH)]
    finals = refs.pop(0)
    dq_old = None if first else refs.pop(0)
    dkv = refs.pop(0)
    dq_refs = refs
    tokens = q[0].shape[0]
    last = offset == 0

    def work():
        key_rows, value_rows = keys_values(kv)
        key_columns = key_rows.T
        mask = causal_mask(info, tokens) if last else None
        for h in range(QPG):
            query_rows = stacked(q, h)
            grad_rows = stacked(g, h)
            probs = jnp.exp2(scaled_scores(key_rows, query_rows) - finals[h, 0:1])
            if last:
                probs = jnp.where(mask, probs, 0.0)
            grad_probs = lax.dot_general(
                value_rows, grad_rows, CONTRACT_LAST, preferred_element_type=jnp.float32
            )
            grad_scores = (probs * (grad_probs - finals[h, 1:2]) * SCALING).astype(jnp.bfloat16)
            dk = jnp.dot(grad_scores, query_rows, preferred_element_type=jnp.float32)
            dv = jnp.dot(
                probs.astype(jnp.bfloat16), grad_rows, preferred_element_type=jnp.float32
            )
            if h == 0:
                dkv[:, :DH] = dk
                dkv[:, DH:] = dv
            else:
                dkv[:, :DH] += dk
                dkv[:, DH:] += dv
            dq = jnp.dot(key_columns, grad_scores, preferred_element_type=jnp.float32)
            if dq_old is not None:
                dq = dq + dq_old[h]
            if last:
                rows = dq.T.astype(jnp.bfloat16)
                for d in range(KVH):
                    dq_refs[d][:, h * DH : (h + 1) * DH] = rows[d * tokens : (d + 1) * tokens]
            else:
                dq_refs[0][h] = dq

    if last:
        work()
    else:
        pl.when(info[0] >= offset)(work)

        @pl.when(info[0] < offset)
        def _():
            dkv[...] = jnp.zeros_like(dkv)
            dq_refs[0][...] = jnp.zeros_like(dq_refs[0]) if dq_old is None else dq_old[...]


def local_call(kernel, shapes, flops, info, *operands, scratch=()):
    vmem = pl.BlockSpec(memory_space=pltpu.VMEM)
    return pl.pallas_call(
        kernel,
        in_specs=[pl.BlockSpec(memory_space=pltpu.SMEM)] + [vmem] * len(operands),
        out_specs=[vmem] * len(shapes),
        out_shape=shapes,
        scratch_shapes=scratch,
        compiler_params=pltpu.CompilerParams(vmem_limit_bytes=VMEM_BYTES),
        cost_estimate=pl.CostEstimate(flops=flops, bytes_accessed=1 << 20, transcendentals=0),
    )(info, *operands)


def forward_call(offset, last, info, kv, q, g, state):
    tokens = q[0].shape[0]
    span = KVH * tokens
    stats = jax.ShapeDtypeStruct((QPG, 8, span), jnp.float32)
    sums = jax.ShapeDtypeStruct((QPG, DH + EXTRA, span), jnp.float32)
    shapes = [stats] if last else [stats, sums]
    scratch = [pltpu.VMEM(kept.shape, kept.dtype) for kept in (stats, sums)] if last else []
    return local_call(
        partial(forward_kernel, offset, last),
        shapes,
        2 * 2 * QPG * span * span * DH * 2,
        info,
        *kv,
        *q,
        *(g if last else []),
        *state,
        scratch=scratch,
    )


def backward_call(offset, info, kv, q, g, finals, dq_old):
    tokens = q[0].shape[0]
    span = KVH * tokens
    first = dq_old is None
    shapes = [jax.ShapeDtypeStruct((span, 2 * DH), jnp.float32)]
    if offset:
        shapes += [jax.ShapeDtypeStruct((QPG, DH, span), jnp.float32)]
    else:
        shapes += [jax.ShapeDtypeStruct((tokens, QPG * DH), jnp.bfloat16)] * KVH
    return local_call(
        partial(backward_kernel, offset, first),
        shapes,
        5 * 2 * QPG * span * span * DH * 2,
        info,
        *kv,
        *q,
        *g,
        finals,
        *([] if first else [dq_old]),
    )


def place_kernel(info, *refs):
    rank = info[1]
    sources, targets = refs[: 2 * KVH], refs[2 * KVH :]
    query_grad, key_grad, value_grad = targets
    for d in range(KVH):
        head = rank ^ d
        wide = pl.ds(pl.multiple_of(head * (QPG * DH), DH), QPG * DH)
        narrow = pl.ds(pl.multiple_of(head * DH, DH), DH)
        query_grad[:, wide] = sources[d][...]
        key_grad[:, narrow] = sources[KVH + d][:, :DH]
        value_grad[:, narrow] = sources[KVH + d][:, DH:]


def place_call(info, dq, dkv):
    tokens = dq[0].shape[0]
    shapes = [
        jax.ShapeDtypeStruct((tokens, KVH * QPG * DH), jnp.bfloat16),
        jax.ShapeDtypeStruct((tokens, KVH * DH), jnp.bfloat16),
        jax.ShapeDtypeStruct((tokens, KVH * DH), jnp.bfloat16),
    ]
    return local_call(place_kernel, shapes, 0, info, *dq, *dkv)


def per_device(queries, keys, values, out_grad):
    devices = lax.axis_size("seq")
    planes = devices // KVH
    tokens = queries.shape[0]
    device = lax.axis_index("seq")
    rank = device % KVH
    info = jnp.stack([device // KVH, rank]).astype(jnp.int32)

    def swap(array, d):
        if d == 0:
            return array
        return lax.ppermute(array, "seq", [(i, i ^ d) for i in range(devices)])

    def columns(array, head, width):
        return lax.dynamic_slice_in_dim(array, head * width, width, axis=1)

    kv_pieces = []
    for d in range(KVH):
        head = rank ^ d
        piece = jnp.concatenate([columns(keys, head, DH), columns(values, head, DH)], axis=1)
        kv_pieces.append(swap(piece, d))
    q = [swap(columns(queries, rank ^ d, QPG * DH), d) for d in range(KVH)]
    g = [swap(columns(out_grad, rank ^ d, QPG * DH), d) for d in range(KVH)]
    chain = [
        (
            jnp.concatenate(kv_pieces[:2], axis=0),
            jnp.concatenate(kv_pieces[2:], axis=0),
        )
    ]
    for step in range(1, planes):
        pairs = [(i, i + KVH) for i in range((step - 1) * KVH, devices - KVH)]
        chain.append(tuple(lax.ppermute(half, "seq", pairs) for half in chain[-1]))
    state = []
    for offset in range(planes):
        last = offset == planes - 1
        state = forward_call(offset, last, info, chain[offset], q, g, state)
    finals = state[0]

    dq = None
    arrived = None
    for offset in reversed(range(planes)):
        results = backward_call(offset, info, chain[offset], q, g, finals, dq)
        total, dq = results[0], results[1:]
        if offset:
            dq = dq[0]
        if arrived is not None:
            total = total + arrived.astype(jnp.float32)
        total = total.astype(jnp.bfloat16)
        if offset:
            pairs = [(i + KVH, i) for i in range((offset - 1) * KVH, devices - KVH)]
            arrived = lax.ppermute(total, "seq", pairs)
    dq_back = [swap(dq[d], d) for d in range(KVH)]
    dkv_back = [swap(total[d * tokens : (d + 1) * tokens], d) for d in range(KVH)]
    return tuple(place_call(info, dq_back, dkv_back))


def solution(mesh):
    spec = P(("groups", "seq"), None)
    return jax.shard_map(
        per_device,
        mesh=mesh,
        in_specs=(spec,) * 4,
        out_specs=(spec,) * 3,
        check_vma=False,
    )
```

time: 92 us -> 80.9 us (0.88)
  starting transfers between devices: 43 us -> 31.5 us
  waiting for transfers between devices: 19.8 us -> 26.7 us
  Pallas kernels: 24.7 us -> 19.2 us
  local copies, waits for them, and re-layouts: 2.31 us -> 1.16 us
    ppermute x12 -> x9, starting transfers between devices: 27.6 us -> 16.5 us  [the longest x6 12.4 us: per_device(): lax.ppermute(half, 'seq', pairs)]
    ppermute x12 -> x15, waiting for transfers between devices: 3.52 us -> 12.4 us  [swap(): return lax.ppermute(array, 'seq', [(i, i ^ d) for i in range(devices)])]
    pallas_call x9, Pallas kernels: 24.7 us -> 19.2 us  [local_call(): pl.pallas_call(kernel, in_specs=[pl.BlockSpec(memory_space=pltpu.SMEM)] +...]
    ppermute x12 -> x9, waiting for transfers between devices: 16.3 us -> 14.3 us  [the longest x3 14.3 us: per_device(): arrived = lax.ppermute(total, 'seq', pairs)]
    dynamic_slice x2 -> x3, local copies, waits for them, and re-layouts: 2.26 us -> 1.13 us  [columns(): return lax.dynamic_slice_in_dim(array, head * width, width, axis=1)]
    ppermute x12 -> x15, starting transfers between devices: 15.4 us -> 14.9 us  [swap(): return lax.ppermute(array, 'seq', [(i, i ^ d) for i in range(devices)])]
  transfers between devices with their start and end apart: 24 -> 24, of which waited for: 9 -> 8; matrix products, arithmetic and copies ran while one was open for 2% -> 0% of each run, Pallas kernels for 23% -> 20%
where the time goes in v2:
time: 80.9 us; the launch traced here: 79.9 us
  starting transfers between devices  31.5 us (39%)
  waiting for transfers between devices  26.7 us (33%)
  Pallas kernels  19.2 us (24%)
  local copies, waits for them, and re-layouts  1.16 us (1%)
  between operations  1 us (1%)
    pallas_call x9, Pallas kernels, local_call(): pl.pallas_call(kernel, in_specs=[pl.BlockSpec(memory_space=pltpu.SMEM)] +...  19.2 us
    ppermute x15, starting transfers between devices, swap(): return lax.ppermute(array, 'seq', [(i, i ^ d) for i in range(devices)])  14.9 us
    ppermute x3, waiting for transfers between devices, per_device(): arrived = lax.ppermute(total, 'seq', pairs)  14.3 us
    ppermute x6, starting transfers between devices, per_device(): lax.ppermute(half, 'seq', pairs)  12.4 us
    ppermute x15, waiting for transfers between devices, swap(): return lax.ppermute(array, 'seq', [(i, i ^ d) for i in range(devices)])  12.4 us
    ppermute x3, starting transfers between devices, per_device(): arrived = lax.ppermute(total, 'seq', pairs)  4.11 us
  transfers between devices with their start and end apart: 24, of which 8 were waited for; matrix products, arithmetic and copies ran while one was open for 0% of the time, Pallas kernels for 20%

profile of v2, /device:TPU:9, one launch (start us, length us, event | category | flops | bytes accessed | tf_op | source)
XLA Modules:
  0.0 79.9 jit_solution(2652655898206755683)
XLA Ops:
  0.7 1.0 %constant_dynamic-slice_fusion.8 = (bf16[128,128]{1,0:T(8,128)(2,1)S(1)}, bf16[128,128]{1,0:T(8,128)(2,1)S(1)}, bf16[128,128]{1,0:T(8,128)(2,1)S(1)}, bf16[128,1...) fusion(bf16[128,512]{1,0:T(8,128)(2,1)} %param.6, ...), kind=kLoop, calls=%fused_computation.17 | loop fusion | bytes 524304 | tf_op jit(solution)/shard_map/dynamic_slice | solution.py:250
  1.7 1.3 %collective-permute-start.1 = (bf16[128,256]{1,0:T(8,128)(2,1)S(1)}, bf16[128,256]{1,0:T(8,128)(2,1)S(1)}, u32[]{:S(2)}, u32[]{:S(2)}) collective-permute-start(bf16[128,256]{1,0:T(8,128)(2,1)S(1)} %pad_maximum_fusion.2), channel_id=1, source_target_pairs={{0,2},{1,3},{2,0},{3,1},{4,6},{5,7},{6,4},{7,5},{8,10},{9,11},{10,... | collective-permute-start | bytes 196616 | tf_op jit(solution)/shard_map/ppermute | solution.py:247
  3.0 1.0 %collective-permute-start = (bf16[128,256]{1,0:T(8,128)(2,1)S(1)}, bf16[128,256]{1,0:T(8,128)(2,1)S(1)}, u32[]{:S(2)}, u32[]{:S(2)}) collective-permute-start(bf16[128,256]{1,0:T(8,128)(2,1)S(1)} %pad_maximum_fusion.1), channel_id=1, source_target_pairs={{0,1},{1,0},{2,3},{3,2},{4,5},{5,4},{6,7},{7,6},{8,9},{9,8},{10,11... | collective-permute-start | bytes 196616 | tf_op jit(solution)/shard_map/ppermute | solution.py:247
  4.1 0.2 collective-permute-start.2
  4.3 0.6 collective-permute-done.1
  4.9 3.0 %collective-permute-done.2 = bf16[128,256]{1,0:T(8,128)(2,1)S(1)} collective-permute-done((bf16[128,256]{1,0:T(8,128)(2,1)S(1)}, bf16[128,256]{1,0:T(8,128)(2,1)S(1)}, u32[]{:S(2)}, u32[]{:S(2)}) %collective-permute-start.2) | collective-permute-done | bytes 65568 | tf_op jit(solution)/shard_map/ppermute | solution.py:247
  7.9 3.2 %collective-permute-start.12 = (bf16[256,256]{1,0:T(8,128)(2,1)S(1)}, bf16[256,256]{1,0:T(8,128)(2,1)S(1)}, u32[]{:S(2)}, u32[]{:S(2)}) collective-permute-start(bf16[256,256]{1,0:T(8,128)(2,1)S(1)} %constant_dynamic-update-slice_fusion.refs_1_), channel_id=1, source_target_pairs={{0,4},{1,5},{2,6},{3,7},{4,8},{5,9},{6,10},{7,11},{8,12},{9,13},{1... | collective-permute-start | bytes 393224 | tf_op jit(solution)/shard_map/ppermute | solution.py:267
  11.1 0.0 collective-permute-done
  11.1 3.2 %collective-permute-start.9 = (bf16[256,256]{1,0:T(8,128)(2,1)S(1)}, bf16[256,256]{1,0:T(8,128)(2,1)S(1)}, u32[]{:S(2)}, u32[]{:S(2)}) collective-permute-start(bf16[256,256]{1,0:T(8,128)(2,1)S(1)} %pad_maximum_fusion.refs_0_), channel_id=1, source_target_pairs={{0,4},{1,5},{2,6},{3,7},{4,8},{5,9},{6,10},{7,11},{8,12},{9,13},{1... | collective-permute-start | bytes 393224 | tf_op jit(solution)/shard_map/ppermute | solution.py:267
  14.3 0.1 constant_dynamic-slice_fusion.4
  14.4 1.4 %collective-permute-start.5 = (bf16[128,640]{1,0:T(8,128)(2,1)S(1)}, bf16[128,640]{1,0:T(8,128)(2,1)S(1)}, u32[]{:S(2)}, u32[]{:S(2)}) collective-permute-start(bf16[128,640]{1,0:T(8,128)(2,1)S(1)} %get-tuple-element.41), channel_id=1, source_target_pairs={{0,3},{1,2},{2,1},{3,0},{4,7},{5,6},{6,5},{7,4},{8,11},{9,10},{10,... | collective-permute-start | bytes 491528 | tf_op jit(solution)/shard_map/ppermute | solution.py:247
  15.8 0.0 collective-permute-start.3
  15.8 0.6 collective-permute-start.4
  16.4 0.1 constant_dynamic-slice_fusion
  16.5 0.0 collective-permute-done.12.refs_1_
  16.5 1.8 %collective-permute-start.13 = (bf16[256,256]{1,0:T(8,128)(2,1)S(1)}, bf16[256,256]{1,0:T(8,128)(2,1)S(1)}, u32[]{:S(2)}, u32[]{:S(2)}) collective-permute-start(bf16[256,256]{1,0:T(8,128)(2,1)S(1)} %collective-permute-done.12.refs_1_), channel_id=1, source_target_pairs={{4,8},{5,9},{6,10},{7,11},{8,12},{9,13},{10,14},{11,15},{20,24},{2... | collective-permute-start | bytes 393224 | tf_op jit(solution)/shard_map/ppermute | solution.py:267
  18.3 0.0 collective-permute-done.9.refs_0_
  18.3 2.9 %collective-permute-start.10 = (bf16[256,256]{1,0:T(8,128)(2,1)S(1)}, bf16[256,256]{1,0:T(8,128)(2,1)S(1)}, u32[]{:S(2)}, u32[]{:S(2)}) collective-permute-start(bf16[256,256]{1,0:T(8,128)(2,1)S(1)} %collective-permute-done.9.refs_0_), channel_id=1, source_target_pairs={{4,8},{5,9},{6,10},{7,11},{8,12},{9,13},{10,14},{11,15},{20,24},{2... | collective-permute-start | bytes 393224 | tf_op jit(solution)/shard_map/ppermute | solution.py:267
  21.2 0.1 pad_add_fusion.info
  21.3 0.0 collective-permute-done.5.refs_5_
  21.3 2.6 %collective-permute-start.8 = (bf16[128,640]{1,0:T(8,128)(2,1)S(1)}, bf16[128,640]{1,0:T(8,128)(2,1)S(1)}, u32[]{:S(2)}, u32[]{:S(2)}) collective-permute-start(bf16[128,640]{1,0:T(8,128)(2,1)S(1)} %get-tuple-element.37), channel_id=1, source_target_pairs={{0,3},{1,2},{2,1},{3,0},{4,7},{5,6},{6,5},{7,4},{8,11},{9,10},{10,... | collective-permute-start | bytes 491528 | tf_op jit(solution)/shard_map/ppermute | solution.py:247
  23.9 0.0 collective-permute-done.3.refs_3_
  23.9 0.0 collective-permute-start.6
  23.9 0.7 collective-permute-done.4.refs_4_
  24.6 0.9 %collective-permute-start.7 = (bf16[128,640]{1,0:T(8,128)(2,1)S(1)}, bf16[128,640]{1,0:T(8,128)(2,1)S(1)}, u32[]{:S(2)}, u32[]{:S(2)}) collective-permute-start(bf16[128,640]{1,0:T(8,128)(2,1)S(1)} %get-tuple-element.40), channel_id=1, source_target_pairs={{0,2},{1,3},{2,0},{3,1},{4,6},{5,7},{6,4},{7,5},{8,10},{9,11},{10,... | collective-permute-start | bytes 491528 | tf_op jit(solution)/shard_map/ppermute | solution.py:247
  25.5 3.2 %shard_map.67 = (f32[5,8,512]{2,1,0:T(8,128)S(1)}, f32[5,136,512]{2,1,0:T(8,128)S(1)}) custom-call(s32[2]{0:T(128)S(1)} %pad_add_fusion.info, bf16[256,256]{1,0:T(8,128)(2,1)S(1)} %pad_maximum_fusion.refs_0_, bf16[256,256]{1,0:T(8,128)(2,1)S(1)} %constant_dynamic-update-slice_fusion.refs_1_, bf16[128,640]{1,0:T(8,128)(2,1)S(1)} %get-tuple-element.43.refs_2_, ...), custom_call_target="tpu_custom_call" | custom-call | flops 1342177280 | bytes 1048576 | tf_op jit(solution)/shard_map/pallas_call | solution.py:160
  28.7 0.0 collective-permute-done.13.refs_1_
  28.7 0.7 collective-permute-start.14
  29.4 0.0 collective-permute-done.10.refs_0_
  29.4 0.7 collective-permute-start.11
  30.0 3.4 %shard_map.68 = (f32[5,8,512]{2,1,0:T(8,128)S(1)}, f32[5,136,512]{2,1,0:T(8,128)S(1)}) custom-call(s32[2]{0:T(128)S(1)} %pad_add_fusion.info, bf16[256,256]{1,0:T(8,128)(2,1)S(1)} %collective-permute-done.9.refs_0_, bf16[256,256]{1,0:T(8,128)(2,1)S(1)} %collective-permute-done.12.refs_1_, bf16[128,640]{1,0:T(8,128)(2,1)S(1)} %get-tuple-element.43.refs_2_, ...), custom_call_target="tpu_custom_call" | custom-call | flops 1342177280 | bytes 1048576 | tf_op jit(solution)/shard_map/pallas_call | solution.py:160
  33.4 0.7 shard_map.69
  34.1 0.0 collective-permute-done.8.refs_9_
  34.1 0.0 collective-permute-done.6.refs_7_
  34.1 0.0 collective-permute-done.7.refs_8_
  34.1 0.0 collective-permute-done.14.refs_1_
  34.1 0.0 collective-permute-done.11.refs_0_
  34.1 0.9 %shard_map.70.refs_10_ = f32[5,8,512]{2,1,0:T(8,128)S(1)} custom-call(s32[2]{0:T(128)S(1)} %pad_add_fusion.info, bf16[256,256]{1,0:T(8,128)(2,1)S(1)} %collective-permute-done.11.refs_0_, bf16[256,256]{1,0:T(8,128)(2,1)S(1)} %collective-permute-done.14.refs_1_, bf16[128,640]{1,0:T(8,128)(2,1)S(1)} %get-tuple-element.43.refs_2_, ...), custom_call_target="tpu_custom_call" | custom-call | flops 1342177280 | bytes 1048576 | tf_op jit(solution)/shard_map/pallas_call | solution.py:160
  35.0 0.9 %shard_map.71 = (f32[512,256]{1,0:T(8,128)S(1)}, f32[5,128,512]{2,1,0:T(8,128)S(1)}) custom-call(s32[2]{0:T(128)S(1)} %pad_add_fusion.info, bf16[256,256]{1,0:T(8,128)(2,1)S(1)} %collective-permute-done.11.refs_0_, bf16[256,256]{1,0:T(8,128)(2,1)S(1)} %collective-permute-done.14.refs_1_, bf16[128,640]{1,0:T(8,128)(2,1)S(1)} %get-tuple-element.43.refs_2_, ...), custom_call_target="tpu_custom_call" | custom-call | flops 3355443200 | bytes 1048576 | tf_op jit(solution)/shard_map/pallas_call | solution.py:160
  35.9 0.7 collective-permute-start.18
  36.6 0.7 shard_map.72
  37.3 0.0 collective-permute-done.18
  37.3 0.1 add_convert_fusion.2
  37.4 1.3 %collective-permute-start.19 = (bf16[512,256]{1,0:T(8,128)(2,1)S(1)}, bf16[512,256]{1,0:T(8,128)(2,1)S(1)}, u32[]{:S(2)}, u32[]{:S(2)}) collective-permute-start(bf16[512,256]{1,0:T(8,128)(2,1)S(1)} %add_convert_fusion.2), channel_id=1, source_target_pairs={{8,4},{9,5},{10,6},{11,7},{12,8},{13,9},{14,10},{15,11},{24,20},{2... | collective-permute-start | bytes 786440 | tf_op jit(solution)/shard_map/ppermute | solution.py:286
  38.7 3.8 %shard_map.73 = (f32[512,256]{1,0:T(8,128)S(1)}, f32[5,128,512]{2,1,0:T(8,128)S(1)}) custom-call(s32[2]{0:T(128)S(1)} %pad_add_fusion.info, bf16[256,256]{1,0:T(8,128)(2,1)S(1)} %collective-permute-done.9.refs_0_, bf16[256,256]{1,0:T(8,128)(2,1)S(1)} %collective-permute-done.12.refs_1_, bf16[128,640]{1,0:T(8,128)(2,1)S(1)} %get-tuple-element.43.refs_2_, ...), custom_call_target="tpu_custom_call" | custom-call | flops 3355443200 | bytes 1048576 | tf_op jit(solution)/shard_map/pallas_call | solution.py:160
  42.5 14.3 %collective-permute-done.19 = bf16[512,256]{1,0:T(8,128)(2,1)S(1)} collective-permute-done((bf16[512,256]{1,0:T(8,128)(2,1)S(1)}, bf16[512,256]{1,0:T(8,128)(2,1)S(1)}, u32[]{:S(2)}, u32[]{:S(2)}) %collective-permute-start.19) | collective-permute-done | bytes 262176 | tf_op jit(solution)/shard_map/ppermute | solution.py:286
  56.7 0.1 add_convert_fusion.1
  56.8 2.1 %collective-permute-start.20 = (bf16[512,256]{1,0:T(8,128)(2,1)S(1)}, bf16[512,256]{1,0:T(8,128)(2,1)S(1)}, u32[]{:S(2)}, u32[]{:S(2)}) collective-permute-start(bf16[512,256]{1,0:T(8,128)(2,1)S(1)} %add_convert_fusion.1), channel_id=1, source_target_pairs={{4,0},{5,1},{6,2},{7,3},{8,4},{9,5},{10,6},{11,7},{12,8},{13,9},{1... | collective-permute-start | bytes 786440 | tf_op jit(solution)/shard_map/ppermute | solution.py:286
  58.9 4.3 %shard_map.74 = (f32[512,256]{1,0:T(8,128)S(1)}, bf16[128,640]{1,0:T(8,128)(2,1)S(1)}, bf16[128,640]{1,0:T(8,128)(2,1)S(1)}, bf16[128,640]{1,0:T(8,128)(2,1)S(1)}, bf16[128,640]{1,0:T(8,128)(2,1)S(1)}) custom-call(s32[2]{0:T(128)S(1)} %pad_add_fusion.info, bf16[256,256]{1,0:T(8,128)(2,1)S(1)} %pad_maximum_fusion.refs_0_, ...), custom_call_target="tpu_custom_call" | custom-call | flops 3355443200 | bytes 1048576 | tf_op jit(solution)/shard_map/pallas_call | solution.py:160
  63.2 3.0 %collective-permute-start.15 = (bf16[128,640]{1,0:T(8,128)(2,1)S(1)}, bf16[128,640]{1,0:T(8,128)(2,1)S(1)}, u32[]{:S(2)}, u32[]{:S(2)}) collective-permute-start(bf16[128,640]{1,0:T(8,128)(2,1)S(1)} %get-tuple-element.30), channel_id=1, source_target_pairs={{0,1},{1,0},{2,3},{3,2},{4,5},{5,4},{6,7},{7,6},{8,9},{9,8},{10,11... | collective-permute-start | bytes 491528 | tf_op jit(solution)/shard_map/ppermute | solution.py:247
  66.2 0.9 %collective-permute-start.16 = (bf16[128,640]{1,0:T(8,128)(2,1)S(1)}, bf16[128,640]{1,0:T(8,128)(2,1)S(1)}, u32[]{:S(2)}, u32[]{:S(2)}) collective-permute-start(bf16[128,640]{1,0:T(8,128)(2,1)S(1)} %get-tuple-element.31), channel_id=1, source_target_pairs={{0,2},{1,3},{2,0},{3,1},{4,6},{5,7},{6,4},{7,5},{8,10},{9,11},{10,... | collective-permute-start | bytes 491528 | tf_op jit(solution)/shard_map/ppermute | solution.py:247
  67.2 0.8 collective-permute-start.17
  67.9 0.0 collective-permute-done.20
  67.9 0.1 add_convert_fusion
  68.0 1.0 %collective-permute-start.23 = (bf16[128,256]{1,0:T(8,128)(2,1)S(1)}, bf16[128,256]{1,0:T(8,128)(2,1)S(1)}, u32[]{:S(2)}, u32[]{:S(2)}) collective-permute-start(bf16[128,256]{1,0:T(8,128)(2,1)S(1)} %get-tuple-element.45), channel_id=1, source_target_pairs={{0,3},{1,2},{2,1},{3,0},{4,7},{5,6},{6,5},{7,4},{8,11},{9,10},{10,... | collective-permute-start | bytes 196616 | tf_op jit(solution)/shard_map/ppermute | solution.py:247
  69.1 0.5 collective-permute-start.22
  69.6 0.0 collective-permute-done.15.refs_1_
  69.6 0.6 collective-permute-start.21
  70.2 1.8 %collective-permute-done.16.refs_2_ = bf16[128,640]{1,0:T(8,128)(2,1)S(1)} collective-permute-done((bf16[128,640]{1,0:T(8,128)(2,1)S(1)}, bf16[128,640]{1,0:T(8,128)(2,1)S(1)}, u32[]{:S(2)}, u32[]{:S(2)}) %collective-permute-start.16) | collective-permute-done | bytes 163872 | tf_op jit(solution)/shard_map/ppermute | solution.py:247
  72.0 4.4 %collective-permute-done.17.refs_3_ = bf16[128,640]{1,0:T(8,128)(2,1)S(1)} collective-permute-done((bf16[128,640]{1,0:T(8,128)(2,1)S(1)}, bf16[128,640]{1,0:T(8,128)(2,1)S(1)}, u32[]{:S(2)}, u32[]{:S(2)}) %collective-permute-start.17) | collective-permute-done | bytes 163872 | tf_op jit(solution)/shard_map/ppermute | solution.py:247
  76.4 1.1 %collective-permute-done.23.refs_7_ = bf16[128,256]{1,0:T(8,128)(2,1)S(1)} collective-permute-done((bf16[128,256]{1,0:T(8,128)(2,1)S(1)}, bf16[128,256]{1,0:T(8,128)(2,1)S(1)}, u32[]{:S(2)}, u32[]{:S(2)}) %collective-permute-start.23) | collective-permute-done | bytes 65568 | tf_op jit(solution)/shard_map/ppermute | solution.py:247
  77.5 0.8 collective-permute-done.22.refs_6_
  78.3 0.0 collective-permute-done.21.refs_5_
  78.3 1.6 %shard_map.75 = (bf16[128,2560]{1,0:T(8,128)(2,1)}, bf16[128,512]{1,0:T(8,128)(2,1)}, bf16[128,512]{1,0:T(8,128)(2,1)}) custom-call(s32[2]{0:T(128)S(1)} %pad_add_fusion.info, bf16[128,640]{1,0:T(8,128)(2,1)S(1)} %get-tuple-element.29.refs_0_, bf16[128,640]{1,0:T(8,128)(2,1)S(1)} %collective-permute-done.15.refs_1_, ...), custom_call_target="tpu_custom_call" | custom-call | bytes 1048576 | tf_op jit(solution)/shard_map/pallas_call | solution.py:160
  (12 shorter events, 0.1 us)
Async XLA Ops:
  0.6 13.7 %copy-start = (bf16[128,2560]{1,0:T(8,128)(2,1)S(1)}, bf16[128,2560]{1,0:T(8,128)(2,1)}, u32[]{:S(2)}) copy-start(bf16[128,2560]{1,0:T(8,128)(2,1)} %param.4) | copy-start | bytes 1966084
  0.7 15.8 %copy-start.1 = (bf16[128,2560]{1,0:T(8,128)(2,1)S(1)}, bf16[128,2560]{1,0:T(8,128)(2,1)}, u32[]{:S(2)}) copy-start(bf16[128,2560]{1,0:T(8,128)(2,1)} %param.7) | copy-start | bytes 1966084
  1.7 3.2 %collective-permute-start.1 = (bf16[128,256]{1,0:T(8,128)(2,1)S(1)}, bf16[128,256]{1,0:T(8,128)(2,1)S(1)}, u32[]{:S(2)}, u32[]{:S(2)}) collective-permute-start(bf16[128,256]{1,0:T(8,128)(2,1)S(1)} %pad_maximum_fusion.2), channel_id=1, source_target_pairs={{0,2},{1,3},{2,0},{3,1},{4,6},{5,7},{6,4},{7,5},{8,10},{9,11},{10,... | collective-permute-start | bytes 196616 | tf_op jit(solution)/shard_map/ppermute | solution.py:247
  3.0 8.0 %collective-permute-start = (bf16[128,256]{1,0:T(8,128)(2,1)S(1)}, bf16[128,256]{1,0:T(8,128)(2,1)S(1)}, u32[]{:S(2)}, u32[]{:S(2)}) collective-permute-start(bf16[128,256]{1,0:T(8,128)(2,1)S(1)} %pad_maximum_fusion.1), channel_id=1, source_target_pairs={{0,1},{1,0},{2,3},{3,2},{4,5},{5,4},{6,7},{7,6},{8,9},{9,8},{10,11... | collective-permute-start | bytes 196616 | tf_op jit(solution)/shard_map/ppermute | solution.py:247
  4.1 3.8 %collective-permute-start.2 = (bf16[128,256]{1,0:T(8,128)(2,1)S(1)}, bf16[128,256]{1,0:T(8,128)(2,1)S(1)}, u32[]{:S(2)}, u32[]{:S(2)}) collective-permute-start(bf16[128,256]{1,0:T(8,128)(2,1)S(1)} %pad_maximum_fusion.3), channel_id=1, source_target_pairs={{0,3},{1,2},{2,1},{3,0},{4,7},{5,6},{6,5},{7,4},{8,11},{9,10},{10,... | collective-permute-start | bytes 196616 | tf_op jit(solution)/shard_map/ppermute | solution.py:247
  7.9 8.7 %collective-permute-start.12 = (bf16[256,256]{1,0:T(8,128)(2,1)S(1)}, bf16[256,256]{1,0:T(8,128)(2,1)S(1)}, u32[]{:S(2)}, u32[]{:S(2)}) collective-permute-start(bf16[256,256]{1,0:T(8,128)(2,1)S(1)} %constant_dynamic-update-slice_fusion.refs_1_), channel_id=1, source_target_pairs={{0,4},{1,5},{2,6},{3,7},{4,8},{5,9},{6,10},{7,11},{8,12},{9,13},{1... | collective-permute-start | bytes 393224 | tf_op jit(solution)/shard_map/ppermute | solution.py:267
  11.1 7.3 %collective-permute-start.9 = (bf16[256,256]{1,0:T(8,128)(2,1)S(1)}, bf16[256,256]{1,0:T(8,128)(2,1)S(1)}, u32[]{:S(2)}, u32[]{:S(2)}) collective-permute-start(bf16[256,256]{1,0:T(8,128)(2,1)S(1)} %pad_maximum_fusion.refs_0_), channel_id=1, source_target_pairs={{0,4},{1,5},{2,6},{3,7},{4,8},{5,9},{6,10},{7,11},{8,12},{9,13},{1... | collective-permute-start | bytes 393224 | tf_op jit(solution)/shard_map/ppermute | solution.py:267
  14.4 6.9 %collective-permute-start.5 = (bf16[128,640]{1,0:T(8,128)(2,1)S(1)}, bf16[128,640]{1,0:T(8,128)(2,1)S(1)}, u32[]{:S(2)}, u32[]{:S(2)}) collective-permute-start(bf16[128,640]{1,0:T(8,128)(2,1)S(1)} %get-tuple-element.41), channel_id=1, source_target_pairs={{0,3},{1,2},{2,1},{3,0},{4,7},{5,6},{6,5},{7,4},{8,11},{9,10},{10,... | collective-permute-start | bytes 491528 | tf_op jit(solution)/shard_map/ppermute | solution.py:247
  15.8 8.1 %collective-permute-start.3 = (bf16[128,640]{1,0:T(8,128)(2,1)S(1)}, bf16[128,640]{1,0:T(8,128)(2,1)S(1)}, u32[]{:S(2)}, u32[]{:S(2)}) collective-permute-start(bf16[128,640]{1,0:T(8,128)(2,1)S(1)} %get-tuple-element.42), channel_id=1, source_target_pairs={{0,1},{1,0},{2,3},{3,2},{4,5},{5,4},{6,7},{7,6},{8,9},{9,8},{10,11... | collective-permute-start | bytes 491528 | tf_op jit(solution)/shard_map/ppermute | solution.py:247
  15.8 8.8 %collective-permute-start.4 = (bf16[128,640]{1,0:T(8,128)(2,1)S(1)}, bf16[128,640]{1,0:T(8,128)(2,1)S(1)}, u32[]{:S(2)}, u32[]{:S(2)}) collective-permute-start(bf16[128,640]{1,0:T(8,128)(2,1)S(1)} %get-tuple-element.44), channel_id=1, source_target_pairs={{0,2},{1,3},{2,0},{3,1},{4,6},{5,7},{6,4},{7,5},{8,10},{9,11},{10,... | collective-permute-start | bytes 491528 | tf_op jit(solution)/shard_map/ppermute | solution.py:247
  16.5 12.2 %collective-permute-start.13 = (bf16[256,256]{1,0:T(8,128)(2,1)S(1)}, bf16[256,256]{1,0:T(8,128)(2,1)S(1)}, u32[]{:S(2)}, u32[]{:S(2)}) collective-permute-start(bf16[256,256]{1,0:T(8,128)(2,1)S(1)} %collective-permute-done.12.refs_1_), channel_id=1, source_target_pairs={{4,8},{5,9},{6,10},{7,11},{8,12},{9,13},{10,14},{11,15},{20,24},{2... | collective-permute-start | bytes 393224 | tf_op jit(solution)/shard_map/ppermute | solution.py:267
  18.3 11.0 %collective-permute-start.10 = (bf16[256,256]{1,0:T(8,128)(2,1)S(1)}, bf16[256,256]{1,0:T(8,128)(2,1)S(1)}, u32[]{:S(2)}, u32[]{:S(2)}) collective-permute-start(bf16[256,256]{1,0:T(8,128)(2,1)S(1)} %collective-permute-done.9.refs_0_), channel_id=1, source_target_pairs={{4,8},{5,9},{6,10},{7,11},{8,12},{9,13},{10,14},{11,15},{20,24},{2... | collective-permute-start | bytes 393224 | tf_op jit(solution)/shard_map/ppermute | solution.py:267
  21.3 12.8 %collective-permute-start.8 = (bf16[128,640]{1,0:T(8,128)(2,1)S(1)}, bf16[128,640]{1,0:T(8,128)(2,1)S(1)}, u32[]{:S(2)}, u32[]{:S(2)}) collective-permute-start(bf16[128,640]{1,0:T(8,128)(2,1)S(1)} %get-tuple-element.37), channel_id=1, source_target_pairs={{0,3},{1,2},{2,1},{3,0},{4,7},{5,6},{6,5},{7,4},{8,11},{9,10},{10,... | collective-permute-start | bytes 491528 | tf_op jit(solution)/shard_map/ppermute | solution.py:247
  23.9 10.2 %collective-permute-start.6 = (bf16[128,640]{1,0:T(8,128)(2,1)S(1)}, bf16[128,640]{1,0:T(8,128)(2,1)S(1)}, u32[]{:S(2)}, u32[]{:S(2)}) collective-permute-start(bf16[128,640]{1,0:T(8,128)(2,1)S(1)} %get-tuple-element.38), channel_id=1, source_target_pairs={{0,1},{1,0},{2,3},{3,2},{4,5},{5,4},{6,7},{7,6},{8,9},{9,8},{10,11... | collective-permute-start | bytes 491528 | tf_op jit(solution)/shard_map/ppermute | solution.py:247
  24.6 9.5 %collective-permute-start.7 = (bf16[128,640]{1,0:T(8,128)(2,1)S(1)}, bf16[128,640]{1,0:T(8,128)(2,1)S(1)}, u32[]{:S(2)}, u32[]{:S(2)}) collective-permute-start(bf16[128,640]{1,0:T(8,128)(2,1)S(1)} %get-tuple-element.40), channel_id=1, source_target_pairs={{0,2},{1,3},{2,0},{3,1},{4,6},{5,7},{6,4},{7,5},{8,10},{9,11},{10,... | collective-permute-start | bytes 491528 | tf_op jit(solution)/shard_map/ppermute | solution.py:247
  28.7 5.4 %collective-permute-start.14 = (bf16[256,256]{1,0:T(8,128)(2,1)S(1)}, bf16[256,256]{1,0:T(8,128)(2,1)S(1)}, u32[]{:S(2)}, u32[]{:S(2)}) collective-permute-start(bf16[256,256]{1,0:T(8,128)(2,1)S(1)} %collective-permute-done.13.refs_1_), channel_id=1, source_target_pairs={{8,12},{9,13},{10,14},{11,15},{24,28},{25,29},{26,30},{27,31}} | collective-permute-start | bytes 393224 | tf_op jit(solution)/shard_map/ppermute | solution.py:267
  29.4 4.7 %collective-permute-start.11 = (bf16[256,256]{1,0:T(8,128)(2,1)S(1)}, bf16[256,256]{1,0:T(8,128)(2,1)S(1)}, u32[]{:S(2)}, u32[]{:S(2)}) collective-permute-start(bf16[256,256]{1,0:T(8,128)(2,1)S(1)} %collective-permute-done.10.refs_0_), channel_id=1, source_target_pairs={{8,12},{9,13},{10,14},{11,15},{24,28},{25,29},{26,30},{27,31}} | collective-permute-start | bytes 393224 | tf_op jit(solution)/shard_map/ppermute | solution.py:267
  35.9 1.4 %collective-permute-start.18 = (bf16[512,256]{1,0:T(8,128)(2,1)S(1)}, bf16[512,256]{1,0:T(8,128)(2,1)S(1)}, u32[]{:S(2)}, u32[]{:S(2)}) collective-permute-start(bf16[512,256]{1,0:T(8,128)(2,1)S(1)} %convert_element_type.21), channel_id=1, source_target_pairs={{12,8},{13,9},{14,10},{15,11},{28,24},{29,25},{30,26},{31,27}} | collective-permute-start | bytes 786440 | tf_op jit(solution)/shard_map/ppermute | solution.py:286
  37.4 19.4 %collective-permute-start.19 = (bf16[512,256]{1,0:T(8,128)(2,1)S(1)}, bf16[512,256]{1,0:T(8,128)(2,1)S(1)}, u32[]{:S(2)}, u32[]{:S(2)}) collective-permute-start(bf16[512,256]{1,0:T(8,128)(2,1)S(1)} %add_convert_fusion.2), channel_id=1, source_target_pairs={{8,4},{9,5},{10,6},{11,7},{12,8},{13,9},{14,10},{15,11},{24,20},{2... | collective-permute-start | bytes 786440 | tf_op jit(solution)/shard_map/ppermute | solution.py:286
  56.8 11.1 %collective-permute-start.20 = (bf16[512,256]{1,0:T(8,128)(2,1)S(1)}, bf16[512,256]{1,0:T(8,128)(2,1)S(1)}, u32[]{:S(2)}, u32[]{:S(2)}) collective-permute-start(bf16[512,256]{1,0:T(8,128)(2,1)S(1)} %add_convert_fusion.1), channel_id=1, source_target_pairs={{4,0},{5,1},{6,2},{7,3},{8,4},{9,5},{10,6},{11,7},{12,8},{13,9},{1... | collective-permute-start | bytes 786440 | tf_op jit(solution)/shard_map/ppermute | solution.py:286
  63.2 6.4 %collective-permute-start.15 = (bf16[128,640]{1,0:T(8,128)(2,1)S(1)}, bf16[128,640]{1,0:T(8,128)(2,1)S(1)}, u32[]{:S(2)}, u32[]{:S(2)}) collective-permute-start(bf16[128,640]{1,0:T(8,128)(2,1)S(1)} %get-tuple-element.30), channel_id=1, source_target_pairs={{0,1},{1,0},{2,3},{3,2},{4,5},{5,4},{6,7},{7,6},{8,9},{9,8},{10,11... | collective-permute-start | bytes 491528 | tf_op jit(solution)/shard_map/ppermute | solution.py:247
  66.2 5.8 %collective-permute-start.16 = (bf16[128,640]{1,0:T(8,128)(2,1)S(1)}, bf16[128,640]{1,0:T(8,128)(2,1)S(1)}, u32[]{:S(2)}, u32[]{:S(2)}) collective-permute-start(bf16[128,640]{1,0:T(8,128)(2,1)S(1)} %get-tuple-element.31), channel_id=1, source_target_pairs={{0,2},{1,3},{2,0},{3,1},{4,6},{5,7},{6,4},{7,5},{8,10},{9,11},{10,... | collective-permute-start | bytes 491528 | tf_op jit(solution)/shard_map/ppermute | solution.py:247
  67.2 9.3 %collective-permute-start.17 = (bf16[128,640]{1,0:T(8,128)(2,1)S(1)}, bf16[128,640]{1,0:T(8,128)(2,1)S(1)}, u32[]{:S(2)}, u32[]{:S(2)}) collective-permute-start(bf16[128,640]{1,0:T(8,128)(2,1)S(1)} %get-tuple-element.32), channel_id=1, source_target_pairs={{0,3},{1,2},{2,1},{3,0},{4,7},{5,6},{6,5},{7,4},{8,11},{9,10},{10,... | collective-permute-start | bytes 491528 | tf_op jit(solution)/shard_map/ppermute | solution.py:247
  68.0 9.5 %collective-permute-start.23 = (bf16[128,256]{1,0:T(8,128)(2,1)S(1)}, bf16[128,256]{1,0:T(8,128)(2,1)S(1)}, u32[]{:S(2)}, u32[]{:S(2)}) collective-permute-start(bf16[128,256]{1,0:T(8,128)(2,1)S(1)} %get-tuple-element.45), channel_id=1, source_target_pairs={{0,3},{1,2},{2,1},{3,0},{4,7},{5,6},{6,5},{7,4},{8,11},{9,10},{10,... | collective-permute-start | bytes 196616 | tf_op jit(solution)/shard_map/ppermute | solution.py:247
  69.1 9.3 %collective-permute-start.22 = (bf16[128,256]{1,0:T(8,128)(2,1)S(1)}, bf16[128,256]{1,0:T(8,128)(2,1)S(1)}, u32[]{:S(2)}, u32[]{:S(2)}) collective-permute-start(bf16[128,256]{1,0:T(8,128)(2,1)S(1)} %get-tuple-element.46), channel_id=1, source_target_pairs={{0,2},{1,3},{2,0},{3,1},{4,6},{5,7},{6,4},{7,5},{8,10},{9,11},{10,... | collective-permute-start | bytes 196616 | tf_op jit(solution)/shard_map/ppermute | solution.py:247
  69.6 8.7 %collective-permute-start.21 = (bf16[128,256]{1,0:T(8,128)(2,1)S(1)}, bf16[128,256]{1,0:T(8,128)(2,1)S(1)}, u32[]{:S(2)}, u32[]{:S(2)}) collective-permute-start(bf16[128,256]{1,0:T(8,128)(2,1)S(1)} %get-tuple-element.47), channel_id=1, source_target_pairs={{0,1},{1,0},{2,3},{3,2},{4,5},{5,4},{6,7},{7,6},{8,9},{9,8},{10,11... | collective-permute-start | bytes 196616 | tf_op jit(solution)/shard_map/ppermute | solution.py:247

commit v3 on v2

--- a/solution.py
+++ b/solution.py
@@ -61,23 +61,21 @@
         span = key_rows.shape[0]
         left = jnp.concatenate([value_rows.T, jnp.ones((EXTRA, span), jnp.bfloat16)], axis=0)
         mask = None if offset else causal_mask(info, tokens)
+        scores = []
         for h in range(QPG):
-            scores = scaled_scores(key_rows, stacked(q, h))
-            if offset == 0:
-                scores = jnp.where(mask, scores, -jnp.inf)
-            top = jnp.max(scores, axis=0, keepdims=True)
+            raw = scaled_scores(key_rows, stacked(q, h))
+            scores.append(raw if offset else jnp.where(mask, raw, -jnp.inf))
+        tops = [jnp.max(raw, axis=0, keepdims=True) for raw in scores]
+        for h in range(QPG):
+            top = tops[h]
             if offset:
                 old_top = old_stats[h, 0:1]
                 top = jnp.maximum(old_top, top)
-                shrink = jnp.exp2(old_top - top)
-            weights = jnp.exp2(scores - top)
-            total = jnp.sum(weights, axis=0, keepdims=True)
-            added = jnp.dot(left, weights.astype(jnp.bfloat16), preferred_element_type=jnp.float32)
+            weights = jnp.exp2(scores[h] - top).astype(jnp.bfloat16)
+            added = jnp.dot(left, weights, preferred_element_type=jnp.float32)
             if offset:
-                total = total + shrink * old_stats[h, 1:2]
-                added = added + shrink * old_sums[h]
+                added = added + jnp.exp2(old_top - top) * old_sums[h]
             stats[h, 0:1] = top
-            stats[h, 1:2] = total
             sums[h] = added
 
     if offset == 0:
@@ -94,8 +92,9 @@
         for h in range(QPG):
             grads = stacked(g, h).T.astype(jnp.float32)
             weighted = jnp.sum(sums[h, :DH] * grads, axis=0, keepdims=True)
-            finals[h, 0:1] = stats[h, 0:1] + jnp.log2(stats[h, 1:2])
-            finals[h, 1:2] = weighted / sums[h, DH : DH + 1]
+            total = sums[h, DH : DH + 1]
+            finals[h, 0:1] = stats[h, 0:1] + jnp.log2(total)
+            finals[h, 1:2] = weighted / total
 
 
 def backward_kernel(offset, first, info, *refs):
@@ -249,19 +248,21 @@
     def columns(array, head, width):
         return lax.dynamic_slice_in_dim(array, head * width, width, axis=1)
 
+    def after(array, *others):
+        return lax.optimization_barrier((array,) + others)[0]
+
     kv_pieces = []
     for d in range(KVH):
         head = rank ^ d
         piece = jnp.concatenate([columns(keys, head, DH), columns(values, head, DH)], axis=1)
         kv_pieces.append(swap(piece, d))
-    q = [swap(columns(queries, rank ^ d, QPG * DH), d) for d in range(KVH)]
-    g = [swap(columns(out_grad, rank ^ d, QPG * DH), d) for d in range(KVH)]
-    chain = [
-        (
-            jnp.concatenate(kv_pieces[:2], axis=0),
-            jnp.concatenate(kv_pieces[2:], axis=0),
-        )
-    ]
+    q_slices = [columns(queries, rank ^ d, QPG * DH) for d in range(KVH)]
+    g_slices = [columns(out_grad, rank ^ d, QPG * DH) for d in range(KVH)]
+    q = [swap(q_slices[d], d) for d in range(KVH)]
+    g = [swap(g_slices[d], d) for d in range(KVH)]
+    near = jnp.concatenate(kv_pieces[:2], axis=0)
+    far = jnp.concatenate([after(kv_pieces[2], near, *q_slices), kv_pieces[3]], axis=0)
+    chain = [(near, far)]
     for step in range(1, planes):
         pairs = [(i, i + KVH) for i in range((step - 1) * KVH, devices - KVH)]
         chain.append(tuple(lax.ppermute(half, "seq", pairs) for half in chain[-1]))

time: 80.9 us -> 77.1 us (0.953)
  Pallas kernels: 19.2 us -> 17.7 us
  waiting for transfers between devices: 26.7 us -> 25.5 us
  starting transfers between devices: 31.5 us -> 30.4 us
    ppermute x15, waiting for transfers between devices: 12.4 us -> 9.95 us  [swap(): return lax.ppermute(array, 'seq', [(i, i ^ d) for i in range(devices)])]
    pallas_call x9, Pallas kernels: 19.2 us -> 17.7 us  [local_call(): pl.pallas_call(kernel, in_specs=[pl.BlockSpec(memory_space=pltpu.SMEM)] +...]
    ppermute x3, waiting for transfers between devices: 14.3 us -> 15.5 us  [per_device(): arrived = lax.ppermute(total, 'seq', pairs)]
  transfers between devices with their start and end apart: 24 -> 24, of which waited for: 8 -> 7; matrix products, arithmetic and copies ran while one was open for 0% -> 0% of each run, Pallas kernels for 20% -> 19%
where the time goes in v3:
time: 77.1 us; the launch traced here: 76 us
  starting transfers between devices  30.4 us (39%)
  waiting for transfers between devices  25.5 us (33%)
  Pallas kernels  17.7 us (23%)
  local copies, waits for them, and re-layouts  1.15 us (1%)
  between operations  1.01 us (1%)
    pallas_call x9, Pallas kernels, local_call(): pl.pallas_call(kernel, in_specs=[pl.BlockSpec(memory_space=pltpu.SMEM)] +...  17.7 us
    ppermute x3, waiting for transfers between devices, per_device(): arrived = lax.ppermute(total, 'seq', pairs)  15.5 us
    ppermute x15, starting transfers between devices, swap(): return lax.ppermute(array, 'seq', [(i, i ^ d) for i in range(devices)])  14.4 us
    ppermute x6, starting transfers between devices, per_device(): lax.ppermute(half, 'seq', pairs)  12.1 us
    ppermute x15, waiting for transfers between devices, swap(): return lax.ppermute(array, 'seq', [(i, i ^ d) for i in range(devices)])  9.95 us
    ppermute x3, starting transfers between devices, per_device(): arrived = lax.ppermute(total, 'seq', pairs)  3.89 us
  transfers between devices with their start and end apart: 24, of which 7 were waited for; matrix products, arithmetic and copies ran while one was open for 0% of the time, Pallas kernels for 19%

profile of v3, /device:TPU:9, one launch (start us, length us, event | category | flops | bytes accessed | tf_op | source)
XLA Modules:
  0.0 76.0 jit_solution(12407508206655947579)
XLA Ops:
  0.7 1.0 %constant_dynamic-slice_fusion.4 = (bf16[128,128]{1,0:T(8,128)(2,1)S(1)}, bf16[128,128]{1,0:T(8,128)(2,1)S(1)}, bf16[128,128]{1,0:T(8,128)(2,1)S(1)}, bf16[128,1...) fusion(bf16[128,512]{1,0:T(8,128)(2,1)} %param.6, ...), kind=kLoop, calls=%fused_computation.13 | loop fusion | bytes 524304 | tf_op jit(solution)/shard_map/dynamic_slice | solution.py:249
  1.7 1.3 %collective-permute-start.1 = (bf16[128,256]{1,0:T(8,128)(2,1)S(1)}, bf16[128,256]{1,0:T(8,128)(2,1)S(1)}, u32[]{:S(2)}, u32[]{:S(2)}) collective-permute-start(bf16[128,256]{1,0:T(8,128)(2,1)S(1)} %pad_maximum_fusion.2), channel_id=1, source_target_pairs={{0,2},{1,3},{2,0},{3,1},{4,6},{5,7},{6,4},{7,5},{8,10},{9,11},{10,... | collective-permute-start | bytes 196616 | tf_op jit(solution)/shard_map/ppermute | solution.py:246
  3.0 1.0 %collective-permute-start = (bf16[128,256]{1,0:T(8,128)(2,1)S(1)}, bf16[128,256]{1,0:T(8,128)(2,1)S(1)}, u32[]{:S(2)}, u32[]{:S(2)}) collective-permute-start(bf16[128,256]{1,0:T(8,128)(2,1)S(1)} %pad_maximum_fusion.1), channel_id=1, source_target_pairs={{0,1},{1,0},{2,3},{3,2},{4,5},{5,4},{6,7},{7,6},{8,9},{9,8},{10,11... | collective-permute-start | bytes 196616 | tf_op jit(solution)/shard_map/ppermute | solution.py:246
  4.1 0.2 collective-permute-start.2
  4.3 0.1 constant_dynamic-slice_fusion.6
  4.3 0.6 collective-permute-done
  5.0 3.2 %collective-permute-start.9 = (bf16[256,256]{1,0:T(8,128)(2,1)S(1)}, bf16[256,256]{1,0:T(8,128)(2,1)S(1)}, u32[]{:S(2)}, u32[]{:S(2)}) collective-permute-start(bf16[256,256]{1,0:T(8,128)(2,1)S(1)} %pad_maximum_fusion.refs_0_), channel_id=1, source_target_pairs={{0,4},{1,5},{2,6},{3,7},{4,8},{5,9},{6,10},{7,11},{8,12},{9,13},{1... | collective-permute-start | bytes 393224 | tf_op jit(solution)/shard_map/ppermute | solution.py:268
  8.2 0.0 collective-permute-done.1
  8.2 0.0 collective-permute-done.2
  8.2 3.2 %collective-permute-start.12 = (bf16[256,256]{1,0:T(8,128)(2,1)S(1)}, bf16[256,256]{1,0:T(8,128)(2,1)S(1)}, u32[]{:S(2)}, u32[]{:S(2)}) collective-permute-start(bf16[256,256]{1,0:T(8,128)(2,1)S(1)} %constant_dynamic-update-slice_fusion.refs_1_), channel_id=1, source_target_pairs={{0,4},{1,5},{2,6},{3,7},{4,8},{5,9},{6,10},{7,11},{8,12},{9,13},{1... | collective-permute-start | bytes 393224 | tf_op jit(solution)/shard_map/ppermute | solution.py:268
  11.4 1.6 %collective-permute-start.5 = (bf16[128,640]{1,0:T(8,128)(2,1)S(1)}, bf16[128,640]{1,0:T(8,128)(2,1)S(1)}, u32[]{:S(2)}, u32[]{:S(2)}) collective-permute-start(bf16[128,640]{1,0:T(8,128)(2,1)S(1)} %get-tuple-element.43), channel_id=1, source_target_pairs={{0,3},{1,2},{2,1},{3,0},{4,7},{5,6},{6,5},{7,4},{8,11},{9,10},{10,... | collective-permute-start | bytes 491528 | tf_op jit(solution)/shard_map/ppermute | solution.py:246
  13.1 0.0 collective-permute-start.3
  13.1 0.7 collective-permute-start.4
  13.8 0.1 constant_dynamic-slice_fusion
  13.8 0.0 collective-permute-done.9.refs_0_
  13.9 2.4 %collective-permute-start.10 = (bf16[256,256]{1,0:T(8,128)(2,1)S(1)}, bf16[256,256]{1,0:T(8,128)(2,1)S(1)}, u32[]{:S(2)}, u32[]{:S(2)}) collective-permute-start(bf16[256,256]{1,0:T(8,128)(2,1)S(1)} %collective-permute-done.9.refs_0_), channel_id=1, source_target_pairs={{4,8},{5,9},{6,10},{7,11},{8,12},{9,13},{10,14},{11,15},{20,24},{2... | collective-permute-start | bytes 393224 | tf_op jit(solution)/shard_map/ppermute | solution.py:268
  16.3 0.0 collective-permute-done.12.refs_1_
  16.3 1.9 %collective-permute-start.13 = (bf16[256,256]{1,0:T(8,128)(2,1)S(1)}, bf16[256,256]{1,0:T(8,128)(2,1)S(1)}, u32[]{:S(2)}, u32[]{:S(2)}) collective-permute-start(bf16[256,256]{1,0:T(8,128)(2,1)S(1)} %collective-permute-done.12.refs_1_), channel_id=1, source_target_pairs={{4,8},{5,9},{6,10},{7,11},{8,12},{9,13},{10,14},{11,15},{20,24},{2... | collective-permute-start | bytes 393224 | tf_op jit(solution)/shard_map/ppermute | solution.py:268
  18.2 0.1 pad_add_fusion.info
  18.3 0.0 collective-permute-done.5.refs_5_
  18.3 2.1 %collective-permute-start.8 = (bf16[128,640]{1,0:T(8,128)(2,1)S(1)}, bf16[128,640]{1,0:T(8,128)(2,1)S(1)}, u32[]{:S(2)}, u32[]{:S(2)}) collective-permute-start(bf16[128,640]{1,0:T(8,128)(2,1)S(1)} %get-tuple-element.39), channel_id=1, source_target_pairs={{0,3},{1,2},{2,1},{3,0},{4,7},{5,6},{6,5},{7,4},{8,11},{9,10},{10,... | collective-permute-start | bytes 491528 | tf_op jit(solution)/shard_map/ppermute | solution.py:246
  20.4 0.0 collective-permute-done.3.refs_3_
  20.4 0.0 collective-permute-start.6
  20.4 1.2 %collective-permute-done.4.refs_4_ = bf16[128,640]{1,0:T(8,128)(2,1)S(1)} collective-permute-done((bf16[128,640]{1,0:T(8,128)(2,1)S(1)}, bf16[128,640]{1,0:T(8,128)(2,1)S(1)}, u32[]{:S(2)}, u32[]{:S(2)}) %collective-permute-start.4) | collective-permute-done | bytes 163872 | tf_op jit(solution)/shard_map/ppermute | solution.py:246
  21.6 0.6 collective-permute-start.7
  22.2 2.5 %shard_map.67 = (f32[5,8,512]{2,1,0:T(8,128)S(1)}, f32[5,136,512]{2,1,0:T(8,128)S(1)}) custom-call(s32[2]{0:T(128)S(1)} %pad_add_fusion.info, bf16[256,256]{1,0:T(8,128)(2,1)S(1)} %pad_maximum_fusion.refs_0_, bf16[256,256]{1,0:T(8,128)(2,1)S(1)} %constant_dynamic-update-slice_fusion.refs_1_, bf16[128,640]{1,0:T(8,128)(2,1)S(1)} %get-tuple-element.45.refs_2_, ...), custom_call_target="tpu_custom_call" | custom-call | flops 1342177280 | bytes 1048576 | tf_op jit(solution)/shard_map/pallas_call | solution.py:159
  24.7 0.0 collective-permute-done.10.refs_0_
  24.7 0.7 collective-permute-start.11
  25.4 0.0 collective-permute-done.13.refs_1_
  25.4 0.7 collective-permute-start.14
  26.0 2.5 %shard_map.68 = (f32[5,8,512]{2,1,0:T(8,128)S(1)}, f32[5,136,512]{2,1,0:T(8,128)S(1)}) custom-call(s32[2]{0:T(128)S(1)} %pad_add_fusion.info, bf16[256,256]{1,0:T(8,128)(2,1)S(1)} %collective-permute-done.9.refs_0_, bf16[256,256]{1,0:T(8,128)(2,1)S(1)} %collective-permute-done.12.refs_1_, bf16[128,640]{1,0:T(8,128)(2,1)S(1)} %get-tuple-element.45.refs_2_, ...), custom_call_target="tpu_custom_call" | custom-call | flops 1342177280 | bytes 1048576 | tf_op jit(solution)/shard_map/pallas_call | solution.py:159
  28.5 0.7 shard_map.69
  29.2 0.0 collective-permute-done.8.refs_9_
  29.2 0.0 collective-permute-done.6.refs_7_
  29.2 0.0 collective-permute-done.7.refs_8_
  29.2 0.0 collective-permute-done.11.refs_0_
  29.2 0.0 collective-permute-done.14.refs_1_
  29.2 0.9 %shard_map.70.refs_10_ = f32[5,8,512]{2,1,0:T(8,128)S(1)} custom-call(s32[2]{0:T(128)S(1)} %pad_add_fusion.info, bf16[256,256]{1,0:T(8,128)(2,1)S(1)} %collective-permute-done.11.refs_0_, bf16[256,256]{1,0:T(8,128)(2,1)S(1)} %collective-permute-done.14.refs_1_, bf16[128,640]{1,0:T(8,128)(2,1)S(1)} %get-tuple-element.45.refs_2_, ...), custom_call_target="tpu_custom_call" | custom-call | flops 1342177280 | bytes 1048576 | tf_op jit(solution)/shard_map/pallas_call | solution.py:159
  30.1 0.9 %shard_map.71 = (f32[512,256]{1,0:T(8,128)S(1)}, f32[5,128,512]{2,1,0:T(8,128)S(1)}) custom-call(s32[2]{0:T(128)S(1)} %pad_add_fusion.info, bf16[256,256]{1,0:T(8,128)(2,1)S(1)} %collective-permute-done.11.refs_0_, bf16[256,256]{1,0:T(8,128)(2,1)S(1)} %collective-permute-done.14.refs_1_, bf16[128,640]{1,0:T(8,128)(2,1)S(1)} %get-tuple-element.45.refs_2_, ...), custom_call_target="tpu_custom_call" | custom-call | flops 3355443200 | bytes 1048576 | tf_op jit(solution)/shard_map/pallas_call | solution.py:159
  31.0 0.7 collective-permute-start.18
  31.7 0.7 shard_map.72
  32.4 0.0 collective-permute-done.18
  32.4 0.1 add_convert_fusion.2
  32.5 1.3 %collective-permute-start.19 = (bf16[512,256]{1,0:T(8,128)(2,1)S(1)}, bf16[512,256]{1,0:T(8,128)(2,1)S(1)}, u32[]{:S(2)}, u32[]{:S(2)}) collective-permute-start(bf16[512,256]{1,0:T(8,128)(2,1)S(1)} %add_convert_fusion.2), channel_id=1, source_target_pairs={{8,4},{9,5},{10,6},{11,7},{12,8},{13,9},{14,10},{15,11},{24,20},{2... | collective-permute-start | bytes 786440 | tf_op jit(solution)/shard_map/ppermute | solution.py:287
  33.8 3.8 %shard_map.73 = (f32[512,256]{1,0:T(8,128)S(1)}, f32[5,128,512]{2,1,0:T(8,128)S(1)}) custom-call(s32[2]{0:T(128)S(1)} %pad_add_fusion.info, bf16[256,256]{1,0:T(8,128)(2,1)S(1)} %collective-permute-done.9.refs_0_, bf16[256,256]{1,0:T(8,128)(2,1)S(1)} %collective-permute-done.12.refs_1_, bf16[128,640]{1,0:T(8,128)(2,1)S(1)} %get-tuple-element.45.refs_2_, ...), custom_call_target="tpu_custom_call" | custom-call | flops 3355443200 | bytes 1048576 | tf_op jit(solution)/shard_map/pallas_call | solution.py:159
  37.6 15.5 %collective-permute-done.19 = bf16[512,256]{1,0:T(8,128)(2,1)S(1)} collective-permute-done((bf16[512,256]{1,0:T(8,128)(2,1)S(1)}, bf16[512,256]{1,0:T(8,128)(2,1)S(1)}, u32[]{:S(2)}, u32[]{:S(2)}) %collective-permute-start.19) | collective-permute-done | bytes 262176 | tf_op jit(solution)/shard_map/ppermute | solution.py:287
  53.1 0.1 add_convert_fusion.1
  53.2 1.9 %collective-permute-start.20 = (bf16[512,256]{1,0:T(8,128)(2,1)S(1)}, bf16[512,256]{1,0:T(8,128)(2,1)S(1)}, u32[]{:S(2)}, u32[]{:S(2)}) collective-permute-start(bf16[512,256]{1,0:T(8,128)(2,1)S(1)} %add_convert_fusion.1), channel_id=1, source_target_pairs={{4,0},{5,1},{6,2},{7,3},{8,4},{9,5},{10,6},{11,7},{12,8},{13,9},{1... | collective-permute-start | bytes 786440 | tf_op jit(solution)/shard_map/ppermute | solution.py:287
  55.1 4.3 %shard_map.74 = (f32[512,256]{1,0:T(8,128)S(1)}, bf16[128,640]{1,0:T(8,128)(2,1)S(1)}, bf16[128,640]{1,0:T(8,128)(2,1)S(1)}, bf16[128,640]{1,0:T(8,128)(2,1)S(1)}, bf16[128,640]{1,0:T(8,128)(2,1)S(1)}) custom-call(s32[2]{0:T(128)S(1)} %pad_add_fusion.info, bf16[256,256]{1,0:T(8,128)(2,1)S(1)} %pad_maximum_fusion.refs_0_, ...), custom_call_target="tpu_custom_call" | custom-call | flops 3355443200 | bytes 1048576 | tf_op jit(solution)/shard_map/pallas_call | solution.py:159
  59.4 3.0 %collective-permute-start.15 = (bf16[128,640]{1,0:T(8,128)(2,1)S(1)}, bf16[128,640]{1,0:T(8,128)(2,1)S(1)}, u32[]{:S(2)}, u32[]{:S(2)}) collective-permute-start(bf16[128,640]{1,0:T(8,128)(2,1)S(1)} %get-tuple-element.32), channel_id=1, source_target_pairs={{0,1},{1,0},{2,3},{3,2},{4,5},{5,4},{6,7},{7,6},{8,9},{9,8},{10,11... | collective-permute-start | bytes 491528 | tf_op jit(solution)/shard_map/ppermute | solution.py:246
  62.4 0.7 collective-permute-start.16
  63.0 1.1 %collective-permute-start.17 = (bf16[128,640]{1,0:T(8,128)(2,1)S(1)}, bf16[128,640]{1,0:T(8,128)(2,1)S(1)}, u32[]{:S(2)}, u32[]{:S(2)}) collective-permute-start(bf16[128,640]{1,0:T(8,128)(2,1)S(1)} %get-tuple-element.34), channel_id=1, source_target_pairs={{0,3},{1,2},{2,1},{3,0},{4,7},{5,6},{6,5},{7,4},{8,11},{9,10},{10,... | collective-permute-start | bytes 491528 | tf_op jit(solution)/shard_map/ppermute | solution.py:246
  64.1 0.0 collective-permute-done.20
  64.1 0.1 add_convert_fusion
  64.2 0.8 %collective-permute-start.23 = (bf16[128,256]{1,0:T(8,128)(2,1)S(1)}, bf16[128,256]{1,0:T(8,128)(2,1)S(1)}, u32[]{:S(2)}, u32[]{:S(2)}) collective-permute-start(bf16[128,256]{1,0:T(8,128)(2,1)S(1)} %get-tuple-element.47), channel_id=1, source_target_pairs={{0,3},{1,2},{2,1},{3,0},{4,7},{5,6},{6,5},{7,4},{8,11},{9,10},{10,... | collective-permute-start | bytes 196616 | tf_op jit(solution)/shard_map/ppermute | solution.py:246
  65.0 0.8 %collective-permute-start.22 = (bf16[128,256]{1,0:T(8,128)(2,1)S(1)}, bf16[128,256]{1,0:T(8,128)(2,1)S(1)}, u32[]{:S(2)}, u32[]{:S(2)}) collective-permute-start(bf16[128,256]{1,0:T(8,128)(2,1)S(1)} %get-tuple-element.48), channel_id=1, source_target_pairs={{0,2},{1,3},{2,0},{3,1},{4,6},{5,7},{6,4},{7,5},{8,10},{9,11},{10,... | collective-permute-start | bytes 196616 | tf_op jit(solution)/shard_map/ppermute | solution.py:246
  65.8 0.0 collective-permute-done.15.refs_1_
  65.8 0.5 collective-permute-start.21
  66.4 1.8 %collective-permute-done.16.refs_2_ = bf16[128,640]{1,0:T(8,128)(2,1)S(1)} collective-permute-done((bf16[128,640]{1,0:T(8,128)(2,1)S(1)}, bf16[128,640]{1,0:T(8,128)(2,1)S(1)}, u32[]{:S(2)}, u32[]{:S(2)}) %collective-permute-start.16) | collective-permute-done | bytes 163872 | tf_op jit(solution)/shard_map/ppermute | solution.py:246
  68.1 4.4 %collective-permute-done.17.refs_3_ = bf16[128,640]{1,0:T(8,128)(2,1)S(1)} collective-permute-done((bf16[128,640]{1,0:T(8,128)(2,1)S(1)}, bf16[128,640]{1,0:T(8,128)(2,1)S(1)}, u32[]{:S(2)}, u32[]{:S(2)}) %collective-permute-start.17) | collective-permute-done | bytes 163872 | tf_op jit(solution)/shard_map/ppermute | solution.py:246
  72.6 1.1 %collective-permute-done.23.refs_7_ = bf16[128,256]{1,0:T(8,128)(2,1)S(1)} collective-permute-done((bf16[128,256]{1,0:T(8,128)(2,1)S(1)}, bf16[128,256]{1,0:T(8,128)(2,1)S(1)}, u32[]{:S(2)}, u32[]{:S(2)}) %collective-permute-start.23) | collective-permute-done | bytes 65568 | tf_op jit(solution)/shard_map/ppermute | solution.py:246
  73.7 0.8 %collective-permute-done.22.refs_6_ = bf16[128,256]{1,0:T(8,128)(2,1)S(1)} collective-permute-done((bf16[128,256]{1,0:T(8,128)(2,1)S(1)}, bf16[128,256]{1,0:T(8,128)(2,1)S(1)}, u32[]{:S(2)}, u32[]{:S(2)}) %collective-permute-start.22) | collective-permute-done | bytes 65568 | tf_op jit(solution)/shard_map/ppermute | solution.py:246
  74.5 0.0 collective-permute-done.21.refs_5_
  74.5 1.6 %shard_map.75 = (bf16[128,2560]{1,0:T(8,128)(2,1)}, bf16[128,512]{1,0:T(8,128)(2,1)}, bf16[128,512]{1,0:T(8,128)(2,1)}) custom-call(s32[2]{0:T(128)S(1)} %pad_add_fusion.info, bf16[128,640]{1,0:T(8,128)(2,1)S(1)} %get-tuple-element.31.refs_0_, bf16[128,640]{1,0:T(8,128)(2,1)S(1)} %collective-permute-done.15.refs_1_, ...), custom_call_target="tpu_custom_call" | custom-call | bytes 1048576 | tf_op jit(solution)/shard_map/pallas_call | solution.py:159
  (12 shorter events, 0.1 us)
Async XLA Ops:
  0.6 3.6 %copy-start = (bf16[128,2560]{1,0:T(8,128)(2,1)S(1)}, bf16[128,2560]{1,0:T(8,128)(2,1)}, u32[]{:S(2)}) copy-start(bf16[128,2560]{1,0:T(8,128)(2,1)} %param.4) | copy-start | bytes 1966084
  0.7 13.1 %copy-start.1 = (bf16[128,2560]{1,0:T(8,128)(2,1)S(1)}, bf16[128,2560]{1,0:T(8,128)(2,1)}, u32[]{:S(2)}) copy-start(bf16[128,2560]{1,0:T(8,128)(2,1)} %param.7) | copy-start | bytes 1966084
  1.7 6.5 %collective-permute-start.1 = (bf16[128,256]{1,0:T(8,128)(2,1)S(1)}, bf16[128,256]{1,0:T(8,128)(2,1)S(1)}, u32[]{:S(2)}, u32[]{:S(2)}) collective-permute-start(bf16[128,256]{1,0:T(8,128)(2,1)S(1)} %pad_maximum_fusion.2), channel_id=1, source_target_pairs={{0,2},{1,3},{2,0},{3,1},{4,6},{5,7},{6,4},{7,5},{8,10},{9,11},{10,... | collective-permute-start | bytes 196616 | tf_op jit(solution)/shard_map/ppermute | solution.py:246
  3.0 1.9 %collective-permute-start = (bf16[128,256]{1,0:T(8,128)(2,1)S(1)}, bf16[128,256]{1,0:T(8,128)(2,1)S(1)}, u32[]{:S(2)}, u32[]{:S(2)}) collective-permute-start(bf16[128,256]{1,0:T(8,128)(2,1)S(1)} %pad_maximum_fusion.1), channel_id=1, source_target_pairs={{0,1},{1,0},{2,3},{3,2},{4,5},{5,4},{6,7},{7,6},{8,9},{9,8},{10,11... | collective-permute-start | bytes 196616 | tf_op jit(solution)/shard_map/ppermute | solution.py:246
  4.1 4.1 %collective-permute-start.2 = (bf16[128,256]{1,0:T(8,128)(2,1)S(1)}, bf16[128,256]{1,0:T(8,128)(2,1)S(1)}, u32[]{:S(2)}, u32[]{:S(2)}) collective-permute-start(bf16[128,256]{1,0:T(8,128)(2,1)S(1)} %pad_maximum_fusion.3), channel_id=1, source_target_pairs={{0,3},{1,2},{2,1},{3,0},{4,7},{5,6},{6,5},{7,4},{8,11},{9,10},{10,... | collective-permute-start | bytes 196616 | tf_op jit(solution)/shard_map/ppermute | solution.py:246
  5.0 8.9 %collective-permute-start.9 = (bf16[256,256]{1,0:T(8,128)(2,1)S(1)}, bf16[256,256]{1,0:T(8,128)(2,1)S(1)}, u32[]{:S(2)}, u32[]{:S(2)}) collective-permute-start(bf16[256,256]{1,0:T(8,128)(2,1)S(1)} %pad_maximum_fusion.refs_0_), channel_id=1, source_target_pairs={{0,4},{1,5},{2,6},{3,7},{4,8},{5,9},{6,10},{7,11},{8,12},{9,13},{1... | collective-permute-start | bytes 393224 | tf_op jit(solution)/shard_map/ppermute | solution.py:268
  8.2 8.1 %collective-permute-start.12 = (bf16[256,256]{1,0:T(8,128)(2,1)S(1)}, bf16[256,256]{1,0:T(8,128)(2,1)S(1)}, u32[]{:S(2)}, u32[]{:S(2)}) collective-permute-start(bf16[256,256]{1,0:T(8,128)(2,1)S(1)} %constant_dynamic-update-slice_fusion.refs_1_), channel_id=1, source_target_pairs={{0,4},{1,5},{2,6},{3,7},{4,8},{5,9},{6,10},{7,11},{8,12},{9,13},{1... | collective-permute-start | bytes 393224 | tf_op jit(solution)/shard_map/ppermute | solution.py:268
  11.4 6.9 %collective-permute-start.5 = (bf16[128,640]{1,0:T(8,128)(2,1)S(1)}, bf16[128,640]{1,0:T(8,128)(2,1)S(1)}, u32[]{:S(2)}, u32[]{:S(2)}) collective-permute-start(bf16[128,640]{1,0:T(8,128)(2,1)S(1)} %get-tuple-element.43), channel_id=1, source_target_pairs={{0,3},{1,2},{2,1},{3,0},{4,7},{5,6},{6,5},{7,4},{8,11},{9,10},{10,... | collective-permute-start | bytes 491528 | tf_op jit(solution)/shard_map/ppermute | solution.py:246
  13.1 7.3 %collective-permute-start.3 = (bf16[128,640]{1,0:T(8,128)(2,1)S(1)}, bf16[128,640]{1,0:T(8,128)(2,1)S(1)}, u32[]{:S(2)}, u32[]{:S(2)}) collective-permute-start(bf16[128,640]{1,0:T(8,128)(2,1)S(1)} %get-tuple-element.44), channel_id=1, source_target_pairs={{0,1},{1,0},{2,3},{3,2},{4,5},{5,4},{6,7},{7,6},{8,9},{9,8},{10,11... | collective-permute-start | bytes 491528 | tf_op jit(solution)/shard_map/ppermute | solution.py:246
  13.1 8.5 %collective-permute-start.4 = (bf16[128,640]{1,0:T(8,128)(2,1)S(1)}, bf16[128,640]{1,0:T(8,128)(2,1)S(1)}, u32[]{:S(2)}, u32[]{:S(2)}) collective-permute-start(bf16[128,640]{1,0:T(8,128)(2,1)S(1)} %get-tuple-element.46), channel_id=1, source_target_pairs={{0,2},{1,3},{2,0},{3,1},{4,6},{5,7},{6,4},{7,5},{8,10},{9,11},{10,... | collective-permute-start | bytes 491528 | tf_op jit(solution)/shard_map/ppermute | solution.py:246
  13.9 10.8 %collective-permute-start.10 = (bf16[256,256]{1,0:T(8,128)(2,1)S(1)}, bf16[256,256]{1,0:T(8,128)(2,1)S(1)}, u32[]{:S(2)}, u32[]{:S(2)}) collective-permute-start(bf16[256,256]{1,0:T(8,128)(2,1)S(1)} %collective-permute-done.9.refs_0_), channel_id=1, source_target_pairs={{4,8},{5,9},{6,10},{7,11},{8,12},{9,13},{10,14},{11,15},{20,24},{2... | collective-permute-start | bytes 393224 | tf_op jit(solution)/shard_map/ppermute | solution.py:268
  16.3 9.1 %collective-permute-start.13 = (bf16[256,256]{1,0:T(8,128)(2,1)S(1)}, bf16[256,256]{1,0:T(8,128)(2,1)S(1)}, u32[]{:S(2)}, u32[]{:S(2)}) collective-permute-start(bf16[256,256]{1,0:T(8,128)(2,1)S(1)} %collective-permute-done.12.refs_1_), channel_id=1, source_target_pairs={{4,8},{5,9},{6,10},{7,11},{8,12},{9,13},{10,14},{11,15},{20,24},{2... | collective-permute-start | bytes 393224 | tf_op jit(solution)/shard_map/ppermute | solution.py:268
  18.3 10.9 %collective-permute-start.8 = (bf16[128,640]{1,0:T(8,128)(2,1)S(1)}, bf16[128,640]{1,0:T(8,128)(2,1)S(1)}, u32[]{:S(2)}, u32[]{:S(2)}) collective-permute-start(bf16[128,640]{1,0:T(8,128)(2,1)S(1)} %get-tuple-element.39), channel_id=1, source_target_pairs={{0,3},{1,2},{2,1},{3,0},{4,7},{5,6},{6,5},{7,4},{8,11},{9,10},{10,... | collective-permute-start | bytes 491528 | tf_op jit(solution)/shard_map/ppermute | solution.py:246
  20.4 8.8 %collective-permute-start.6 = (bf16[128,640]{1,0:T(8,128)(2,1)S(1)}, bf16[128,640]{1,0:T(8,128)(2,1)S(1)}, u32[]{:S(2)}, u32[]{:S(2)}) collective-permute-start(bf16[128,640]{1,0:T(8,128)(2,1)S(1)} %get-tuple-element.40), channel_id=1, source_target_pairs={{0,1},{1,0},{2,3},{3,2},{4,5},{5,4},{6,7},{7,6},{8,9},{9,8},{10,11... | collective-permute-start | bytes 491528 | tf_op jit(solution)/shard_map/ppermute | solution.py:246
  21.6 7.6 %collective-permute-start.7 = (bf16[128,640]{1,0:T(8,128)(2,1)S(1)}, bf16[128,640]{1,0:T(8,128)(2,1)S(1)}, u32[]{:S(2)}, u32[]{:S(2)}) collective-permute-start(bf16[128,640]{1,0:T(8,128)(2,1)S(1)} %get-tuple-element.42), channel_id=1, source_target_pairs={{0,2},{1,3},{2,0},{3,1},{4,6},{5,7},{6,4},{7,5},{8,10},{9,11},{10,... | collective-permute-start | bytes 491528 | tf_op jit(solution)/shard_map/ppermute | solution.py:246
  24.7 4.5 %collective-permute-start.11 = (bf16[256,256]{1,0:T(8,128)(2,1)S(1)}, bf16[256,256]{1,0:T(8,128)(2,1)S(1)}, u32[]{:S(2)}, u32[]{:S(2)}) collective-permute-start(bf16[256,256]{1,0:T(8,128)(2,1)S(1)} %collective-permute-done.10.refs_0_), channel_id=1, source_target_pairs={{8,12},{9,13},{10,14},{11,15},{24,28},{25,29},{26,30},{27,31}} | collective-permute-start | bytes 393224 | tf_op jit(solution)/shard_map/ppermute | solution.py:268
  25.4 3.9 %collective-permute-start.14 = (bf16[256,256]{1,0:T(8,128)(2,1)S(1)}, bf16[256,256]{1,0:T(8,128)(2,1)S(1)}, u32[]{:S(2)}, u32[]{:S(2)}) collective-permute-start(bf16[256,256]{1,0:T(8,128)(2,1)S(1)} %collective-permute-done.13.refs_1_), channel_id=1, source_target_pairs={{8,12},{9,13},{10,14},{11,15},{24,28},{25,29},{26,30},{27,31}} | collective-permute-start | bytes 393224 | tf_op jit(solution)/shard_map/ppermute | solution.py:268
  31.0 1.4 %collective-permute-start.18 = (bf16[512,256]{1,0:T(8,128)(2,1)S(1)}, bf16[512,256]{1,0:T(8,128)(2,1)S(1)}, u32[]{:S(2)}, u32[]{:S(2)}) collective-permute-start(bf16[512,256]{1,0:T(8,128)(2,1)S(1)} %convert_element_type.21), channel_id=1, source_target_pairs={{12,8},{13,9},{14,10},{15,11},{28,24},{29,25},{30,26},{31,27}} | collective-permute-start | bytes 786440 | tf_op jit(solution)/shard_map/ppermute | solution.py:287
  32.5 20.6 %collective-permute-start.19 = (bf16[512,256]{1,0:T(8,128)(2,1)S(1)}, bf16[512,256]{1,0:T(8,128)(2,1)S(1)}, u32[]{:S(2)}, u32[]{:S(2)}) collective-permute-start(bf16[512,256]{1,0:T(8,128)(2,1)S(1)} %add_convert_fusion.2), channel_id=1, source_target_pairs={{8,4},{9,5},{10,6},{11,7},{12,8},{13,9},{14,10},{15,11},{24,20},{2... | collective-permute-start | bytes 786440 | tf_op jit(solution)/shard_map/ppermute | solution.py:287
  53.2 10.9 %collective-permute-start.20 = (bf16[512,256]{1,0:T(8,128)(2,1)S(1)}, bf16[512,256]{1,0:T(8,128)(2,1)S(1)}, u32[]{:S(2)}, u32[]{:S(2)}) collective-permute-start(bf16[512,256]{1,0:T(8,128)(2,1)S(1)} %add_convert_fusion.1), channel_id=1, source_target_pairs={{4,0},{5,1},{6,2},{7,3},{8,4},{9,5},{10,6},{11,7},{12,8},{13,9},{1... | collective-permute-start | bytes 786440 | tf_op jit(solution)/shard_map/ppermute | solution.py:287
  59.4 6.5 %collective-permute-start.15 = (bf16[128,640]{1,0:T(8,128)(2,1)S(1)}, bf16[128,640]{1,0:T(8,128)(2,1)S(1)}, u32[]{:S(2)}, u32[]{:S(2)}) collective-permute-start(bf16[128,640]{1,0:T(8,128)(2,1)S(1)} %get-tuple-element.32), channel_id=1, source_target_pairs={{0,1},{1,0},{2,3},{3,2},{4,5},{5,4},{6,7},{7,6},{8,9},{9,8},{10,11... | collective-permute-start | bytes 491528 | tf_op jit(solution)/shard_map/ppermute | solution.py:246
  62.4 5.8 %collective-permute-start.16 = (bf16[128,640]{1,0:T(8,128)(2,1)S(1)}, bf16[128,640]{1,0:T(8,128)(2,1)S(1)}, u32[]{:S(2)}, u32[]{:S(2)}) collective-permute-start(bf16[128,640]{1,0:T(8,128)(2,1)S(1)} %get-tuple-element.33), channel_id=1, source_target_pairs={{0,2},{1,3},{2,0},{3,1},{4,6},{5,7},{6,4},{7,5},{8,10},{9,11},{10,... | collective-permute-start | bytes 491528 | tf_op jit(solution)/shard_map/ppermute | solution.py:246
  63.0 9.5 %collective-permute-start.17 = (bf16[128,640]{1,0:T(8,128)(2,1)S(1)}, bf16[128,640]{1,0:T(8,128)(2,1)S(1)}, u32[]{:S(2)}, u32[]{:S(2)}) collective-permute-start(bf16[128,640]{1,0:T(8,128)(2,1)S(1)} %get-tuple-element.34), channel_id=1, source_target_pairs={{0,3},{1,2},{2,1},{3,0},{4,7},{5,6},{6,5},{7,4},{8,11},{9,10},{10,... | collective-permute-start | bytes 491528 | tf_op jit(solution)/shard_map/ppermute | solution.py:246
  64.2 9.5 %collective-permute-start.23 = (bf16[128,256]{1,0:T(8,128)(2,1)S(1)}, bf16[128,256]{1,0:T(8,128)(2,1)S(1)}, u32[]{:S(2)}, u32[]{:S(2)}) collective-permute-start(bf16[128,256]{1,0:T(8,128)(2,1)S(1)} %get-tuple-element.47), channel_id=1, source_target_pairs={{0,3},{1,2},{2,1},{3,0},{4,7},{5,6},{6,5},{7,4},{8,11},{9,10},{10,... | collective-permute-start | bytes 196616 | tf_op jit(solution)/shard_map/ppermute | solution.py:246
  65.0 9.4 %collective-permute-start.22 = (bf16[128,256]{1,0:T(8,128)(2,1)S(1)}, bf16[128,256]{1,0:T(8,128)(2,1)S(1)}, u32[]{:S(2)}, u32[]{:S(2)}) collective-permute-start(bf16[128,256]{1,0:T(8,128)(2,1)S(1)} %get-tuple-element.48), channel_id=1, source_target_pairs={{0,2},{1,3},{2,0},{3,1},{4,6},{5,7},{6,4},{7,5},{8,10},{9,11},{10,... | collective-permute-start | bytes 196616 | tf_op jit(solution)/shard_map/ppermute | solution.py:246
  65.8 8.6 %collective-permute-start.21 = (bf16[128,256]{1,0:T(8,128)(2,1)S(1)}, bf16[128,256]{1,0:T(8,128)(2,1)S(1)}, u32[]{:S(2)}, u32[]{:S(2)}) collective-permute-start(bf16[128,256]{1,0:T(8,128)(2,1)S(1)} %get-tuple-element.49), channel_id=1, source_target_pairs={{0,1},{1,0},{2,3},{3,2},{4,5},{5,4},{6,7},{7,6},{8,9},{9,8},{10,11... | collective-permute-start | bytes 196616 | tf_op jit(solution)/shard_map/ppermute | solution.py:246

commit v4 on v3

--- a/solution.py
+++ b/solution.py
@@ -163,7 +163,7 @@
         out_shape=shapes,
         scratch_shapes=scratch,
         compiler_params=pltpu.CompilerParams(vmem_limit_bytes=VMEM_BYTES),
-        cost_estimate=pl.CostEstimate(flops=flops, bytes_accessed=1 << 20, transcendentals=0),
+        cost_estimate=pl.CostEstimate(flops=flops // 10, bytes_accessed=0, transcendentals=0),
     )(info, *operands)
 
 
@@ -209,27 +209,27 @@
     )
 
 
-def place_kernel(info, *refs):
-    rank = info[1]
-    sources, targets = refs[: 2 * KVH], refs[2 * KVH :]
-    query_grad, key_grad, value_grad = targets
+def place_queries_kernel(info, *refs):
     for d in range(KVH):
-        head = rank ^ d
-        wide = pl.ds(pl.multiple_of(head * (QPG * DH), DH), QPG * DH)
-        narrow = pl.ds(pl.multiple_of(head * DH, DH), DH)
-        query_grad[:, wide] = sources[d][...]
-        key_grad[:, narrow] = sources[KVH + d][:, :DH]
-        value_grad[:, narrow] = sources[KVH + d][:, DH:]
+        wide = pl.ds(pl.multiple_of((info[1] ^ d) * (QPG * DH), DH), QPG * DH)
+        refs[KVH][:, wide] = refs[d][...]
+
+
+def place_keys_kernel(info, *refs):
+    for d in range(KVH):
+        narrow = pl.ds(pl.multiple_of((info[1] ^ d) * DH, DH), DH)
+        refs[KVH][:, narrow] = refs[d][:, :DH]
+        refs[KVH + 1][:, narrow] = refs[d][:, DH:]
 
 
 def place_call(info, dq, dkv):
     tokens = dq[0].shape[0]
-    shapes = [
-        jax.ShapeDtypeStruct((tokens, KVH * QPG * DH), jnp.bfloat16),
-        jax.ShapeDtypeStruct((tokens, KVH * DH), jnp.bfloat16),
-        jax.ShapeDtypeStruct((tokens, KVH * DH), jnp.bfloat16),
-    ]
-    return local_call(place_kernel, shapes, 0, info, *dq, *dkv)
+    wide = jax.ShapeDtypeStruct((tokens, KVH * QPG * DH), jnp.bfloat16)
+    narrow = jax.ShapeDtypeStruct((tokens, KVH * DH), jnp.bfloat16)
+    return (
+        *local_call(place_queries_kernel, [wide], 0, info, *dq),
+        *local_call(place_keys_kernel, [narrow, narrow], 0, info, *dkv),
+    )
 
 
 def per_device(queries, keys, values, out_grad):
@@ -275,16 +275,20 @@
     dq = None
     arrived = None
     for offset in reversed(range(planes)):
-        results = backward_call(offset, info, chain[offset], q, g, finals, dq)
+        kv = chain[offset]
+        if offset == 0 and arrived:
+            kv = (after(kv[0], arrived[0]),) + kv[1:]
+        results = backward_call(offset, info, kv, q, g, finals, dq)
         total, dq = results[0], results[1:]
         if offset:
             dq = dq[0]
-        if arrived is not None:
-            total = total + arrived.astype(jnp.float32)
-        total = total.astype(jnp.bfloat16)
         if offset:
-            pairs = [(i + KVH, i) for i in range((offset - 1) * KVH, devices - KVH)]
-            arrived = lax.ppermute(total, "seq", pairs)
+            pairs = [(i + offset * KVH, i) for i in range(devices - offset * KVH)]
+            arrived = arrived or []
+            arrived.append(lax.ppermute(total.astype(jnp.bfloat16), "seq", pairs))
+    for part in arrived:
+        total = total + part.astype(jnp.float32)
+    total = total.astype(jnp.bfloat16)
     dq_back = [swap(dq[d], d) for d in range(KVH)]
     dkv_back = [swap(total[d * tokens : (d + 1) * tokens], d) for d in range(KVH)]
     return tuple(place_call(info, dq_back, dkv_back))

time: 77.1 us -> 74.9 us (0.971)
  the two profiles are of different devices: /device:TPU:9 before, /device:TPU:0 now
where the time goes in v4:
time: 74.9 us; the launch traced here: 74.6 us
  waiting for transfers between devices  34.2 us (46%)
  starting transfers between devices  24 us (32%)
  Pallas kernels  13.9 us (19%)
  local copies, waits for them, and re-layouts  1.17 us (2%)
  between operations  1 us (1%)
    ppermute x3, waiting for transfers between devices, per_device(): arrived.append(lax.ppermute(total.astype(jnp.bfloat16), 'seq', pairs))  22.8 us
    pallas_call x10, Pallas kernels, local_call(): pl.pallas_call(kernel, in_specs=[pl.BlockSpec(memory_space=pltpu.SMEM)] +...  13.9 us
    ppermute x15, waiting for transfers between devices, swap(): return lax.ppermute(array, 'seq', [(i, i ^ d) for i in range(devices)])  11.3 us
    ppermute x15, starting transfers between devices, swap(): return lax.ppermute(array, 'seq', [(i, i ^ d) for i in range(devices)])  10.5 us
    ppermute x6, starting transfers between devices, per_device(): lax.ppermute(half, 'seq', pairs)  9.63 us
    ppermute x3, starting transfers between devices, per_device(): arrived.append(lax.ppermute(total.astype(jnp.bfloat16), 'seq', pairs))  3.88 us
  transfers between devices with their start and end apart: 24, of which 9 were waited for; matrix products, arithmetic and copies ran while one was open for 1% of the time, Pallas kernels for 14%

profile of v4, /device:TPU:0, one launch (start us, length us, event | category | flops | bytes accessed | tf_op | source)
XLA Modules:
  0.0 74.6 jit_solution(14789417802261664873)
XLA Ops:
  0.7 1.0 %constant_dynamic-slice_fusion.4 = (bf16[128,128]{1,0:T(8,128)(2,1)S(1)}, bf16[128,128]{1,0:T(8,128)(2,1)S(1)}, bf16[128,128]{1,0:T(8,128)(2,1)S(1)}, bf16[128,1...) fusion(bf16[128,512]{1,0:T(8,128)(2,1)} %param.6, ...), kind=kLoop, calls=%fused_computation.11 | loop fusion | bytes 524304 | tf_op jit(solution)/shard_map/dynamic_slice | solution.py:249
  1.7 3.0 %collective-permute-start.4 = (bf16[128,256]{1,0:T(8,128)(2,1)S(1)}, bf16[128,256]{1,0:T(8,128)(2,1)S(1)}, u32[]{:S(2)}, u32[]{:S(2)}) collective-permute-start(bf16[128,256]{1,0:T(8,128)(2,1)S(1)} %pad_maximum_fusion.2), channel_id=1, source_target_pairs={{0,2},{1,3},{2,0},{3,1},{4,6},{5,7},{6,4},{7,5},{8,10},{9,11},{10,... | collective-permute-start | bytes 196616 | tf_op jit(solution)/shard_map/ppermute | solution.py:246
  4.8 0.1 collective-permute-start
  4.8 0.2 collective-permute-start.5
  5.0 0.1 constant_dynamic-slice_fusion.6
  5.1 1.0 %collective-permute-done = bf16[128,256]{1,0:T(8,128)(2,1)S(1)} collective-permute-done((bf16[128,256]{1,0:T(8,128)(2,1)S(1)}, bf16[128,256]{1,0:T(8,128)(2,1)S(1)}, u32[]{:S(2)}, u32[]{:S(2)}) %collective-permute-start) | collective-permute-done | bytes 65568 | tf_op jit(solution)/shard_map/ppermute | solution.py:246
  6.1 3.5 %collective-permute-start.1 = (bf16[256,256]{1,0:T(8,128)(2,1)S(1)}, bf16[256,256]{1,0:T(8,128)(2,1)S(1)}, u32[]{:S(2)}, u32[]{:S(2)}) collective-permute-start(bf16[256,256]{1,0:T(8,128)(2,1)S(1)} %pad_maximum_fusion.refs_0_), channel_id=1, source_target_pairs={{0,4},{1,5},{2,6},{3,7},{4,8},{5,9},{6,10},{7,11},{8,12},{9,13},{1... | collective-permute-start | bytes 393224 | tf_op jit(solution)/shard_map/ppermute | solution.py:268
  9.6 0.0 collective-permute-done.4
  9.6 0.0 collective-permute-done.5
  9.6 3.5 %collective-permute-start.6 = (bf16[256,256]{1,0:T(8,128)(2,1)S(1)}, bf16[256,256]{1,0:T(8,128)(2,1)S(1)}, u32[]{:S(2)}, u32[]{:S(2)}) collective-permute-start(bf16[256,256]{1,0:T(8,128)(2,1)S(1)} %constant_dynamic-update-slice_fusion.refs_1_), channel_id=1, source_target_pairs={{0,4},{1,5},{2,6},{3,7},{4,8},{5,9},{6,10},{7,11},{8,12},{9,13},{1... | collective-permute-start | bytes 393224 | tf_op jit(solution)/shard_map/ppermute | solution.py:268
  13.1 0.2 collective-permute-start.11
  13.3 1.1 %collective-permute-start.9 = (bf16[128,640]{1,0:T(8,128)(2,1)S(1)}, bf16[128,640]{1,0:T(8,128)(2,1)S(1)}, u32[]{:S(2)}, u32[]{:S(2)}) collective-permute-start(bf16[128,640]{1,0:T(8,128)(2,1)S(1)} %get-tuple-element.50), channel_id=1, source_target_pairs={{0,1},{1,0},{2,3},{3,2},{4,5},{5,4},{6,7},{7,6},{8,9},{9,8},{10,11... | collective-permute-start | bytes 491528 | tf_op jit(solution)/shard_map/ppermute | solution.py:246
  14.4 1.0 %collective-permute-start.10 = (bf16[128,640]{1,0:T(8,128)(2,1)S(1)}, bf16[128,640]{1,0:T(8,128)(2,1)S(1)}, u32[]{:S(2)}, u32[]{:S(2)}) collective-permute-start(bf16[128,640]{1,0:T(8,128)(2,1)S(1)} %get-tuple-element.52), channel_id=1, source_target_pairs={{0,2},{1,3},{2,0},{3,1},{4,6},{5,7},{6,4},{7,5},{8,10},{9,11},{10,... | collective-permute-start | bytes 491528 | tf_op jit(solution)/shard_map/ppermute | solution.py:246
  15.3 0.0 collective-permute-done.1.refs_0_
  15.3 0.7 collective-permute-start.2
  16.0 0.0 collective-permute-done.6.refs_1_
  16.0 0.7 collective-permute-start.7
  16.7 0.0 copy-done.1
  16.7 0.1 constant_dynamic-slice_fusion
  16.8 2.9 %collective-permute-done.11.refs_5_ = bf16[128,640]{1,0:T(8,128)(2,1)S(1)} collective-permute-done((bf16[128,640]{1,0:T(8,128)(2,1)S(1)}, bf16[128,640]{1,0:T(8,128)(2,1)S(1)}, u32[]{:S(2)}, u32[]{:S(2)}) %collective-permute-start.11) | collective-permute-done | bytes 163872 | tf_op jit(solution)/shard_map/ppermute | solution.py:246
  19.7 0.1 collective-permute-start.14
  19.8 0.0 collective-permute-done.9.refs_3_
  19.8 0.9 %collective-permute-start.12 = (bf16[128,640]{1,0:T(8,128)(2,1)S(1)}, bf16[128,640]{1,0:T(8,128)(2,1)S(1)}, u32[]{:S(2)}, u32[]{:S(2)}) collective-permute-start(bf16[128,640]{1,0:T(8,128)(2,1)S(1)} %get-tuple-element.46), channel_id=1, source_target_pairs={{0,1},{1,0},{2,3},{3,2},{4,5},{5,4},{6,7},{7,6},{8,9},{9,8},{10,11... | collective-permute-start | bytes 491528 | tf_op jit(solution)/shard_map/ppermute | solution.py:246
  20.8 2.0 %collective-permute-done.10.refs_4_ = bf16[128,640]{1,0:T(8,128)(2,1)S(1)} collective-permute-done((bf16[128,640]{1,0:T(8,128)(2,1)S(1)}, bf16[128,640]{1,0:T(8,128)(2,1)S(1)}, u32[]{:S(2)}, u32[]{:S(2)}) %collective-permute-start.10) | collective-permute-done | bytes 163872 | tf_op jit(solution)/shard_map/ppermute | solution.py:246
  22.8 0.9 %collective-permute-start.13 = (bf16[128,640]{1,0:T(8,128)(2,1)S(1)}, bf16[128,640]{1,0:T(8,128)(2,1)S(1)}, u32[]{:S(2)}, u32[]{:S(2)}) collective-permute-start(bf16[128,640]{1,0:T(8,128)(2,1)S(1)} %get-tuple-element.48), channel_id=1, source_target_pairs={{0,2},{1,3},{2,0},{3,1},{4,6},{5,7},{6,4},{7,5},{8,10},{9,11},{10,... | collective-permute-start | bytes 491528 | tf_op jit(solution)/shard_map/ppermute | solution.py:246
  23.6 0.0 collective-permute-done.2.refs_0_
  23.6 0.7 collective-permute-start.3
  24.3 0.0 collective-permute-done.7.refs_1_
  24.3 0.7 collective-permute-start.8
  25.0 0.1 pad_add_fusion.info
  25.1 2.5 %shard_map.67 = (f32[5,8,512]{2,1,0:T(8,128)S(1)}, f32[5,136,512]{2,1,0:T(8,128)S(1)}) custom-call(s32[2]{0:T(128)S(1)} %pad_add_fusion.info, bf16[256,256]{1,0:T(8,128)(2,1)S(1)} %pad_maximum_fusion.refs_0_, bf16[256,256]{1,0:T(8,128)(2,1)S(1)} %constant_dynamic-update-slice_fusion.refs_1_, bf16[128,640]{1,0:T(8,128)(2,1)S(1)} %get-tuple-element.51.refs_2_, ...), custom_call_target="tpu_custom_call" | custom-call | flops 134217728 | tf_op jit(solution)/shard_map/pallas_call | solution.py:159
  27.6 0.7 shard_map.68
  28.2 0.7 shard_map.69
  28.9 0.0 collective-permute-done.14.refs_9_
  28.9 0.0 collective-permute-done.12.refs_7_
  28.9 1.0 %collective-permute-done.13.refs_8_ = bf16[128,640]{1,0:T(8,128)(2,1)S(1)} collective-permute-done((bf16[128,640]{1,0:T(8,128)(2,1)S(1)}, bf16[128,640]{1,0:T(8,128)(2,1)S(1)}, u32[]{:S(2)}, u32[]{:S(2)}) %collective-permute-start.13) | collective-permute-done | bytes 163872 | tf_op jit(solution)/shard_map/ppermute | solution.py:246
  29.9 0.0 collective-permute-done.3.refs_0_
  29.9 0.0 collective-permute-done.8.refs_1_
  29.9 0.9 %shard_map.70.refs_10_ = f32[5,8,512]{2,1,0:T(8,128)S(1)} custom-call(s32[2]{0:T(128)S(1)} %pad_add_fusion.info, bf16[256,256]{1,0:T(8,128)(2,1)S(1)} %collective-permute-done.3.refs_0_, bf16[256,256]{1,0:T(8,128)(2,1)S(1)} %collective-permute-done.8.refs_1_, bf16[128,640]{1,0:T(8,128)(2,1)S(1)} %get-tuple-element.51.refs_2_, ...), custom_call_target="tpu_custom_call" | custom-call | flops 134217728 | tf_op jit(solution)/shard_map/pallas_call | solution.py:159
  30.8 0.9 %shard_map.71 = (f32[512,256]{1,0:T(8,128)S(1)}, f32[5,128,512]{2,1,0:T(8,128)S(1)}) custom-call(s32[2]{0:T(128)S(1)} %pad_add_fusion.info, bf16[256,256]{1,0:T(8,128)(2,1)S(1)} %collective-permute-done.3.refs_0_, bf16[256,256]{1,0:T(8,128)(2,1)S(1)} %collective-permute-done.8.refs_1_, bf16[128,640]{1,0:T(8,128)(2,1)S(1)} %get-tuple-element.51.refs_2_, ...), custom_call_target="tpu_custom_call" | custom-call | flops 335544320 | tf_op jit(solution)/shard_map/pallas_call | solution.py:159
  31.7 1.3 %collective-permute-start.15 = (bf16[512,256]{1,0:T(8,128)(2,1)S(1)}, bf16[512,256]{1,0:T(8,128)(2,1)S(1)}, u32[]{:S(2)}, u32[]{:S(2)}) collective-permute-start(bf16[512,256]{1,0:T(8,128)(2,1)S(1)} %convert_element_type.21), channel_id=1, source_target_pairs={{12,0},{13,1},{14,2},{15,3},{28,16},{29,17},{30,18},{31,19}} | collective-permute-start | bytes 786440 | tf_op jit(solution)/shard_map/ppermute | solution.py:288
  33.0 0.7 shard_map.72
  33.7 0.7 shard_map.73
  34.4 1.3 %collective-permute-start.20 = (bf16[512,256]{1,0:T(8,128)(2,1)S(1)}, bf16[512,256]{1,0:T(8,128)(2,1)S(1)}, u32[]{:S(2)}, u32[]{:S(2)}) collective-permute-start(bf16[512,256]{1,0:T(8,128)(2,1)S(1)} %convert_element_type.25), channel_id=1, source_target_pairs={{4,0},{5,1},{6,2},{7,3},{8,4},{9,5},{10,6},{11,7},{12,8},{13,9},{1... | collective-permute-start | bytes 786440 | tf_op jit(solution)/shard_map/ppermute | solution.py:288
  35.7 1.3 %collective-permute-start.19 = (bf16[512,256]{1,0:T(8,128)(2,1)S(1)}, bf16[512,256]{1,0:T(8,128)(2,1)S(1)}, u32[]{:S(2)}, u32[]{:S(2)}) collective-permute-start(bf16[512,256]{1,0:T(8,128)(2,1)S(1)} %convert_element_type.23), channel_id=1, source_target_pairs={{8,0},{9,1},{10,2},{11,3},{12,4},{13,5},{14,6},{15,7},{24,16},{25,... | collective-permute-start | bytes 786440 | tf_op jit(solution)/shard_map/ppermute | solution.py:288
  37.0 12.3 %collective-permute-done.15 = bf16[512,256]{1,0:T(8,128)(2,1)S(1)} collective-permute-done((bf16[512,256]{1,0:T(8,128)(2,1)S(1)}, bf16[512,256]{1,0:T(8,128)(2,1)S(1)}, u32[]{:S(2)}, u32[]{:S(2)}) %collective-permute-start.15) | collective-permute-done | bytes 262176 | tf_op jit(solution)/shard_map/ppermute | solution.py:288
  49.3 4.3 %shard_map.74 = (f32[512,256]{1,0:T(8,128)S(1)}, bf16[128,640]{1,0:T(8,128)(2,1)S(1)}, bf16[128,640]{1,0:T(8,128)(2,1)S(1)}, bf16[128,640]{1,0:T(8,128)(2,1)S(1)}, bf16[128,640]{1,0:T(8,128)(2,1)S(1)}) custom-call(s32[2]{0:T(128)S(1)} %pad_add_fusion.info, bf16[256,256]{1,0:T(8,128)(2,1)S(1)} %pad_maximum_fusion.refs_0_, ...), custom_call_target="tpu_custom_call" | custom-call | flops 335544320 | tf_op jit(solution)/shard_map/pallas_call | solution.py:159
  53.6 0.1 collective-permute-start.16
  53.7 1.1 %collective-permute-start.17 = (bf16[128,640]{1,0:T(8,128)(2,1)S(1)}, bf16[128,640]{1,0:T(8,128)(2,1)S(1)}, u32[]{:S(2)}, u32[]{:S(2)}) collective-permute-start(bf16[128,640]{1,0:T(8,128)(2,1)S(1)} %get-tuple-element.38), channel_id=1, source_target_pairs={{0,2},{1,3},{2,0},{3,1},{4,6},{5,7},{6,4},{7,5},{8,10},{9,11},{10,... | collective-permute-start | bytes 491528 | tf_op jit(solution)/shard_map/ppermute | solution.py:246
  54.8 0.7 collective-permute-start.18
  55.6 0.0 collective-permute-done.20
  55.6 10.5 %collective-permute-done.19 = bf16[512,256]{1,0:T(8,128)(2,1)S(1)} collective-permute-done((bf16[512,256]{1,0:T(8,128)(2,1)S(1)}, bf16[512,256]{1,0:T(8,128)(2,1)S(1)}, u32[]{:S(2)}, u32[]{:S(2)}) %collective-permute-start.19) | collective-permute-done | bytes 262176 | tf_op jit(solution)/shard_map/ppermute | solution.py:288
  66.1 0.1 add_convert_fusion
  66.2 0.1 collective-permute-start.23
  66.3 1.1 %collective-permute-start.22 = (bf16[128,256]{1,0:T(8,128)(2,1)S(1)}, bf16[128,256]{1,0:T(8,128)(2,1)S(1)}, u32[]{:S(2)}, u32[]{:S(2)}) collective-permute-start(bf16[128,256]{1,0:T(8,128)(2,1)S(1)} %get-tuple-element.54), channel_id=1, source_target_pairs={{0,2},{1,3},{2,0},{3,1},{4,6},{5,7},{6,4},{7,5},{8,10},{9,11},{10,... | collective-permute-start | bytes 196616 | tf_op jit(solution)/shard_map/ppermute | solution.py:246
  67.4 3.2 %collective-permute-done.23.refs_3_ = bf16[128,256]{1,0:T(8,128)(2,1)S(1)} collective-permute-done((bf16[128,256]{1,0:T(8,128)(2,1)S(1)}, bf16[128,256]{1,0:T(8,128)(2,1)S(1)}, u32[]{:S(2)}, u32[]{:S(2)}) %collective-permute-start.23) | collective-permute-done | bytes 65568 | tf_op jit(solution)/shard_map/ppermute | solution.py:246
  70.6 0.0 collective-permute-start.21
  70.6 0.8 %collective-permute-done.22.refs_2_ = bf16[128,256]{1,0:T(8,128)(2,1)S(1)} collective-permute-done((bf16[128,256]{1,0:T(8,128)(2,1)S(1)}, bf16[128,256]{1,0:T(8,128)(2,1)S(1)}, u32[]{:S(2)}, u32[]{:S(2)}) %collective-permute-start.22) | collective-permute-done | bytes 65568 | tf_op jit(solution)/shard_map/ppermute | solution.py:246
  71.4 0.5 collective-permute-done.21.refs_1_
  71.9 1.3 %shard_map.76 = (bf16[128,512]{1,0:T(8,128)(2,1)}, bf16[128,512]{1,0:T(8,128)(2,1)}) custom-call(s32[2]{0:T(128)S(1)} %pad_add_fusion.info, bf16[128,256]{1,0:T(8,128)(2,1)S(1)} %get-tuple-element.56.refs_0_, bf16[128,256]{1,0:T(8,128)(2,1)S(1)} %collective-permute-done.21.refs_1_, bf16[128,256]{1,0:T(8,128)(2,1)S(1)} %collective-permute-done.22.refs_2_, ...), custom_call_target="tpu_custom_call" | custom-call | tf_op jit(solution)/shard_map/pallas_call | solution.py:159
  73.1 0.0 collective-permute-done.16.refs_1_
  73.1 0.0 collective-permute-done.17.refs_2_
  73.1 0.0 collective-permute-done.18.refs_3_
  73.2 1.4 %shard_map.75 = bf16[128,2560]{1,0:T(8,128)(2,1)} custom-call(s32[2]{0:T(128)S(1)} %pad_add_fusion.info, bf16[128,640]{1,0:T(8,128)(2,1)S(1)} %get-tuple-element.36.refs_0_, bf16[128,640]{1,0:T(8,128)(2,1)S(1)} %collective-permute-done.16.refs_1_, bf16[128,640]{1,0:T(8,128)(2,1)S(1)} %collective-permute-done.17.refs_2_, ...), custom_call_target="tpu_custom_call" | custom-call | tf_op jit(solution)/shard_map/pallas_call | solution.py:159
  (13 shorter events, 0.2 us)
Async XLA Ops:
  0.6 4.4 %copy-start = (bf16[128,2560]{1,0:T(8,128)(2,1)S(1)}, bf16[128,2560]{1,0:T(8,128)(2,1)}, u32[]{:S(2)}) copy-start(bf16[128,2560]{1,0:T(8,128)(2,1)} %param.4) | copy-start | bytes 1966084
  0.7 16.0 %copy-start.1 = (bf16[128,2560]{1,0:T(8,128)(2,1)S(1)}, bf16[128,2560]{1,0:T(8,128)(2,1)}, u32[]{:S(2)}) copy-start(bf16[128,2560]{1,0:T(8,128)(2,1)} %param.7) | copy-start | bytes 1966084
  1.7 7.9 %collective-permute-start.4 = (bf16[128,256]{1,0:T(8,128)(2,1)S(1)}, bf16[128,256]{1,0:T(8,128)(2,1)S(1)}, u32[]{:S(2)}, u32[]{:S(2)}) collective-permute-start(bf16[128,256]{1,0:T(8,128)(2,1)S(1)} %pad_maximum_fusion.2), channel_id=1, source_target_pairs={{0,2},{1,3},{2,0},{3,1},{4,6},{5,7},{6,4},{7,5},{8,10},{9,11},{10,... | collective-permute-start | bytes 196616 | tf_op jit(solution)/shard_map/ppermute | solution.py:246
  4.8 1.3 %collective-permute-start = (bf16[128,256]{1,0:T(8,128)(2,1)S(1)}, bf16[128,256]{1,0:T(8,128)(2,1)S(1)}, u32[]{:S(2)}, u32[]{:S(2)}) collective-permute-start(bf16[128,256]{1,0:T(8,128)(2,1)S(1)} %pad_maximum_fusion.1), channel_id=1, source_target_pairs={{0,1},{1,0},{2,3},{3,2},{4,5},{5,4},{6,7},{7,6},{8,9},{9,8},{10,11... | collective-permute-start | bytes 196616 | tf_op jit(solution)/shard_map/ppermute | solution.py:246
  4.8 4.8 %collective-permute-start.5 = (bf16[128,256]{1,0:T(8,128)(2,1)S(1)}, bf16[128,256]{1,0:T(8,128)(2,1)S(1)}, u32[]{:S(2)}, u32[]{:S(2)}) collective-permute-start(bf16[128,256]{1,0:T(8,128)(2,1)S(1)} %pad_maximum_fusion.3), channel_id=1, source_target_pairs={{0,3},{1,2},{2,1},{3,0},{4,7},{5,6},{6,5},{7,4},{8,11},{9,10},{10,... | collective-permute-start | bytes 196616 | tf_op jit(solution)/shard_map/ppermute | solution.py:246
  6.1 9.2 %collective-permute-start.1 = (bf16[256,256]{1,0:T(8,128)(2,1)S(1)}, bf16[256,256]{1,0:T(8,128)(2,1)S(1)}, u32[]{:S(2)}, u32[]{:S(2)}) collective-permute-start(bf16[256,256]{1,0:T(8,128)(2,1)S(1)} %pad_maximum_fusion.refs_0_), channel_id=1, source_target_pairs={{0,4},{1,5},{2,6},{3,7},{4,8},{5,9},{6,10},{7,11},{8,12},{9,13},{1... | collective-permute-start | bytes 393224 | tf_op jit(solution)/shard_map/ppermute | solution.py:268
  9.6 6.4 %collective-permute-start.6 = (bf16[256,256]{1,0:T(8,128)(2,1)S(1)}, bf16[256,256]{1,0:T(8,128)(2,1)S(1)}, u32[]{:S(2)}, u32[]{:S(2)}) collective-permute-start(bf16[256,256]{1,0:T(8,128)(2,1)S(1)} %constant_dynamic-update-slice_fusion.refs_1_), channel_id=1, source_target_pairs={{0,4},{1,5},{2,6},{3,7},{4,8},{5,9},{6,10},{7,11},{8,12},{9,13},{1... | collective-permute-start | bytes 393224 | tf_op jit(solution)/shard_map/ppermute | solution.py:268
  13.1 6.6 %collective-permute-start.11 = (bf16[128,640]{1,0:T(8,128)(2,1)S(1)}, bf16[128,640]{1,0:T(8,128)(2,1)S(1)}, u32[]{:S(2)}, u32[]{:S(2)}) collective-permute-start(bf16[128,640]{1,0:T(8,128)(2,1)S(1)} %get-tuple-element.49), channel_id=1, source_target_pairs={{0,3},{1,2},{2,1},{3,0},{4,7},{5,6},{6,5},{7,4},{8,11},{9,10},{10,... | collective-permute-start | bytes 491528 | tf_op jit(solution)/shard_map/ppermute | solution.py:246
  13.3 6.5 %collective-permute-start.9 = (bf16[128,640]{1,0:T(8,128)(2,1)S(1)}, bf16[128,640]{1,0:T(8,128)(2,1)S(1)}, u32[]{:S(2)}, u32[]{:S(2)}) collective-permute-start(bf16[128,640]{1,0:T(8,128)(2,1)S(1)} %get-tuple-element.50), channel_id=1, source_target_pairs={{0,1},{1,0},{2,3},{3,2},{4,5},{5,4},{6,7},{7,6},{8,9},{9,8},{10,11... | collective-permute-start | bytes 491528 | tf_op jit(solution)/shard_map/ppermute | solution.py:246
  14.4 8.4 %collective-permute-start.10 = (bf16[128,640]{1,0:T(8,128)(2,1)S(1)}, bf16[128,640]{1,0:T(8,128)(2,1)S(1)}, u32[]{:S(2)}, u32[]{:S(2)}) collective-permute-start(bf16[128,640]{1,0:T(8,128)(2,1)S(1)} %get-tuple-element.52), channel_id=1, source_target_pairs={{0,2},{1,3},{2,0},{3,1},{4,6},{5,7},{6,4},{7,5},{8,10},{9,11},{10,... | collective-permute-start | bytes 491528 | tf_op jit(solution)/shard_map/ppermute | solution.py:246
  15.3 8.3 %collective-permute-start.2 = (bf16[256,256]{1,0:T(8,128)(2,1)S(1)}, bf16[256,256]{1,0:T(8,128)(2,1)S(1)}, u32[]{:S(2)}, u32[]{:S(2)}) collective-permute-start(bf16[256,256]{1,0:T(8,128)(2,1)S(1)} %collective-permute-done.1.refs_0_), channel_id=1, source_target_pairs={{4,8},{5,9},{6,10},{7,11},{8,12},{9,13},{10,14},{11,15},{20,24},{2... | collective-permute-start | bytes 393224 | tf_op jit(solution)/shard_map/ppermute | solution.py:268
  16.0 8.3 %collective-permute-start.7 = (bf16[256,256]{1,0:T(8,128)(2,1)S(1)}, bf16[256,256]{1,0:T(8,128)(2,1)S(1)}, u32[]{:S(2)}, u32[]{:S(2)}) collective-permute-start(bf16[256,256]{1,0:T(8,128)(2,1)S(1)} %collective-permute-done.6.refs_1_), channel_id=1, source_target_pairs={{4,8},{5,9},{6,10},{7,11},{8,12},{9,13},{10,14},{11,15},{20,24},{2... | collective-permute-start | bytes 393224 | tf_op jit(solution)/shard_map/ppermute | solution.py:268
  19.7 9.2 %collective-permute-start.14 = (bf16[128,640]{1,0:T(8,128)(2,1)S(1)}, bf16[128,640]{1,0:T(8,128)(2,1)S(1)}, u32[]{:S(2)}, u32[]{:S(2)}) collective-permute-start(bf16[128,640]{1,0:T(8,128)(2,1)S(1)} %get-tuple-element.45), channel_id=1, source_target_pairs={{0,3},{1,2},{2,1},{3,0},{4,7},{5,6},{6,5},{7,4},{8,11},{9,10},{10,... | collective-permute-start | bytes 491528 | tf_op jit(solution)/shard_map/ppermute | solution.py:246
  19.8 9.1 %collective-permute-start.12 = (bf16[128,640]{1,0:T(8,128)(2,1)S(1)}, bf16[128,640]{1,0:T(8,128)(2,1)S(1)}, u32[]{:S(2)}, u32[]{:S(2)}) collective-permute-start(bf16[128,640]{1,0:T(8,128)(2,1)S(1)} %get-tuple-element.46), channel_id=1, source_target_pairs={{0,1},{1,0},{2,3},{3,2},{4,5},{5,4},{6,7},{7,6},{8,9},{9,8},{10,11... | collective-permute-start | bytes 491528 | tf_op jit(solution)/shard_map/ppermute | solution.py:246
  22.8 7.1 %collective-permute-start.13 = (bf16[128,640]{1,0:T(8,128)(2,1)S(1)}, bf16[128,640]{1,0:T(8,128)(2,1)S(1)}, u32[]{:S(2)}, u32[]{:S(2)}) collective-permute-start(bf16[128,640]{1,0:T(8,128)(2,1)S(1)} %get-tuple-element.48), channel_id=1, source_target_pairs={{0,2},{1,3},{2,0},{3,1},{4,6},{5,7},{6,4},{7,5},{8,10},{9,11},{10,... | collective-permute-start | bytes 491528 | tf_op jit(solution)/shard_map/ppermute | solution.py:246
  23.6 6.3 %collective-permute-start.3 = (bf16[256,256]{1,0:T(8,128)(2,1)S(1)}, bf16[256,256]{1,0:T(8,128)(2,1)S(1)}, u32[]{:S(2)}, u32[]{:S(2)}) collective-permute-start(bf16[256,256]{1,0:T(8,128)(2,1)S(1)} %collective-permute-done.2.refs_0_), channel_id=1, source_target_pairs={{8,12},{9,13},{10,14},{11,15},{24,28},{25,29},{26,30},{27,31}} | collective-permute-start | bytes 393224 | tf_op jit(solution)/shard_map/ppermute | solution.py:268
  24.3 5.6 %collective-permute-start.8 = (bf16[256,256]{1,0:T(8,128)(2,1)S(1)}, bf16[256,256]{1,0:T(8,128)(2,1)S(1)}, u32[]{:S(2)}, u32[]{:S(2)}) collective-permute-start(bf16[256,256]{1,0:T(8,128)(2,1)S(1)} %collective-permute-done.7.refs_1_), channel_id=1, source_target_pairs={{8,12},{9,13},{10,14},{11,15},{24,28},{25,29},{26,30},{27,31}} | collective-permute-start | bytes 393224 | tf_op jit(solution)/shard_map/ppermute | solution.py:268
  31.7 17.7 %collective-permute-start.15 = (bf16[512,256]{1,0:T(8,128)(2,1)S(1)}, bf16[512,256]{1,0:T(8,128)(2,1)S(1)}, u32[]{:S(2)}, u32[]{:S(2)}) collective-permute-start(bf16[512,256]{1,0:T(8,128)(2,1)S(1)} %convert_element_type.21), channel_id=1, source_target_pairs={{12,0},{13,1},{14,2},{15,3},{28,16},{29,17},{30,18},{31,19}} | collective-permute-start | bytes 786440 | tf_op jit(solution)/shard_map/ppermute | solution.py:288
  34.4 21.2 %collective-permute-start.20 = (bf16[512,256]{1,0:T(8,128)(2,1)S(1)}, bf16[512,256]{1,0:T(8,128)(2,1)S(1)}, u32[]{:S(2)}, u32[]{:S(2)}) collective-permute-start(bf16[512,256]{1,0:T(8,128)(2,1)S(1)} %convert_element_type.25), channel_id=1, source_target_pairs={{4,0},{5,1},{6,2},{7,3},{8,4},{9,5},{10,6},{11,7},{12,8},{13,9},{1... | collective-permute-start | bytes 786440 | tf_op jit(solution)/shard_map/ppermute | solution.py:288
  35.7 30.4 %collective-permute-start.19 = (bf16[512,256]{1,0:T(8,128)(2,1)S(1)}, bf16[512,256]{1,0:T(8,128)(2,1)S(1)}, u32[]{:S(2)}, u32[]{:S(2)}) collective-permute-start(bf16[512,256]{1,0:T(8,128)(2,1)S(1)} %convert_element_type.23), channel_id=1, source_target_pairs={{8,0},{9,1},{10,2},{11,3},{12,4},{13,5},{14,6},{15,7},{24,16},{25,... | collective-permute-start | bytes 786440 | tf_op jit(solution)/shard_map/ppermute | solution.py:288
  53.6 19.5 %collective-permute-start.16 = (bf16[128,640]{1,0:T(8,128)(2,1)S(1)}, bf16[128,640]{1,0:T(8,128)(2,1)S(1)}, u32[]{:S(2)}, u32[]{:S(2)}) collective-permute-start(bf16[128,640]{1,0:T(8,128)(2,1)S(1)} %get-tuple-element.37), channel_id=1, source_target_pairs={{0,1},{1,0},{2,3},{3,2},{4,5},{5,4},{6,7},{7,6},{8,9},{9,8},{10,11... | collective-permute-start | bytes 491528 | tf_op jit(solution)/shard_map/ppermute | solution.py:246
  53.7 19.4 %collective-permute-start.17 = (bf16[128,640]{1,0:T(8,128)(2,1)S(1)}, bf16[128,640]{1,0:T(8,128)(2,1)S(1)}, u32[]{:S(2)}, u32[]{:S(2)}) collective-permute-start(bf16[128,640]{1,0:T(8,128)(2,1)S(1)} %get-tuple-element.38), channel_id=1, source_target_pairs={{0,2},{1,3},{2,0},{3,1},{4,6},{5,7},{6,4},{7,5},{8,10},{9,11},{10,... | collective-permute-start | bytes 491528 | tf_op jit(solution)/shard_map/ppermute | solution.py:246
  54.8 18.3 %collective-permute-start.18 = (bf16[128,640]{1,0:T(8,128)(2,1)S(1)}, bf16[128,640]{1,0:T(8,128)(2,1)S(1)}, u32[]{:S(2)}, u32[]{:S(2)}) collective-permute-start(bf16[128,640]{1,0:T(8,128)(2,1)S(1)} %get-tuple-element.39), channel_id=1, source_target_pairs={{0,3},{1,2},{2,1},{3,0},{4,7},{5,6},{6,5},{7,4},{8,11},{9,10},{10,... | collective-permute-start | bytes 491528 | tf_op jit(solution)/shard_map/ppermute | solution.py:246
  66.2 4.4 %collective-permute-start.23 = (bf16[128,256]{1,0:T(8,128)(2,1)S(1)}, bf16[128,256]{1,0:T(8,128)(2,1)S(1)}, u32[]{:S(2)}, u32[]{:S(2)}) collective-permute-start(bf16[128,256]{1,0:T(8,128)(2,1)S(1)} %get-tuple-element.53), channel_id=1, source_target_pairs={{0,3},{1,2},{2,1},{3,0},{4,7},{5,6},{6,5},{7,4},{8,11},{9,10},{10,... | collective-permute-start | bytes 196616 | tf_op jit(solution)/shard_map/ppermute | solution.py:246
  66.3 5.1 %collective-permute-start.22 = (bf16[128,256]{1,0:T(8,128)(2,1)S(1)}, bf16[128,256]{1,0:T(8,128)(2,1)S(1)}, u32[]{:S(2)}, u32[]{:S(2)}) collective-permute-start(bf16[128,256]{1,0:T(8,128)(2,1)S(1)} %get-tuple-element.54), channel_id=1, source_target_pairs={{0,2},{1,3},{2,0},{3,1},{4,6},{5,7},{6,4},{7,5},{8,10},{9,11},{10,... | collective-permute-start | bytes 196616 | tf_op jit(solution)/shard_map/ppermute | solution.py:246
  70.6 1.3 %collective-permute-start.21 = (bf16[128,256]{1,0:T(8,128)(2,1)S(1)}, bf16[128,256]{1,0:T(8,128)(2,1)S(1)}, u32[]{:S(2)}, u32[]{:S(2)}) collective-permute-start(bf16[128,256]{1,0:T(8,128)(2,1)S(1)} %get-tuple-element.55), channel_id=1, source_target_pairs={{0,1},{1,0},{2,3},{3,2},{4,5},{5,4},{6,7},{7,6},{8,9},{9,8},{10,11... | collective-permute-start | bytes 196616 | tf_op jit(solution)/shard_map/ppermute | solution.py:246

commit v5 on v3

--- a/solution.py
+++ b/solution.py
@@ -43,17 +43,17 @@
     return raw * (SCALING * LOG2E)
 
 
-def forward_kernel(offset, last, info, *refs):
+def forward_kernel(offset, planes, info, *refs):
     refs = list(refs)
     kv = [refs.pop(0) for _ in range(2)]
     q = [refs.pop(0) for _ in range(KVH)]
-    g = [refs.pop(0) for _ in range(KVH)] if last else None
+    top_plane = offset == planes - 1
+    closes = offset >= planes - 2
+    g = [refs.pop(0) for _ in range(KVH)] if closes else None
     if offset:
         old_stats, old_sums = refs.pop(0), refs.pop(0)
-    if last:
-        finals, stats, sums = refs
-    else:
-        stats, sums = refs
+    finals = refs.pop(0) if closes else None
+    stats, sums = refs
     tokens = q[0].shape[0]
 
     def update():
@@ -78,17 +78,7 @@
             stats[h, 0:1] = top
             sums[h] = added
 
-    if offset == 0:
-        update()
-    else:
-        pl.when(info[0] >= offset)(update)
-
-        @pl.when(info[0] < offset)
-        def _():
-            stats[...] = old_stats[...]
-            sums[...] = old_sums[...]
-
-    if last:
+    def close():
         for h in range(QPG):
             grads = stacked(g, h).T.astype(jnp.float32)
             weighted = jnp.sum(sums[h, :DH] * grads, axis=0, keepdims=True)
@@ -96,29 +86,44 @@
             finals[h, 0:1] = stats[h, 0:1] + jnp.log2(total)
             finals[h, 1:2] = weighted / total
 
-
-def backward_kernel(offset, first, info, *refs):
+    if offset == 0:
+        update()
+    else:
+        pl.when(info[0] >= offset)(update)
+    if offset and not top_plane:
+
+        @pl.when(info[0] < offset)
+        def _():
+            stats[...] = old_stats[...]
+            sums[...] = old_sums[...]
+
+    if closes:
+        pl.when((info[0] == planes - 1) == top_plane)(close)
+
+
+def backward_kernel(offset, planes, top_plane, first, info, *refs):
     refs = list(refs)
+    plane = info[0]
     kv = [refs.pop(0) for _ in range(2)]
     q = [refs.pop(0) for _ in range(KVH)]
     g = [refs.pop(0) for _ in range(KVH)]
     finals = refs.pop(0)
     dq_old = None if first else refs.pop(0)
+    own = offset == 0
+    passed = [refs.pop(0) for _ in range(1 + KVH)] if own and top_plane else None
     dkv = refs.pop(0)
-    dq_refs = refs
+    gathered = None if own else refs.pop()
+    ordered = refs[-5:] if own else None
+    dq_refs = refs[:-5] if own else refs
     tokens = q[0].shape[0]
-    last = offset == 0
 
     def work():
         key_rows, value_rows = keys_values(kv)
         key_columns = key_rows.T
-        mask = causal_mask(info, tokens) if last else None
         for h in range(QPG):
             query_rows = stacked(q, h)
             grad_rows = stacked(g, h)
             probs = jnp.exp2(scaled_scores(key_rows, query_rows) - finals[h, 0:1])
-            if last:
-                probs = jnp.where(mask, probs, 0.0)
             grad_probs = lax.dot_general(
                 value_rows, grad_rows, CONTRACT_LAST, preferred_element_type=jnp.float32
             )
@@ -128,30 +133,108 @@
                 probs.astype(jnp.bfloat16), grad_rows, preferred_element_type=jnp.float32
             )
             if h == 0:
-                dkv[:, :DH] = dk
-                dkv[:, DH:] = dv
+                gathered[:, :DH] = dk
+                gathered[:, DH:] = dv
             else:
-                dkv[:, :DH] += dk
-                dkv[:, DH:] += dv
+                gathered[:, :DH] += dk
+                gathered[:, DH:] += dv
             dq = jnp.dot(key_columns, grad_scores, preferred_element_type=jnp.float32)
             if dq_old is not None:
-                dq = dq + dq_old[h]
-            if last:
-                rows = dq.T.astype(jnp.bfloat16)
-                for d in range(KVH):
-                    dq_refs[d][:, h * DH : (h + 1) * DH] = rows[d * tokens : (d + 1) * tokens]
-            else:
-                dq_refs[0][h] = dq
-
-    if last:
-        work()
+                earlier = dq_old[h]
+                if not top_plane:
+                    earlier = jnp.where(plane > offset, earlier, 0.0)
+                dq = dq + earlier
+            dq_refs[0][h] = dq
+        dkv[...] = gathered[...].astype(dkv.dtype)
+
+    def own_work():
+        rank = info[1]
+
+        def place(j):
+            return pl.ds(pl.multiple_of((j ^ rank) * tokens, tokens), tokens)
+
+        def in_order(ref, h, row, rows):
+            return jnp.concatenate(
+                [ref[h, row : row + rows, place(j)] for j in range(KVH)], axis=1
+            )
+
+        kv_rows, q_rows, g_rows, dq_rows, dkv_rows = ordered
+        for d in range(KVH):
+            half = kv[d // 2]
+            kv_rows[place(d), :] = half[d % 2 * tokens : (d % 2 + 1) * tokens, :]
+            q_rows[place(d), :] = q[d][...]
+            g_rows[place(d), :] = g[d][...]
+        span = KVH * tokens
+        half = span // 2
+        masks = []
+        for part in range(2):
+            shape = (half * (part + 1), half)
+            key_at = lax.broadcasted_iota(jnp.int32, shape, 0)
+            masks.append(key_at <= lax.broadcasted_iota(jnp.int32, shape, 1) + part * half)
+        key_columns = kv_rows[:, :DH].T
+        for h in range(QPG):
+            columns = slice(h * DH, (h + 1) * DH)
+            log_total = in_order(finals, h, 0, 1)
+            row_delta = in_order(finals, h, 1, 1)
+            earlier = None
+            if dq_old is not None:
+                earlier = in_order(dq_old, h, 0, DH)
+                if not top_plane:
+                    earlier = jnp.where(plane > offset, earlier, 0.0)
+            for part in range(2):
+                reach = half * (part + 1)
+                lanes = slice(part * half, (part + 1) * half)
+                query_rows = q_rows[lanes, columns]
+                grad_rows = g_rows[lanes, columns]
+                scores = scaled_scores(kv_rows[:reach, :DH], query_rows)
+                probs = jnp.exp2(scores - log_total[:, lanes])
+                probs = jnp.where(masks[part], probs, 0.0)
+                grad_probs = lax.dot_general(
+                    kv_rows[:reach, DH:],
+                    grad_rows,
+                    CONTRACT_LAST,
+                    preferred_element_type=jnp.float32,
+                )
+                grad_scores = (probs * (grad_probs - row_delta[:, lanes]) * SCALING).astype(
+                    jnp.bfloat16
+                )
+                dk = jnp.dot(grad_scores, query_rows, preferred_element_type=jnp.float32)
+                dv = jnp.dot(
+                    probs.astype(jnp.bfloat16), grad_rows, preferred_element_type=jnp.float32
+                )
+                if h == 0 and part == 0:
+                    dkv_rows[:reach, :DH] = dk
+                    dkv_rows[:reach, DH:] = dv
+                elif h == 0:
+                    dkv_rows[:half, :DH] += dk[:half]
+                    dkv_rows[:half, DH:] += dv[:half]
+                    dkv_rows[half:, :DH] = dk[half:]
+                    dkv_rows[half:, DH:] = dv[half:]
+                else:
+                    dkv_rows[:reach, :DH] += dk
+                    dkv_rows[:reach, DH:] += dv
+                dq = jnp.dot(
+                    key_columns[:, :reach], grad_scores, preferred_element_type=jnp.float32
+                )
+                if earlier is not None:
+                    dq = dq + earlier[:, lanes]
+                dq_rows[lanes, columns] = dq.T.astype(jnp.bfloat16)
+        for d in range(KVH):
+            dq_refs[d][...] = dq_rows[place(d), :]
+            dkv[d * tokens : (d + 1) * tokens, :] = dkv_rows[place(d), :]
+
+    if own:
+        work = own_work
+    if top_plane:
+        pl.when(plane == planes - 1)(work)
+        if own:
+
+            @pl.when(plane < planes - 1)
+            def _():
+                for source, target in zip(passed, [dkv] + dq_refs):
+                    target[...] = source[...]
     else:
-        pl.when(info[0] >= offset)(work)
-
-        @pl.when(info[0] < offset)
-        def _():
-            dkv[...] = jnp.zeros_like(dkv)
-            dq_refs[0][...] = jnp.zeros_like(dq_refs[0]) if dq_old is None else dq_old[...]
+        pl.when((plane >= offset) & (plane < planes - 1))(work)
 
 
 def local_call(kernel, shapes, flops, info, *operands, scratch=()):
@@ -163,41 +246,48 @@
         out_shape=shapes,
         scratch_shapes=scratch,
         compiler_params=pltpu.CompilerParams(vmem_limit_bytes=VMEM_BYTES),
-        cost_estimate=pl.CostEstimate(flops=flops, bytes_accessed=1 << 20, transcendentals=0),
+        cost_estimate=pl.CostEstimate(flops=flops // 10, bytes_accessed=0, transcendentals=0),
     )(info, *operands)
 
 
-def forward_call(offset, last, info, kv, q, g, state):
+def forward_call(offset, planes, info, kv, q, g, state):
     tokens = q[0].shape[0]
     span = KVH * tokens
     stats = jax.ShapeDtypeStruct((QPG, 8, span), jnp.float32)
     sums = jax.ShapeDtypeStruct((QPG, DH + EXTRA, span), jnp.float32)
-    shapes = [stats] if last else [stats, sums]
-    scratch = [pltpu.VMEM(kept.shape, kept.dtype) for kept in (stats, sums)] if last else []
+    top_plane = offset == planes - 1
+    closes = offset >= planes - 2
+    shapes = [stats] * closes + [stats, sums] * (not top_plane)
+    kept = [pltpu.VMEM(part.shape, part.dtype) for part in (stats, sums)] * top_plane
     return local_call(
-        partial(forward_kernel, offset, last),
+        partial(forward_kernel, offset, planes),
         shapes,
         2 * 2 * QPG * span * span * DH * 2,
         info,
         *kv,
         *q,
-        *(g if last else []),
+        *(g if closes else []),
         *state,
-        scratch=scratch,
+        scratch=kept,
     )
 
 
-def backward_call(offset, info, kv, q, g, finals, dq_old):
+def backward_call(offset, planes, top_plane, info, kv, q, g, finals, dq_old, passed):
     tokens = q[0].shape[0]
     span = KVH * tokens
     first = dq_old is None
-    shapes = [jax.ShapeDtypeStruct((span, 2 * DH), jnp.float32)]
+    kind = jnp.bfloat16 if offset else jnp.float32
+    shapes = [jax.ShapeDtypeStruct((span, 2 * DH), kind)]
     if offset:
         shapes += [jax.ShapeDtypeStruct((QPG, DH, span), jnp.float32)]
     else:
         shapes += [jax.ShapeDtypeStruct((tokens, QPG * DH), jnp.bfloat16)] * KVH
+    kept = [(2 * DH, jnp.float32)]
+    if offset == 0:
+        wide = (QPG * DH, jnp.bfloat16)
+        kept = [(2 * DH, jnp.bfloat16), wide, wide, wide] + kept
     return local_call(
-        partial(backward_kernel, offset, first),
+        partial(backward_kernel, offset, planes, top_plane, first),
         shapes,
         5 * 2 * QPG * span * span * DH * 2,
         info,
@@ -206,6 +296,8 @@
         *g,
         finals,
         *([] if first else [dq_old]),
+        *passed,
+        scratch=[pltpu.VMEM((span, width), kind) for width, kind in kept],
     )
 
 
@@ -267,24 +359,48 @@
         pairs = [(i, i + KVH) for i in range((step - 1) * KVH, devices - KVH)]
         chain.append(tuple(lax.ppermute(half, "seq", pairs) for half in chain[-1]))
     state = []
-    for offset in range(planes):
-        last = offset == planes - 1
-        state = forward_call(offset, last, info, chain[offset], q, g, state)
-    finals = state[0]
-
-    dq = None
-    arrived = None
-    for offset in reversed(range(planes)):
-        results = backward_call(offset, info, chain[offset], q, g, finals, dq)
-        total, dq = results[0], results[1:]
-        if offset:
-            dq = dq[0]
-        if arrived is not None:
-            total = total + arrived.astype(jnp.float32)
-        total = total.astype(jnp.bfloat16)
-        if offset:
-            pairs = [(i + KVH, i) for i in range((offset - 1) * KVH, devices - KVH)]
-            arrived = lax.ppermute(total, "seq", pairs)
+    for offset in range(planes - 1):
+        state = forward_call(offset, planes, info, chain[offset], q, g, state)
+    finals, state = state[0], state[1:]
+    arrived = []
+
+    def gradients(top_plane, finals, passed):
+        dq = None
+        start = planes - 1 if top_plane else planes - 2
+        for offset in reversed(range(start + 1)):
+            kv = chain[offset]
+            if top_plane and offset == 0:
+                kv = (after(kv[0], *arrived[: planes - 2]), kv[1])
+            if offset == planes - 2 and not top_plane:
+                kv = (after(kv[0], *chain[-1]), kv[1])
+            results = backward_call(
+                offset,
+                planes,
+                top_plane,
+                info,
+                kv,
+                q,
+                g,
+                finals,
+                dq,
+                passed if offset == 0 else [],
+            )
+            if offset == 0:
+                return results
+            senders = range(devices - KVH, devices) if top_plane else range(offset * KVH, devices - KVH)
+            pairs = [(i, i - offset * KVH) for i in senders]
+            arrived.append(lax.ppermute(results[0], "seq", pairs))
+            dq = results[1]
+
+    lower = gradients(False, finals, [])
+    top_kv = (after(chain[-1][0], lower[1]), chain[-1][1])
+    finals = forward_call(planes - 1, planes, info, top_kv, q, g, state)[0]
+    results = gradients(True, finals, lower)
+    total, dq = results[0], results[1:]
+    for part in arrived:
+        total = total + part.astype(jnp.float32)
+    total = total.astype(jnp.bfloat16)
+    dq = [dq[0], after(dq[1], arrived[planes - 2])] + list(dq[2:])
     dq_back = [swap(dq[d], d) for d in range(KVH)]
     dkv_back = [swap(total[d * tokens : (d + 1) * tokens], d) for d in range(KVH)]
     return tuple(place_call(info, dq_back, dkv_back))

time: 77.1 us -> 74 us (0.960)
  waiting for transfers between devices: 25.5 us -> 19 us
  starting transfers between devices: 30.4 us -> 33.2 us
  Pallas kernels: 17.7 us -> 18.9 us
    ppermute x15, waiting for transfers between devices: 9.95 us -> 4.41 us  [swap(): return lax.ppermute(array, 'seq', [(i, i ^ d) for i in range(devices)])]
    ppermute x15, starting transfers between devices: 14.4 us -> 15.9 us  [swap(): return lax.ppermute(array, 'seq', [(i, i ^ d) for i in range(devices)])]
    ppermute x3 -> x5, starting transfers between devices: 3.89 us -> 5.24 us  [gradients(): arrived.append(lax.ppermute(results[0], 'seq', pairs))]
    pallas_call x9 -> x12, Pallas kernels: 17.7 us -> 18.9 us  [local_call(): pl.pallas_call(kernel, in_specs=[pl.BlockSpec(memory_space=pltpu.SMEM)] +...]
    ppermute x3 -> x5, waiting for transfers between devices: 15.5 us -> 14.6 us  [gradients(): arrived.append(lax.ppermute(results[0], 'seq', pairs))]
  transfers between devices with their start and end apart: 24 -> 26, of which waited for: 7 -> 8; matrix products, arithmetic and copies ran while one was open for 0% -> 1% of each run, Pallas kernels for 19% -> 23%
where the time goes in v5:
time: 74 us; the launch traced here: 73.7 us
  starting transfers between devices  33.2 us (45%)
  waiting for transfers between devices  19 us (26%)
  Pallas kernels  18.9 us (26%)
  local copies, waits for them, and re-layouts  1.17 us (2%)
  between operations  1.02 us (1%)
    pallas_call x12, Pallas kernels, local_call(): pl.pallas_call(kernel, in_specs=[pl.BlockSpec(memory_space=pltpu.SMEM)] +...  18.9 us
    ppermute x15, starting transfers between devices, swap(): return lax.ppermute(array, 'seq', [(i, i ^ d) for i in range(devices)])  15.9 us
    ppermute x5, waiting for transfers between devices, gradients(): arrived.append(lax.ppermute(results[0], 'seq', pairs))  14.6 us
    ppermute x6, starting transfers between devices, per_device(): lax.ppermute(half, 'seq', pairs)  12.1 us
    ppermute x5, starting transfers between devices, gradients(): arrived.append(lax.ppermute(results[0], 'seq', pairs))  5.24 us
    ppermute x15, waiting for transfers between devices, swap(): return lax.ppermute(array, 'seq', [(i, i ^ d) for i in range(devices)])  4.41 us
  transfers between devices with their start and end apart: 26, of which 8 were waited for; matrix products, arithmetic and copies ran while one was open for 1% of the time, Pallas kernels for 23%

profile of v5, /device:TPU:9, one launch (start us, length us, event | category | flops | bytes accessed | tf_op | source)
XLA Modules:
  0.0 73.7 jit_solution(741026725722189627)
XLA Ops:
  0.7 1.0 %constant_dynamic-slice_fusion.4 = (bf16[128,128]{1,0:T(8,128)(2,1)S(1)}, bf16[128,128]{1,0:T(8,128)(2,1)S(1)}, bf16[128,128]{1,0:T(8,128)(2,1)S(1)}, bf16[128,1...) fusion(bf16[128,512]{1,0:T(8,128)(2,1)} %param.6, ...), kind=kLoop, calls=%fused_computation.11 | loop fusion | bytes 524304 | tf_op jit(solution)/shard_map/dynamic_slice | solution.py:341
  1.7 1.3 %collective-permute-start.4 = (bf16[128,256]{1,0:T(8,128)(2,1)S(1)}, bf16[128,256]{1,0:T(8,128)(2,1)S(1)}, u32[]{:S(2)}, u32[]{:S(2)}) collective-permute-start(bf16[128,256]{1,0:T(8,128)(2,1)S(1)} %pad_maximum_fusion.2), channel_id=1, source_target_pairs={{0,2},{1,3},{2,0},{3,1},{4,6},{5,7},{6,4},{7,5},{8,10},{9,11},{10,... | collective-permute-start | bytes 196616 | tf_op jit(solution)/shard_map/ppermute | solution.py:338
  3.0 1.0 %collective-permute-start = (bf16[128,256]{1,0:T(8,128)(2,1)S(1)}, bf16[128,256]{1,0:T(8,128)(2,1)S(1)}, u32[]{:S(2)}, u32[]{:S(2)}) collective-permute-start(bf16[128,256]{1,0:T(8,128)(2,1)S(1)} %pad_maximum_fusion.1), channel_id=1, source_target_pairs={{0,1},{1,0},{2,3},{3,2},{4,5},{5,4},{6,7},{7,6},{8,9},{9,8},{10,11... | collective-permute-start | bytes 196616 | tf_op jit(solution)/shard_map/ppermute | solution.py:338
  4.1 0.2 collective-permute-start.5
  4.3 0.1 constant_dynamic-slice_fusion.6
  4.3 0.6 collective-permute-done
  5.0 3.2 %collective-permute-start.1 = (bf16[256,256]{1,0:T(8,128)(2,1)S(1)}, bf16[256,256]{1,0:T(8,128)(2,1)S(1)}, u32[]{:S(2)}, u32[]{:S(2)}) collective-permute-start(bf16[256,256]{1,0:T(8,128)(2,1)S(1)} %pad_maximum_fusion.refs_0_), channel_id=1, source_target_pairs={{0,4},{1,5},{2,6},{3,7},{4,8},{5,9},{6,10},{7,11},{8,12},{9,13},{1... | collective-permute-start | bytes 393224 | tf_op jit(solution)/shard_map/ppermute | solution.py:360
  8.2 0.0 collective-permute-done.4
  8.2 0.0 collective-permute-done.5
  8.2 3.2 %collective-permute-start.6 = (bf16[256,256]{1,0:T(8,128)(2,1)S(1)}, bf16[256,256]{1,0:T(8,128)(2,1)S(1)}, u32[]{:S(2)}, u32[]{:S(2)}) collective-permute-start(bf16[256,256]{1,0:T(8,128)(2,1)S(1)} %constant_dynamic-update-slice_fusion.refs_1_), channel_id=1, source_target_pairs={{0,4},{1,5},{2,6},{3,7},{4,8},{5,9},{6,10},{7,11},{8,12},{9,13},{1... | collective-permute-start | bytes 393224 | tf_op jit(solution)/shard_map/ppermute | solution.py:360
  11.4 1.6 %collective-permute-start.11 = (bf16[128,640]{1,0:T(8,128)(2,1)S(1)}, bf16[128,640]{1,0:T(8,128)(2,1)S(1)}, u32[]{:S(2)}, u32[]{:S(2)}) collective-permute-start(bf16[128,640]{1,0:T(8,128)(2,1)S(1)} %get-tuple-element.71), channel_id=1, source_target_pairs={{0,3},{1,2},{2,1},{3,0},{4,7},{5,6},{6,5},{7,4},{8,11},{9,10},{10,... | collective-permute-start | bytes 491528 | tf_op jit(solution)/shard_map/ppermute | solution.py:338
  13.1 0.0 collective-permute-start.9
  13.1 0.7 collective-permute-start.10
  13.8 0.0 collective-permute-done.1.refs_0_
  13.8 2.4 %collective-permute-start.2 = (bf16[256,256]{1,0:T(8,128)(2,1)S(1)}, bf16[256,256]{1,0:T(8,128)(2,1)S(1)}, u32[]{:S(2)}, u32[]{:S(2)}) collective-permute-start(bf16[256,256]{1,0:T(8,128)(2,1)S(1)} %collective-permute-done.1.refs_0_), channel_id=1, source_target_pairs={{4,8},{5,9},{6,10},{7,11},{8,12},{9,13},{10,14},{11,15},{20,24},{2... | collective-permute-start | bytes 393224 | tf_op jit(solution)/shard_map/ppermute | solution.py:360
  16.2 0.0 collective-permute-done.6.refs_1_
  16.2 1.9 %collective-permute-start.7 = (bf16[256,256]{1,0:T(8,128)(2,1)S(1)}, bf16[256,256]{1,0:T(8,128)(2,1)S(1)}, u32[]{:S(2)}, u32[]{:S(2)}) collective-permute-start(bf16[256,256]{1,0:T(8,128)(2,1)S(1)} %collective-permute-done.6.refs_1_), channel_id=1, source_target_pairs={{4,8},{5,9},{6,10},{7,11},{8,12},{9,13},{10,14},{11,15},{20,24},{2... | collective-permute-start | bytes 393224 | tf_op jit(solution)/shard_map/ppermute | solution.py:360
  18.1 0.1 constant_dynamic-slice_fusion
  18.2 0.0 collective-permute-done.11.refs_5_
  18.2 2.2 %collective-permute-start.14 = (bf16[128,640]{1,0:T(8,128)(2,1)S(1)}, bf16[128,640]{1,0:T(8,128)(2,1)S(1)}, u32[]{:S(2)}, u32[]{:S(2)}) collective-permute-start(bf16[128,640]{1,0:T(8,128)(2,1)S(1)} %get-tuple-element.67), channel_id=1, source_target_pairs={{0,3},{1,2},{2,1},{3,0},{4,7},{5,6},{6,5},{7,4},{8,11},{9,10},{10,... | collective-permute-start | bytes 491528 | tf_op jit(solution)/shard_map/ppermute | solution.py:338
  20.4 0.0 collective-permute-done.9.refs_3_
  20.4 0.0 collective-permute-start.12
  20.4 1.1 %collective-permute-done.10.refs_4_ = bf16[128,640]{1,0:T(8,128)(2,1)S(1)} collective-permute-done((bf16[128,640]{1,0:T(8,128)(2,1)S(1)}, bf16[128,640]{1,0:T(8,128)(2,1)S(1)}, u32[]{:S(2)}, u32[]{:S(2)}) %collective-permute-start.10) | collective-permute-done | bytes 163872 | tf_op jit(solution)/shard_map/ppermute | solution.py:338
  21.6 0.6 collective-permute-start.13
  22.2 0.0 collective-permute-done.2.refs_0_
  22.2 0.7 collective-permute-start.3
  22.8 0.0 collective-permute-done.7.refs_1_
  22.8 0.7 collective-permute-start.8
  23.5 0.1 pad_add_fusion.info
  23.6 2.5 %shard_map.67 = (f32[5,8,512]{2,1,0:T(8,128)S(1)}, f32[5,136,512]{2,1,0:T(8,128)S(1)}) custom-call(s32[2]{0:T(128)S(1)} %pad_add_fusion.info, bf16[256,256]{1,0:T(8,128)(2,1)S(1)} %pad_maximum_fusion.refs_0_, bf16[256,256]{1,0:T(8,128)(2,1)S(1)} %constant_dynamic-update-slice_fusion.refs_1_, bf16[128,640]{1,0:T(8,128)(2,1)S(1)} %get-tuple-element.73.refs_2_, ...), custom_call_target="tpu_custom_call" | custom-call | flops 134217728 | tf_op jit(solution)/shard_map/pallas_call | solution.py:242
  26.1 2.5 %shard_map.68 = (f32[5,8,512]{2,1,0:T(8,128)S(1)}, f32[5,136,512]{2,1,0:T(8,128)S(1)}) custom-call(s32[2]{0:T(128)S(1)} %pad_add_fusion.info, bf16[256,256]{1,0:T(8,128)(2,1)S(1)} %collective-permute-done.1.refs_0_, bf16[256,256]{1,0:T(8,128)(2,1)S(1)} %collective-permute-done.6.refs_1_, bf16[128,640]{1,0:T(8,128)(2,1)S(1)} %get-tuple-element.73.refs_2_, ...), custom_call_target="tpu_custom_call" | custom-call | flops 134217728 | tf_op jit(solution)/shard_map/pallas_call | solution.py:242
  28.6 0.0 collective-permute-done.14.refs_9_
  28.6 0.1 collective-permute-done.13.refs_8_
  28.7 0.9 %shard_map.69 = (f32[5,8,512]{2,1,0:T(8,128)S(1)}, f32[5,8,512]{2,1,0:T(8,128)S(1)}, f32[5,136,512]{2,1,0:T(8,128)S(1)}) custom-call(s32[2]{0:T(128)S(1)} %pad_add_fusion.info, bf16[256,256]{1,0:T(8,128)(2,1)S(1)} %collective-permute-done.2.refs_0_, bf16[256,256]{1,0:T(8,128)(2,1)S(1)} %collective-permute-done.7.refs_1_, ...), custom_call_target="tpu_custom_call" | custom-call | flops 134217728 | tf_op jit(solution)/shard_map/pallas_call | solution.py:242
  29.7 0.0 collective-permute-done.8.refs_1_
  29.7 0.6 shard_map.70
  30.2 0.7 collective-permute-start.15
  30.9 4.0 %shard_map.71 = (bf16[512,256]{1,0:T(8,128)(2,1)S(1)}, f32[5,128,512]{2,1,0:T(8,128)S(1)}) custom-call(s32[2]{0:T(128)S(1)} %pad_add_fusion.info, bf16[256,256]{1,0:T(8,128)(2,1)S(1)} %collective-permute-done.1.refs_0_, bf16[256,256]{1,0:T(8,128)(2,1)S(1)} %collective-permute-done.6.refs_1_, bf16[128,640]{1,0:T(8,128)(2,1)S(1)} %get-tuple-element.73.refs_2_, ...), custom_call_target="tpu_custom_call" | custom-call | flops 335544320 | tf_op jit(solution)/shard_map/pallas_call | solution.py:242
  34.9 1.9 %collective-permute-start.16 = (bf16[512,256]{1,0:T(8,128)(2,1)S(1)}, bf16[512,256]{1,0:T(8,128)(2,1)S(1)}, u32[]{:S(2)}, u32[]{:S(2)}) collective-permute-start(bf16[512,256]{1,0:T(8,128)(2,1)S(1)} %get-tuple-element.44), channel_id=1, source_target_pairs={{4,0},{5,1},{6,2},{7,3},{8,4},{9,5},{10,6},{11,7},{20,16},{21,17},... | collective-permute-start | bytes 786440 | tf_op jit(solution)/shard_map/ppermute | solution.py:392
  36.8 3.9 %shard_map.72 = (f32[512,256]{1,0:T(8,128)S(1)}, bf16[128,640]{1,0:T(8,128)(2,1)S(1)}, bf16[128,640]{1,0:T(8,128)(2,1)S(1)}, bf16[128,640]{1,0:T(8,128)(2,1)S(1)}, bf16[128,640]{1,0:T(8,128)(2,1)S(1)}) custom-call(s32[2]{0:T(128)S(1)} %pad_add_fusion.info, bf16[256,256]{1,0:T(8,128)(2,1)S(1)} %pad_maximum_fusion.refs_0_, ...), custom_call_target="tpu_custom_call" | custom-call | flops 335544320 | tf_op jit(solution)/shard_map/pallas_call | solution.py:242
  40.7 0.6 shard_map.73.refs_10_
  41.3 0.6 shard_map.74
  41.8 0.7 collective-permute-start.17
  42.5 0.8 %shard_map.75 = (bf16[512,256]{1,0:T(8,128)(2,1)S(1)}, f32[5,128,512]{2,1,0:T(8,128)S(1)}) custom-call(s32[2]{0:T(128)S(1)} %pad_add_fusion.info, bf16[256,256]{1,0:T(8,128)(2,1)S(1)} %collective-permute-done.2.refs_0_, bf16[256,256]{1,0:T(8,128)(2,1)S(1)} %collective-permute-done.7.refs_1_, bf16[128,640]{1,0:T(8,128)(2,1)S(1)} %get-tuple-element.73.refs_2_, ...), custom_call_target="tpu_custom_call" | custom-call | flops 335544320 | tf_op jit(solution)/shard_map/pallas_call | solution.py:242
  43.3 0.6 shard_map.76
  43.9 0.7 collective-permute-start.22
  44.5 1.3 %collective-permute-start.21 = (bf16[512,256]{1,0:T(8,128)(2,1)S(1)}, bf16[512,256]{1,0:T(8,128)(2,1)S(1)}, u32[]{:S(2)}, u32[]{:S(2)}) collective-permute-start(bf16[512,256]{1,0:T(8,128)(2,1)S(1)} %get-tuple-element.65), channel_id=1, source_target_pairs={{12,4},{13,5},{14,6},{15,7},{28,20},{29,21},{30,22},{31,23}} | collective-permute-start | bytes 786440 | tf_op jit(solution)/shard_map/ppermute | solution.py:392
  45.8 0.0 collective-permute-done.15
  45.8 10.0 %collective-permute-done.16 = bf16[512,256]{1,0:T(8,128)(2,1)S(1)} collective-permute-done((bf16[512,256]{1,0:T(8,128)(2,1)S(1)}, bf16[512,256]{1,0:T(8,128)(2,1)S(1)}, u32[]{:S(2)}, u32[]{:S(2)}) %collective-permute-start.16) | collective-permute-done | bytes 262176 | tf_op jit(solution)/shard_map/ppermute | solution.py:392
  55.8 0.6 shard_map.77
  56.5 0.8 %collective-permute-start.19 = (bf16[128,640]{1,0:T(8,128)(2,1)S(1)}, bf16[128,640]{1,0:T(8,128)(2,1)S(1)}, u32[]{:S(2)}, u32[]{:S(2)}) collective-permute-start(bf16[128,640]{1,0:T(8,128)(2,1)S(1)} %get-tuple-element.62), channel_id=1, source_target_pairs={{0,2},{1,3},{2,0},{3,1},{4,6},{5,7},{6,4},{7,5},{8,10},{9,11},{10,... | collective-permute-start | bytes 491528 | tf_op jit(solution)/shard_map/ppermute | solution.py:338
  57.3 2.1 %collective-permute-start.20 = (bf16[128,640]{1,0:T(8,128)(2,1)S(1)}, bf16[128,640]{1,0:T(8,128)(2,1)S(1)}, u32[]{:S(2)}, u32[]{:S(2)}) collective-permute-start(bf16[128,640]{1,0:T(8,128)(2,1)S(1)} %get-tuple-element.63), channel_id=1, source_target_pairs={{0,3},{1,2},{2,1},{3,0},{4,7},{5,6},{6,5},{7,4},{8,11},{9,10},{10,... | collective-permute-start | bytes 491528 | tf_op jit(solution)/shard_map/ppermute | solution.py:338
  59.4 0.0 collective-permute-done.17
  59.4 0.0 collective-permute-start.18
  59.4 0.0 collective-permute-done.22
  59.4 4.6 %collective-permute-done.21 = bf16[512,256]{1,0:T(8,128)(2,1)S(1)} collective-permute-done((bf16[512,256]{1,0:T(8,128)(2,1)S(1)}, bf16[512,256]{1,0:T(8,128)(2,1)S(1)}, u32[]{:S(2)}, u32[]{:S(2)}) %collective-permute-start.21) | collective-permute-done | bytes 262176 | tf_op jit(solution)/shard_map/ppermute | solution.py:392
  64.0 0.2 add_convert_fusion
  64.2 3.4 %collective-permute-start.25 = (bf16[128,256]{1,0:T(8,128)(2,1)S(1)}, bf16[128,256]{1,0:T(8,128)(2,1)S(1)}, u32[]{:S(2)}, u32[]{:S(2)}) collective-permute-start(bf16[128,256]{1,0:T(8,128)(2,1)S(1)} %get-tuple-element.75), channel_id=1, source_target_pairs={{0,3},{1,2},{2,1},{3,0},{4,7},{5,6},{6,5},{7,4},{8,11},{9,10},{10,... | collective-permute-start | bytes 196616 | tf_op jit(solution)/shard_map/ppermute | solution.py:338
  67.6 0.8 %collective-permute-start.24 = (bf16[128,256]{1,0:T(8,128)(2,1)S(1)}, bf16[128,256]{1,0:T(8,128)(2,1)S(1)}, u32[]{:S(2)}, u32[]{:S(2)}) collective-permute-start(bf16[128,256]{1,0:T(8,128)(2,1)S(1)} %get-tuple-element.76), channel_id=1, source_target_pairs={{0,2},{1,3},{2,0},{3,1},{4,6},{5,7},{6,4},{7,5},{8,10},{9,11},{10,... | collective-permute-start | bytes 196616 | tf_op jit(solution)/shard_map/ppermute | solution.py:338
  68.4 1.6 %collective-permute-done.25.refs_7_ = bf16[128,256]{1,0:T(8,128)(2,1)S(1)} collective-permute-done((bf16[128,256]{1,0:T(8,128)(2,1)S(1)}, bf16[128,256]{1,0:T(8,128)(2,1)S(1)}, u32[]{:S(2)}, u32[]{:S(2)}) %collective-permute-start.25) | collective-permute-done | bytes 65568 | tf_op jit(solution)/shard_map/ppermute | solution.py:338
  70.1 1.1 %collective-permute-start.23 = (bf16[128,256]{1,0:T(8,128)(2,1)S(1)}, bf16[128,256]{1,0:T(8,128)(2,1)S(1)}, u32[]{:S(2)}, u32[]{:S(2)}) collective-permute-start(bf16[128,256]{1,0:T(8,128)(2,1)S(1)} %get-tuple-element.77), channel_id=1, source_target_pairs={{0,1},{1,0},{2,3},{3,2},{4,5},{5,4},{6,7},{7,6},{8,9},{9,8},{10,11... | collective-permute-start | bytes 196616 | tf_op jit(solution)/shard_map/ppermute | solution.py:338
  71.2 0.5 collective-permute-done.24.refs_6_
  71.7 0.4 collective-permute-done.23.refs_5_
  72.1 1.6 %shard_map.78 = (bf16[128,2560]{1,0:T(8,128)(2,1)}, bf16[128,512]{1,0:T(8,128)(2,1)}, bf16[128,512]{1,0:T(8,128)(2,1)}) custom-call(s32[2]{0:T(128)S(1)} %pad_add_fusion.info, bf16[128,640]{1,0:T(8,128)(2,1)S(1)} %get-tuple-element.58.refs_0_, bf16[128,640]{1,0:T(8,128)(2,1)S(1)} %collective-permute-done.18.refs_1_, ...), custom_call_target="tpu_custom_call" | custom-call | tf_op jit(solution)/shard_map/pallas_call | solution.py:242
  (16 shorter events, 0.1 us)
Async XLA Ops:
  0.6 3.6 %copy-start = (bf16[128,2560]{1,0:T(8,128)(2,1)S(1)}, bf16[128,2560]{1,0:T(8,128)(2,1)}, u32[]{:S(2)}) copy-start(bf16[128,2560]{1,0:T(8,128)(2,1)} %param.4) | copy-start | bytes 1966084
  0.7 17.4 %copy-start.1 = (bf16[128,2560]{1,0:T(8,128)(2,1)S(1)}, bf16[128,2560]{1,0:T(8,128)(2,1)}, u32[]{:S(2)}) copy-start(bf16[128,2560]{1,0:T(8,128)(2,1)} %param.7) | copy-start | bytes 1966084
  1.7 6.5 %collective-permute-start.4 = (bf16[128,256]{1,0:T(8,128)(2,1)S(1)}, bf16[128,256]{1,0:T(8,128)(2,1)S(1)}, u32[]{:S(2)}, u32[]{:S(2)}) collective-permute-start(bf16[128,256]{1,0:T(8,128)(2,1)S(1)} %pad_maximum_fusion.2), channel_id=1, source_target_pairs={{0,2},{1,3},{2,0},{3,1},{4,6},{5,7},{6,4},{7,5},{8,10},{9,11},{10,... | collective-permute-start | bytes 196616 | tf_op jit(solution)/shard_map/ppermute | solution.py:338
  3.0 1.9 %collective-permute-start = (bf16[128,256]{1,0:T(8,128)(2,1)S(1)}, bf16[128,256]{1,0:T(8,128)(2,1)S(1)}, u32[]{:S(2)}, u32[]{:S(2)}) collective-permute-start(bf16[128,256]{1,0:T(8,128)(2,1)S(1)} %pad_maximum_fusion.1), channel_id=1, source_target_pairs={{0,1},{1,0},{2,3},{3,2},{4,5},{5,4},{6,7},{7,6},{8,9},{9,8},{10,11... | collective-permute-start | bytes 196616 | tf_op jit(solution)/shard_map/ppermute | solution.py:338
  4.1 4.1 %collective-permute-start.5 = (bf16[128,256]{1,0:T(8,128)(2,1)S(1)}, bf16[128,256]{1,0:T(8,128)(2,1)S(1)}, u32[]{:S(2)}, u32[]{:S(2)}) collective-permute-start(bf16[128,256]{1,0:T(8,128)(2,1)S(1)} %pad_maximum_fusion.3), channel_id=1, source_target_pairs={{0,3},{1,2},{2,1},{3,0},{4,7},{5,6},{6,5},{7,4},{8,11},{9,10},{10,... | collective-permute-start | bytes 196616 | tf_op jit(solution)/shard_map/ppermute | solution.py:338
  5.0 8.8 %collective-permute-start.1 = (bf16[256,256]{1,0:T(8,128)(2,1)S(1)}, bf16[256,256]{1,0:T(8,128)(2,1)S(1)}, u32[]{:S(2)}, u32[]{:S(2)}) collective-permute-start(bf16[256,256]{1,0:T(8,128)(2,1)S(1)} %pad_maximum_fusion.refs_0_), channel_id=1, source_target_pairs={{0,4},{1,5},{2,6},{3,7},{4,8},{5,9},{6,10},{7,11},{8,12},{9,13},{1... | collective-permute-start | bytes 393224 | tf_op jit(solution)/shard_map/ppermute | solution.py:360
  8.2 8.0 %collective-permute-start.6 = (bf16[256,256]{1,0:T(8,128)(2,1)S(1)}, bf16[256,256]{1,0:T(8,128)(2,1)S(1)}, u32[]{:S(2)}, u32[]{:S(2)}) collective-permute-start(bf16[256,256]{1,0:T(8,128)(2,1)S(1)} %constant_dynamic-update-slice_fusion.refs_1_), channel_id=1, source_target_pairs={{0,4},{1,5},{2,6},{3,7},{4,8},{5,9},{6,10},{7,11},{8,12},{9,13},{1... | collective-permute-start | bytes 393224 | tf_op jit(solution)/shard_map/ppermute | solution.py:360
  11.4 6.8 %collective-permute-start.11 = (bf16[128,640]{1,0:T(8,128)(2,1)S(1)}, bf16[128,640]{1,0:T(8,128)(2,1)S(1)}, u32[]{:S(2)}, u32[]{:S(2)}) collective-permute-start(bf16[128,640]{1,0:T(8,128)(2,1)S(1)} %get-tuple-element.71), channel_id=1, source_target_pairs={{0,3},{1,2},{2,1},{3,0},{4,7},{5,6},{6,5},{7,4},{8,11},{9,10},{10,... | collective-permute-start | bytes 491528 | tf_op jit(solution)/shard_map/ppermute | solution.py:338
  13.1 7.4 %collective-permute-start.9 = (bf16[128,640]{1,0:T(8,128)(2,1)S(1)}, bf16[128,640]{1,0:T(8,128)(2,1)S(1)}, u32[]{:S(2)}, u32[]{:S(2)}) collective-permute-start(bf16[128,640]{1,0:T(8,128)(2,1)S(1)} %get-tuple-element.72), channel_id=1, source_target_pairs={{0,1},{1,0},{2,3},{3,2},{4,5},{5,4},{6,7},{7,6},{8,9},{9,8},{10,11... | collective-permute-start | bytes 491528 | tf_op jit(solution)/shard_map/ppermute | solution.py:338
  13.1 8.5 %collective-permute-start.10 = (bf16[128,640]{1,0:T(8,128)(2,1)S(1)}, bf16[128,640]{1,0:T(8,128)(2,1)S(1)}, u32[]{:S(2)}, u32[]{:S(2)}) collective-permute-start(bf16[128,640]{1,0:T(8,128)(2,1)S(1)} %get-tuple-element.74), channel_id=1, source_target_pairs={{0,2},{1,3},{2,0},{3,1},{4,6},{5,7},{6,4},{7,5},{8,10},{9,11},{10,... | collective-permute-start | bytes 491528 | tf_op jit(solution)/shard_map/ppermute | solution.py:338
  13.8 8.4 %collective-permute-start.2 = (bf16[256,256]{1,0:T(8,128)(2,1)S(1)}, bf16[256,256]{1,0:T(8,128)(2,1)S(1)}, u32[]{:S(2)}, u32[]{:S(2)}) collective-permute-start(bf16[256,256]{1,0:T(8,128)(2,1)S(1)} %collective-permute-done.1.refs_0_), channel_id=1, source_target_pairs={{4,8},{5,9},{6,10},{7,11},{8,12},{9,13},{10,14},{11,15},{20,24},{2... | collective-permute-start | bytes 393224 | tf_op jit(solution)/shard_map/ppermute | solution.py:360
  16.2 6.6 %collective-permute-start.7 = (bf16[256,256]{1,0:T(8,128)(2,1)S(1)}, bf16[256,256]{1,0:T(8,128)(2,1)S(1)}, u32[]{:S(2)}, u32[]{:S(2)}) collective-permute-start(bf16[256,256]{1,0:T(8,128)(2,1)S(1)} %collective-permute-done.6.refs_1_), channel_id=1, source_target_pairs={{4,8},{5,9},{6,10},{7,11},{8,12},{9,13},{10,14},{11,15},{20,24},{2... | collective-permute-start | bytes 393224 | tf_op jit(solution)/shard_map/ppermute | solution.py:360
  18.2 10.4 %collective-permute-start.14 = (bf16[128,640]{1,0:T(8,128)(2,1)S(1)}, bf16[128,640]{1,0:T(8,128)(2,1)S(1)}, u32[]{:S(2)}, u32[]{:S(2)}) collective-permute-start(bf16[128,640]{1,0:T(8,128)(2,1)S(1)} %get-tuple-element.67), channel_id=1, source_target_pairs={{0,3},{1,2},{2,1},{3,0},{4,7},{5,6},{6,5},{7,4},{8,11},{9,10},{10,... | collective-permute-start | bytes 491528 | tf_op jit(solution)/shard_map/ppermute | solution.py:338
  20.4 8.2 %collective-permute-start.12 = (bf16[128,640]{1,0:T(8,128)(2,1)S(1)}, bf16[128,640]{1,0:T(8,128)(2,1)S(1)}, u32[]{:S(2)}, u32[]{:S(2)}) collective-permute-start(bf16[128,640]{1,0:T(8,128)(2,1)S(1)} %get-tuple-element.68), channel_id=1, source_target_pairs={{0,1},{1,0},{2,3},{3,2},{4,5},{5,4},{6,7},{7,6},{8,9},{9,8},{10,11... | collective-permute-start | bytes 491528 | tf_op jit(solution)/shard_map/ppermute | solution.py:338
  21.6 7.1 %collective-permute-start.13 = (bf16[128,640]{1,0:T(8,128)(2,1)S(1)}, bf16[128,640]{1,0:T(8,128)(2,1)S(1)}, u32[]{:S(2)}, u32[]{:S(2)}) collective-permute-start(bf16[128,640]{1,0:T(8,128)(2,1)S(1)} %get-tuple-element.70), channel_id=1, source_target_pairs={{0,2},{1,3},{2,0},{3,1},{4,6},{5,7},{6,4},{7,5},{8,10},{9,11},{10,... | collective-permute-start | bytes 491528 | tf_op jit(solution)/shard_map/ppermute | solution.py:338
  22.2 7.5 %collective-permute-start.3 = (bf16[256,256]{1,0:T(8,128)(2,1)S(1)}, bf16[256,256]{1,0:T(8,128)(2,1)S(1)}, u32[]{:S(2)}, u32[]{:S(2)}) collective-permute-start(bf16[256,256]{1,0:T(8,128)(2,1)S(1)} %collective-permute-done.2.refs_0_), channel_id=1, source_target_pairs={{8,12},{9,13},{10,14},{11,15},{24,28},{25,29},{26,30},{27,31}} | collective-permute-start | bytes 393224 | tf_op jit(solution)/shard_map/ppermute | solution.py:360
  22.8 6.8 %collective-permute-start.8 = (bf16[256,256]{1,0:T(8,128)(2,1)S(1)}, bf16[256,256]{1,0:T(8,128)(2,1)S(1)}, u32[]{:S(2)}, u32[]{:S(2)}) collective-permute-start(bf16[256,256]{1,0:T(8,128)(2,1)S(1)} %collective-permute-done.7.refs_1_), channel_id=1, source_target_pairs={{8,12},{9,13},{10,14},{11,15},{24,28},{25,29},{26,30},{27,31}} | collective-permute-start | bytes 393224 | tf_op jit(solution)/shard_map/ppermute | solution.py:360
  30.2 15.6 %collective-permute-start.15 = (bf16[512,256]{1,0:T(8,128)(2,1)S(1)}, bf16[512,256]{1,0:T(8,128)(2,1)S(1)}, u32[]{:S(2)}, u32[]{:S(2)}) collective-permute-start(bf16[512,256]{1,0:T(8,128)(2,1)S(1)} %get-tuple-element.42), channel_id=1, source_target_pairs={{8,0},{9,1},{10,2},{11,3},{24,16},{25,17},{26,18},{27,19}} | collective-permute-start | bytes 786440 | tf_op jit(solution)/shard_map/ppermute | solution.py:392
  34.9 20.9 %collective-permute-start.16 = (bf16[512,256]{1,0:T(8,128)(2,1)S(1)}, bf16[512,256]{1,0:T(8,128)(2,1)S(1)}, u32[]{:S(2)}, u32[]{:S(2)}) collective-permute-start(bf16[512,256]{1,0:T(8,128)(2,1)S(1)} %get-tuple-element.44), channel_id=1, source_target_pairs={{4,0},{5,1},{6,2},{7,3},{8,4},{9,5},{10,6},{11,7},{20,16},{21,17},... | collective-permute-start | bytes 786440 | tf_op jit(solution)/shard_map/ppermute | solution.py:392
  41.8 17.5 %collective-permute-start.17 = (bf16[512,256]{1,0:T(8,128)(2,1)S(1)}, bf16[512,256]{1,0:T(8,128)(2,1)S(1)}, u32[]{:S(2)}, u32[]{:S(2)}) collective-permute-start(bf16[512,256]{1,0:T(8,128)(2,1)S(1)} %get-tuple-element.60), channel_id=1, source_target_pairs={{12,0},{13,1},{14,2},{15,3},{28,16},{29,17},{30,18},{31,19}} | collective-permute-start | bytes 786440 | tf_op jit(solution)/shard_map/ppermute | solution.py:392
  43.9 15.5 %collective-permute-start.22 = (bf16[512,256]{1,0:T(8,128)(2,1)S(1)}, bf16[512,256]{1,0:T(8,128)(2,1)S(1)}, u32[]{:S(2)}, u32[]{:S(2)}) collective-permute-start(bf16[512,256]{1,0:T(8,128)(2,1)S(1)} %get-tuple-element.66), channel_id=1, source_target_pairs={{12,8},{13,9},{14,10},{15,11},{28,24},{29,25},{30,26},{31,27}} | collective-permute-start | bytes 786440 | tf_op jit(solution)/shard_map/ppermute | solution.py:392
  44.5 19.5 %collective-permute-start.21 = (bf16[512,256]{1,0:T(8,128)(2,1)S(1)}, bf16[512,256]{1,0:T(8,128)(2,1)S(1)}, u32[]{:S(2)}, u32[]{:S(2)}) collective-permute-start(bf16[512,256]{1,0:T(8,128)(2,1)S(1)} %get-tuple-element.65), channel_id=1, source_target_pairs={{12,4},{13,5},{14,6},{15,7},{28,20},{29,21},{30,22},{31,23}} | collective-permute-start | bytes 786440 | tf_op jit(solution)/shard_map/ppermute | solution.py:392
  56.5 15.6 %collective-permute-start.19 = (bf16[128,640]{1,0:T(8,128)(2,1)S(1)}, bf16[128,640]{1,0:T(8,128)(2,1)S(1)}, u32[]{:S(2)}, u32[]{:S(2)}) collective-permute-start(bf16[128,640]{1,0:T(8,128)(2,1)S(1)} %get-tuple-element.62), channel_id=1, source_target_pairs={{0,2},{1,3},{2,0},{3,1},{4,6},{5,7},{6,4},{7,5},{8,10},{9,11},{10,... | collective-permute-start | bytes 491528 | tf_op jit(solution)/shard_map/ppermute | solution.py:338
  57.3 14.8 %collective-permute-start.20 = (bf16[128,640]{1,0:T(8,128)(2,1)S(1)}, bf16[128,640]{1,0:T(8,128)(2,1)S(1)}, u32[]{:S(2)}, u32[]{:S(2)}) collective-permute-start(bf16[128,640]{1,0:T(8,128)(2,1)S(1)} %get-tuple-element.63), channel_id=1, source_target_pairs={{0,3},{1,2},{2,1},{3,0},{4,7},{5,6},{6,5},{7,4},{8,11},{9,10},{10,... | collective-permute-start | bytes 491528 | tf_op jit(solution)/shard_map/ppermute | solution.py:338
  59.4 12.7 %collective-permute-start.18 = (bf16[128,640]{1,0:T(8,128)(2,1)S(1)}, bf16[128,640]{1,0:T(8,128)(2,1)S(1)}, u32[]{:S(2)}, u32[]{:S(2)}) collective-permute-start(bf16[128,640]{1,0:T(8,128)(2,1)S(1)} %get-tuple-element.61), channel_id=1, source_target_pairs={{0,1},{1,0},{2,3},{3,2},{4,5},{5,4},{6,7},{7,6},{8,9},{9,8},{10,11... | collective-permute-start | bytes 491528 | tf_op jit(solution)/shard_map/ppermute | solution.py:338
  64.2 5.8 %collective-permute-start.25 = (bf16[128,256]{1,0:T(8,128)(2,1)S(1)}, bf16[128,256]{1,0:T(8,128)(2,1)S(1)}, u32[]{:S(2)}, u32[]{:S(2)}) collective-permute-start(bf16[128,256]{1,0:T(8,128)(2,1)S(1)} %get-tuple-element.75), channel_id=1, source_target_pairs={{0,3},{1,2},{2,1},{3,0},{4,7},{5,6},{6,5},{7,4},{8,11},{9,10},{10,... | collective-permute-start | bytes 196616 | tf_op jit(solution)/shard_map/ppermute | solution.py:338
  67.6 4.1 %collective-permute-start.24 = (bf16[128,256]{1,0:T(8,128)(2,1)S(1)}, bf16[128,256]{1,0:T(8,128)(2,1)S(1)}, u32[]{:S(2)}, u32[]{:S(2)}) collective-permute-start(bf16[128,256]{1,0:T(8,128)(2,1)S(1)} %get-tuple-element.76), channel_id=1, source_target_pairs={{0,2},{1,3},{2,0},{3,1},{4,6},{5,7},{6,4},{7,5},{8,10},{9,11},{10,... | collective-permute-start | bytes 196616 | tf_op jit(solution)/shard_map/ppermute | solution.py:338
  70.1 2.0 %collective-permute-start.23 = (bf16[128,256]{1,0:T(8,128)(2,1)S(1)}, bf16[128,256]{1,0:T(8,128)(2,1)S(1)}, u32[]{:S(2)}, u32[]{:S(2)}) collective-permute-start(bf16[128,256]{1,0:T(8,128)(2,1)S(1)} %get-tuple-element.77), channel_id=1, source_target_pairs={{0,1},{1,0},{2,3},{3,2},{4,5},{5,4},{6,7},{7,6},{8,9},{9,8},{10,11... | collective-permute-start | bytes 196616 | tf_op jit(solution)/shard_map/ppermute | solution.py:338

commit v6 on v5

--- a/solution.py
+++ b/solution.py
@@ -237,20 +237,25 @@
         pl.when((plane >= offset) & (plane < planes - 1))(work)
 
 
-def local_call(kernel, shapes, flops, info, *operands, scratch=()):
+def local_call(kernel, shapes, flops, *operands, scratch=()):
     vmem = pl.BlockSpec(memory_space=pltpu.VMEM)
+
+    def placed(*refs):
+        device = lax.axis_index("seq")
+        kernel((lax.div(device, KVH), lax.rem(device, KVH)), *refs)
+
     return pl.pallas_call(
-        kernel,
-        in_specs=[pl.BlockSpec(memory_space=pltpu.SMEM)] + [vmem] * len(operands),
+        placed,
+        in_specs=[vmem] * len(operands),
         out_specs=[vmem] * len(shapes),
         out_shape=shapes,
         scratch_shapes=scratch,
         compiler_params=pltpu.CompilerParams(vmem_limit_bytes=VMEM_BYTES),
         cost_estimate=pl.CostEstimate(flops=flops // 10, bytes_accessed=0, transcendentals=0),
-    )(info, *operands)
-
-
-def forward_call(offset, planes, info, kv, q, g, state):
+    )(*operands)
+
+
+def forward_call(offset, planes, kv, q, g, state):
     tokens = q[0].shape[0]
     span = KVH * tokens
     stats = jax.ShapeDtypeStruct((QPG, 8, span), jnp.float32)
@@ -263,7 +268,6 @@
         partial(forward_kernel, offset, planes),
         shapes,
         2 * 2 * QPG * span * span * DH * 2,
-        info,
         *kv,
         *q,
         *(g if closes else []),
@@ -272,7 +276,7 @@
     )
 
 
-def backward_call(offset, planes, top_plane, info, kv, q, g, finals, dq_old, passed):
+def backward_call(offset, planes, top_plane, kv, q, g, finals, dq_old, passed):
     tokens = q[0].shape[0]
     span = KVH * tokens
     first = dq_old is None
@@ -290,7 +294,6 @@
         partial(backward_kernel, offset, planes, top_plane, first),
         shapes,
         5 * 2 * QPG * span * span * DH * 2,
-        info,
         *kv,
         *q,
         *g,
@@ -314,14 +317,14 @@
         value_grad[:, narrow] = sources[KVH + d][:, DH:]
 
 
-def place_call(info, dq, dkv):
+def place_call(dq, dkv):
     tokens = dq[0].shape[0]
     shapes = [
         jax.ShapeDtypeStruct((tokens, KVH * QPG * DH), jnp.bfloat16),
         jax.ShapeDtypeStruct((tokens, KVH * DH), jnp.bfloat16),
         jax.ShapeDtypeStruct((tokens, KVH * DH), jnp.bfloat16),
     ]
-    return local_call(place_kernel, shapes, 0, info, *dq, *dkv)
+    return local_call(place_kernel, shapes, 0, *dq, *dkv)
 
 
 def per_device(queries, keys, values, out_grad):
@@ -330,7 +333,6 @@
     tokens = queries.shape[0]
     device = lax.axis_index("seq")
     rank = device % KVH
-    info = jnp.stack([device // KVH, rank]).astype(jnp.int32)
 
     def swap(array, d):
         if d == 0:
@@ -360,7 +362,7 @@
         chain.append(tuple(lax.ppermute(half, "seq", pairs) for half in chain[-1]))
     state = []
     for offset in range(planes - 1):
-        state = forward_call(offset, planes, info, chain[offset], q, g, state)
+        state = forward_call(offset, planes, chain[offset], q, g, state)
     finals, state = state[0], state[1:]
     arrived = []
 
@@ -377,7 +379,6 @@
                 offset,
                 planes,
                 top_plane,
-                info,
                 kv,
                 q,
                 g,
@@ -394,7 +395,7 @@
 
     lower = gradients(False, finals, [])
     top_kv = (after(chain[-1][0], lower[1]), chain[-1][1])
-    finals = forward_call(planes - 1, planes, info, top_kv, q, g, state)[0]
+    finals = forward_call(planes - 1, planes, top_kv, q, g, state)[0]
     results = gradients(True, finals, lower)
     total, dq = results[0], results[1:]
     for part in arrived:
@@ -403,7 +404,7 @@
     dq = [dq[0], after(dq[1], arrived[planes - 2])] + list(dq[2:])
     dq_back = [swap(dq[d], d) for d in range(KVH)]
     dkv_back = [swap(total[d * tokens : (d + 1) * tokens], d) for d in range(KVH)]
-    return tuple(place_call(info, dq_back, dkv_back))
+    return tuple(place_call(dq_back, dkv_back))
 
 
 def solution(mesh):

time: 74 us -> 69.2 us (0.935)
  Pallas kernels: 18.9 us -> 12.4 us
  starting transfers between devices: 33.2 us -> 34.4 us
    pallas_call x12, Pallas kernels: 18.9 us -> 12.4 us  [local_call(): pl.pallas_call(placed, in_specs=[vmem] * len(operands), out_specs=[vmem]...]
    ppermute x15, waiting for transfers between devices: 4.41 us -> 7.3 us  [swap(): return lax.ppermute(array, 'seq', [(i, i ^ d) for i in range(devices)])]
    ppermute x5, waiting for transfers between devices: 14.6 us -> 11.8 us  [gradients(): arrived.append(lax.ppermute(results[0], 'seq', pairs))]
    ppermute x15, starting transfers between devices: 15.9 us -> 17.1 us  [swap(): return lax.ppermute(array, 'seq', [(i, i ^ d) for i in range(devices)])]
  transfers between devices with their start and end apart: 26 -> 26, of which waited for: 8 -> 8; matrix products, arithmetic and copies ran while one was open for 1% -> 1% of each run, Pallas kernels for 23% -> 17%
where the time goes in v6:
time: 69.2 us; the launch traced here: 68.4 us
  starting transfers between devices  34.4 us (50%)
  waiting for transfers between devices  19.1 us (28%)
  Pallas kernels  12.4 us (18%)
  local copies, waits for them, and re-layouts  1.17 us (2%)
  between operations  1.02 us (1%)
    ppermute x15, starting transfers between devices, swap(): return lax.ppermute(array, 'seq', [(i, i ^ d) for i in range(devices)])  17.1 us
    pallas_call x12, Pallas kernels, local_call(): pl.pallas_call(placed, in_specs=[vmem] * len(operands), out_specs=[vmem]...  12.4 us
    ppermute x6, starting transfers between devices, per_device(): lax.ppermute(half, 'seq', pairs)  12.1 us
    ppermute x5, waiting for transfers between devices, gradients(): arrived.append(lax.ppermute(results[0], 'seq', pairs))  11.8 us
    ppermute x15, waiting for transfers between devices, swap(): return lax.ppermute(array, 'seq', [(i, i ^ d) for i in range(devices)])  7.3 us
    ppermute x5, starting transfers between devices, gradients(): arrived.append(lax.ppermute(results[0], 'seq', pairs))  5.24 us
  transfers between devices with their start and end apart: 26, of which 8 were waited for; matrix products, arithmetic and copies ran while one was open for 1% of the time, Pallas kernels for 17%

profile of v6, /device:TPU:9, one launch (start us, length us, event | category | flops | bytes accessed | tf_op | source)
XLA Modules:
  0.0 68.4 jit_solution(2093985809945877928)
XLA Ops:
  0.7 1.0 %constant_dynamic-slice_fusion.4 = (bf16[128,128]{1,0:T(8,128)(2,1)S(1)}, bf16[128,128]{1,0:T(8,128)(2,1)S(1)}, bf16[128,128]{1,0:T(8,128)(2,1)S(1)}, bf16[128,1...) fusion(bf16[128,512]{1,0:T(8,128)(2,1)} %param.6, ...), kind=kLoop, calls=%fused_computation.11 | loop fusion | bytes 524304 | tf_op jit(solution)/shard_map/dynamic_slice | solution.py:343
  1.7 1.3 %collective-permute-start.4 = (bf16[128,256]{1,0:T(8,128)(2,1)S(1)}, bf16[128,256]{1,0:T(8,128)(2,1)S(1)}, u32[]{:S(2)}, u32[]{:S(2)}) collective-permute-start(bf16[128,256]{1,0:T(8,128)(2,1)S(1)} %pad_maximum_fusion.2), channel_id=1, source_target_pairs={{0,2},{1,3},{2,0},{3,1},{4,6},{5,7},{6,4},{7,5},{8,10},{9,11},{10,... | collective-permute-start | bytes 196616 | tf_op jit(solution)/shard_map/ppermute | solution.py:340
  3.0 1.0 %collective-permute-start = (bf16[128,256]{1,0:T(8,128)(2,1)S(1)}, bf16[128,256]{1,0:T(8,128)(2,1)S(1)}, u32[]{:S(2)}, u32[]{:S(2)}) collective-permute-start(bf16[128,256]{1,0:T(8,128)(2,1)S(1)} %pad_maximum_fusion.1), channel_id=1, source_target_pairs={{0,1},{1,0},{2,3},{3,2},{4,5},{5,4},{6,7},{7,6},{8,9},{9,8},{10,11... | collective-permute-start | bytes 196616 | tf_op jit(solution)/shard_map/ppermute | solution.py:340
  4.1 0.2 collective-permute-start.5
  4.3 0.1 constant_dynamic-slice_fusion.6
  4.3 0.6 collective-permute-done
  5.0 3.2 %collective-permute-start.1 = (bf16[256,256]{1,0:T(8,128)(2,1)S(1)}, bf16[256,256]{1,0:T(8,128)(2,1)S(1)}, u32[]{:S(2)}, u32[]{:S(2)}) collective-permute-start(bf16[256,256]{1,0:T(8,128)(2,1)S(1)} %pad_maximum_fusion.refs_0_), channel_id=1, source_target_pairs={{0,4},{1,5},{2,6},{3,7},{4,8},{5,9},{6,10},{7,11},{8,12},{9,13},{1... | collective-permute-start | bytes 393224 | tf_op jit(solution)/shard_map/ppermute | solution.py:362
  8.2 0.0 collective-permute-done.4
  8.2 0.0 collective-permute-done.5
  8.2 3.2 %collective-permute-start.6 = (bf16[256,256]{1,0:T(8,128)(2,1)S(1)}, bf16[256,256]{1,0:T(8,128)(2,1)S(1)}, u32[]{:S(2)}, u32[]{:S(2)}) collective-permute-start(bf16[256,256]{1,0:T(8,128)(2,1)S(1)} %constant_dynamic-update-slice_fusion.refs_1_), channel_id=1, source_target_pairs={{0,4},{1,5},{2,6},{3,7},{4,8},{5,9},{6,10},{7,11},{8,12},{9,13},{1... | collective-permute-start | bytes 393224 | tf_op jit(solution)/shard_map/ppermute | solution.py:362
  11.4 1.6 %collective-permute-start.11 = (bf16[128,640]{1,0:T(8,128)(2,1)S(1)}, bf16[128,640]{1,0:T(8,128)(2,1)S(1)}, u32[]{:S(2)}, u32[]{:S(2)}) collective-permute-start(bf16[128,640]{1,0:T(8,128)(2,1)S(1)} %get-tuple-element.71), channel_id=1, source_target_pairs={{0,3},{1,2},{2,1},{3,0},{4,7},{5,6},{6,5},{7,4},{8,11},{9,10},{10,... | collective-permute-start | bytes 491528 | tf_op jit(solution)/shard_map/ppermute | solution.py:340
  13.1 0.0 collective-permute-start.9
  13.1 0.7 %collective-permute-start.10 = (bf16[128,640]{1,0:T(8,128)(2,1)S(1)}, bf16[128,640]{1,0:T(8,128)(2,1)S(1)}, u32[]{:S(2)}, u32[]{:S(2)}) collective-permute-start(bf16[128,640]{1,0:T(8,128)(2,1)S(1)} %get-tuple-element.74), channel_id=1, source_target_pairs={{0,2},{1,3},{2,0},{3,1},{4,6},{5,7},{6,4},{7,5},{8,10},{9,11},{10,... | collective-permute-start | bytes 491528 | tf_op jit(solution)/shard_map/ppermute | solution.py:340
  13.8 0.0 collective-permute-done.1.refs_0_
  13.8 2.4 %collective-permute-start.2 = (bf16[256,256]{1,0:T(8,128)(2,1)S(1)}, bf16[256,256]{1,0:T(8,128)(2,1)S(1)}, u32[]{:S(2)}, u32[]{:S(2)}) collective-permute-start(bf16[256,256]{1,0:T(8,128)(2,1)S(1)} %collective-permute-done.1.refs_0_), channel_id=1, source_target_pairs={{4,8},{5,9},{6,10},{7,11},{8,12},{9,13},{10,14},{11,15},{20,24},{2... | collective-permute-start | bytes 393224 | tf_op jit(solution)/shard_map/ppermute | solution.py:362
  16.2 0.0 collective-permute-done.6.refs_1_
  16.2 1.9 %collective-permute-start.7 = (bf16[256,256]{1,0:T(8,128)(2,1)S(1)}, bf16[256,256]{1,0:T(8,128)(2,1)S(1)}, u32[]{:S(2)}, u32[]{:S(2)}) collective-permute-start(bf16[256,256]{1,0:T(8,128)(2,1)S(1)} %collective-permute-done.6.refs_1_), channel_id=1, source_target_pairs={{4,8},{5,9},{6,10},{7,11},{8,12},{9,13},{10,14},{11,15},{20,24},{2... | collective-permute-start | bytes 393224 | tf_op jit(solution)/shard_map/ppermute | solution.py:362
  18.1 0.1 constant_dynamic-slice_fusion
  18.2 0.0 collective-permute-done.11.refs_5_
  18.2 2.2 %collective-permute-start.14 = (bf16[128,640]{1,0:T(8,128)(2,1)S(1)}, bf16[128,640]{1,0:T(8,128)(2,1)S(1)}, u32[]{:S(2)}, u32[]{:S(2)}) collective-permute-start(bf16[128,640]{1,0:T(8,128)(2,1)S(1)} %get-tuple-element.67), channel_id=1, source_target_pairs={{0,3},{1,2},{2,1},{3,0},{4,7},{5,6},{6,5},{7,4},{8,11},{9,10},{10,... | collective-permute-start | bytes 491528 | tf_op jit(solution)/shard_map/ppermute | solution.py:340
  20.4 0.0 collective-permute-done.9.refs_3_
  20.4 0.0 collective-permute-start.12
  20.4 1.1 %collective-permute-done.10.refs_4_ = bf16[128,640]{1,0:T(8,128)(2,1)S(1)} collective-permute-done((bf16[128,640]{1,0:T(8,128)(2,1)S(1)}, bf16[128,640]{1,0:T(8,128)(2,1)S(1)}, u32[]{:S(2)}, u32[]{:S(2)}) %collective-permute-start.10) | collective-permute-done | bytes 163872 | tf_op jit(solution)/shard_map/ppermute | solution.py:340
  21.6 0.6 collective-permute-start.13
  22.2 0.0 collective-permute-done.2.refs_0_
  22.2 0.7 collective-permute-start.3
  22.8 0.0 collective-permute-done.7.refs_1_
  22.8 0.7 collective-permute-start.8
  23.5 2.0 %shard_map.67 = (f32[5,8,512]{2,1,0:T(8,128)S(1)}, f32[5,136,512]{2,1,0:T(8,128)S(1)}) custom-call(bf16[256,256]{1,0:T(8,128)(2,1)S(1)} %pad_maximum_fusion.refs_0_, bf16[256,256]{1,0:T(8,128)(2,1)S(1)} %constant_dynamic-update-slice_fusion.refs_1_, bf16[128,640]{1,0:T(8,128)(2,1)S(1)} %get-tuple-element.73.refs_2_, ...), custom_call_target="tpu_custom_call" | custom-call | flops 134217728 | tf_op jit(solution)/shard_map/pallas_call | solution.py:247
  25.5 1.9 %shard_map.68 = (f32[5,8,512]{2,1,0:T(8,128)S(1)}, f32[5,136,512]{2,1,0:T(8,128)S(1)}) custom-call(bf16[256,256]{1,0:T(8,128)(2,1)S(1)} %collective-permute-done.1.refs_0_, bf16[256,256]{1,0:T(8,128)(2,1)S(1)} %collective-permute-done.6.refs_1_, bf16[128,640]{1,0:T(8,128)(2,1)S(1)} %get-tuple-element.73.refs_2_, ...), custom_call_target="tpu_custom_call" | custom-call | flops 134217728 | tf_op jit(solution)/shard_map/pallas_call | solution.py:247
  27.4 0.0 collective-permute-done.14.refs_9_
  27.4 0.0 collective-permute-done.12.refs_7_
  27.4 1.3 %collective-permute-done.13.refs_8_ = bf16[128,640]{1,0:T(8,128)(2,1)S(1)} collective-permute-done((bf16[128,640]{1,0:T(8,128)(2,1)S(1)}, bf16[128,640]{1,0:T(8,128)(2,1)S(1)}, u32[]{:S(2)}, u32[]{:S(2)}) %collective-permute-start.13) | collective-permute-done | bytes 163872 | tf_op jit(solution)/shard_map/ppermute | solution.py:340
  28.7 0.3 shard_map.69
  29.1 0.0 collective-permute-done.3.refs_0_
  29.1 0.0 collective-permute-done.8.refs_1_
  29.1 0.7 collective-permute-start.15
  29.8 3.4 %shard_map.71 = (bf16[512,256]{1,0:T(8,128)(2,1)S(1)}, f32[5,128,512]{2,1,0:T(8,128)S(1)}) custom-call(bf16[256,256]{1,0:T(8,128)(2,1)S(1)} %collective-permute-done.1.refs_0_, bf16[256,256]{1,0:T(8,128)(2,1)S(1)} %collective-permute-done.6.refs_1_, bf16[128,640]{1,0:T(8,128)(2,1)S(1)} %get-tuple-element.73.refs_2_, ...), custom_call_target="tpu_custom_call" | custom-call | flops 335544320 | tf_op jit(solution)/shard_map/pallas_call | solution.py:247
  33.2 1.9 %collective-permute-start.16 = (bf16[512,256]{1,0:T(8,128)(2,1)S(1)}, bf16[512,256]{1,0:T(8,128)(2,1)S(1)}, u32[]{:S(2)}, u32[]{:S(2)}) collective-permute-start(bf16[512,256]{1,0:T(8,128)(2,1)S(1)} %get-tuple-element.44), channel_id=1, source_target_pairs={{4,0},{5,1},{6,2},{7,3},{8,4},{9,5},{10,6},{11,7},{20,16},{21,17},... | collective-permute-start | bytes 786440 | tf_op jit(solution)/shard_map/ppermute | solution.py:393
  35.2 3.4 %shard_map.72 = (f32[512,256]{1,0:T(8,128)S(1)}, bf16[128,640]{1,0:T(8,128)(2,1)S(1)}, bf16[128,640]{1,0:T(8,128)(2,1)S(1)}, bf16[128,640]{1,0:T(8,128)(2,1)S(1)}, bf16[128,640]{1,0:T(8,128)(2,1)S(1)}) custom-call(bf16[256,256]{1,0:T(8,128)(2,1)S(1)} %pad_maximum_fusion.refs_0_, bf16[256,256]{1,0:T(8,128)(2,1)S(1)} %constant_dynamic-update-slice_fusion.refs_1_, ...), custom_call_target="tpu_custom_call" | custom-call | flops 335544320 | tf_op jit(solution)/shard_map/pallas_call | solution.py:247
  38.6 0.7 collective-permute-start.17
  39.3 0.2 shard_map.75
  39.6 0.7 collective-permute-start.22
  40.3 1.3 %collective-permute-start.21 = (bf16[512,256]{1,0:T(8,128)(2,1)S(1)}, bf16[512,256]{1,0:T(8,128)(2,1)S(1)}, u32[]{:S(2)}, u32[]{:S(2)}) collective-permute-start(bf16[512,256]{1,0:T(8,128)(2,1)S(1)} %get-tuple-element.65), channel_id=1, source_target_pairs={{12,4},{13,5},{14,6},{15,7},{28,20},{29,21},{30,22},{31,23}} | collective-permute-start | bytes 786440 | tf_op jit(solution)/shard_map/ppermute | solution.py:393
  41.6 0.0 collective-permute-done.15
  41.6 10.9 %collective-permute-done.16 = bf16[512,256]{1,0:T(8,128)(2,1)S(1)} collective-permute-done((bf16[512,256]{1,0:T(8,128)(2,1)S(1)}, bf16[512,256]{1,0:T(8,128)(2,1)S(1)}, u32[]{:S(2)}, u32[]{:S(2)}) %collective-permute-start.16) | collective-permute-done | bytes 262176 | tf_op jit(solution)/shard_map/ppermute | solution.py:393
  52.5 0.1 shard_map.77
  52.6 0.8 %collective-permute-start.19 = (bf16[128,640]{1,0:T(8,128)(2,1)S(1)}, bf16[128,640]{1,0:T(8,128)(2,1)S(1)}, u32[]{:S(2)}, u32[]{:S(2)}) collective-permute-start(bf16[128,640]{1,0:T(8,128)(2,1)S(1)} %get-tuple-element.62), channel_id=1, source_target_pairs={{0,2},{1,3},{2,0},{3,1},{4,6},{5,7},{6,4},{7,5},{8,10},{9,11},{10,... | collective-permute-start | bytes 491528 | tf_op jit(solution)/shard_map/ppermute | solution.py:340
  53.4 4.5 %collective-permute-start.20 = (bf16[128,640]{1,0:T(8,128)(2,1)S(1)}, bf16[128,640]{1,0:T(8,128)(2,1)S(1)}, u32[]{:S(2)}, u32[]{:S(2)}) collective-permute-start(bf16[128,640]{1,0:T(8,128)(2,1)S(1)} %get-tuple-element.63), channel_id=1, source_target_pairs={{0,3},{1,2},{2,1},{3,0},{4,7},{5,6},{6,5},{7,4},{8,11},{9,10},{10,... | collective-permute-start | bytes 491528 | tf_op jit(solution)/shard_map/ppermute | solution.py:340
  57.9 0.0 collective-permute-done.17
  57.9 0.0 collective-permute-start.18
  57.9 0.0 collective-permute-done.22
  57.9 0.9 %collective-permute-done.21 = bf16[512,256]{1,0:T(8,128)(2,1)S(1)} collective-permute-done((bf16[512,256]{1,0:T(8,128)(2,1)S(1)}, bf16[512,256]{1,0:T(8,128)(2,1)S(1)}, u32[]{:S(2)}, u32[]{:S(2)}) %collective-permute-start.21) | collective-permute-done | bytes 262176 | tf_op jit(solution)/shard_map/ppermute | solution.py:393
  58.8 0.2 add_convert_fusion
  59.0 3.4 %collective-permute-start.25 = (bf16[128,256]{1,0:T(8,128)(2,1)S(1)}, bf16[128,256]{1,0:T(8,128)(2,1)S(1)}, u32[]{:S(2)}, u32[]{:S(2)}) collective-permute-start(bf16[128,256]{1,0:T(8,128)(2,1)S(1)} %get-tuple-element.75), channel_id=1, source_target_pairs={{0,3},{1,2},{2,1},{3,0},{4,7},{5,6},{6,5},{7,4},{8,11},{9,10},{10,... | collective-permute-start | bytes 196616 | tf_op jit(solution)/shard_map/ppermute | solution.py:340
  62.4 0.6 collective-permute-start.24
  63.0 3.0 %collective-permute-done.25.refs_7_ = bf16[128,256]{1,0:T(8,128)(2,1)S(1)} collective-permute-done((bf16[128,256]{1,0:T(8,128)(2,1)S(1)}, bf16[128,256]{1,0:T(8,128)(2,1)S(1)}, u32[]{:S(2)}, u32[]{:S(2)}) %collective-permute-start.25) | collective-permute-done | bytes 65568 | tf_op jit(solution)/shard_map/ppermute | solution.py:340
  66.1 0.1 collective-permute-start.23
  66.1 1.0 %collective-permute-done.24.refs_6_ = bf16[128,256]{1,0:T(8,128)(2,1)S(1)} collective-permute-done((bf16[128,256]{1,0:T(8,128)(2,1)S(1)}, bf16[128,256]{1,0:T(8,128)(2,1)S(1)}, u32[]{:S(2)}, u32[]{:S(2)}) %collective-permute-start.24) | collective-permute-done | bytes 65568 | tf_op jit(solution)/shard_map/ppermute | solution.py:340
  67.2 0.2 collective-permute-done.23.refs_5_
  67.3 0.0 collective-permute-done.19.refs_2_
  67.3 0.0 collective-permute-done.20.refs_3_
  67.3 0.0 collective-permute-done.18.refs_1_
  67.3 1.0 %shard_map.78 = (bf16[128,2560]{1,0:T(8,128)(2,1)}, bf16[128,512]{1,0:T(8,128)(2,1)}, bf16[128,512]{1,0:T(8,128)(2,1)}) custom-call(bf16[128,640]{1,0:T(8,128)(2,1)S(1)} %get-tuple-element.58.refs_0_, bf16[128,640]{1,0:T(8,128)(2,1)S(1)} %collective-permute-done.18.refs_1_, bf16[128,640]{1,0:T(8,128)(2,1)S(1)} %collective-permute-done.19.refs_2_, ...), custom_call_target="tpu_custom_call" | custom-call | tf_op jit(solution)/shard_map/pallas_call | solution.py:247
  (15 shorter events, 0.2 us)
Async XLA Ops:
  0.6 3.6 %copy-start = (bf16[128,2560]{1,0:T(8,128)(2,1)S(1)}, bf16[128,2560]{1,0:T(8,128)(2,1)}, u32[]{:S(2)}) copy-start(bf16[128,2560]{1,0:T(8,128)(2,1)} %param.4) | copy-start | bytes 1966084
  0.7 17.4 %copy-start.1 = (bf16[128,2560]{1,0:T(8,128)(2,1)S(1)}, bf16[128,2560]{1,0:T(8,128)(2,1)}, u32[]{:S(2)}) copy-start(bf16[128,2560]{1,0:T(8,128)(2,1)} %param.7) | copy-start | bytes 1966084
  1.7 6.5 %collective-permute-start.4 = (bf16[128,256]{1,0:T(8,128)(2,1)S(1)}, bf16[128,256]{1,0:T(8,128)(2,1)S(1)}, u32[]{:S(2)}, u32[]{:S(2)}) collective-permute-start(bf16[128,256]{1,0:T(8,128)(2,1)S(1)} %pad_maximum_fusion.2), channel_id=1, source_target_pairs={{0,2},{1,3},{2,0},{3,1},{4,6},{5,7},{6,4},{7,5},{8,10},{9,11},{10,... | collective-permute-start | bytes 196616 | tf_op jit(solution)/shard_map/ppermute | solution.py:340
  3.0 1.9 %collective-permute-start = (bf16[128,256]{1,0:T(8,128)(2,1)S(1)}, bf16[128,256]{1,0:T(8,128)(2,1)S(1)}, u32[]{:S(2)}, u32[]{:S(2)}) collective-permute-start(bf16[128,256]{1,0:T(8,128)(2,1)S(1)} %pad_maximum_fusion.1), channel_id=1, source_target_pairs={{0,1},{1,0},{2,3},{3,2},{4,5},{5,4},{6,7},{7,6},{8,9},{9,8},{10,11... | collective-permute-start | bytes 196616 | tf_op jit(solution)/shard_map/ppermute | solution.py:340
  4.1 4.1 %collective-permute-start.5 = (bf16[128,256]{1,0:T(8,128)(2,1)S(1)}, bf16[128,256]{1,0:T(8,128)(2,1)S(1)}, u32[]{:S(2)}, u32[]{:S(2)}) collective-permute-start(bf16[128,256]{1,0:T(8,128)(2,1)S(1)} %pad_maximum_fusion.3), channel_id=1, source_target_pairs={{0,3},{1,2},{2,1},{3,0},{4,7},{5,6},{6,5},{7,4},{8,11},{9,10},{10,... | collective-permute-start | bytes 196616 | tf_op jit(solution)/shard_map/ppermute | solution.py:340
  5.0 8.8 %collective-permute-start.1 = (bf16[256,256]{1,0:T(8,128)(2,1)S(1)}, bf16[256,256]{1,0:T(8,128)(2,1)S(1)}, u32[]{:S(2)}, u32[]{:S(2)}) collective-permute-start(bf16[256,256]{1,0:T(8,128)(2,1)S(1)} %pad_maximum_fusion.refs_0_), channel_id=1, source_target_pairs={{0,4},{1,5},{2,6},{3,7},{4,8},{5,9},{6,10},{7,11},{8,12},{9,13},{1... | collective-permute-start | bytes 393224 | tf_op jit(solution)/shard_map/ppermute | solution.py:362
  8.2 8.0 %collective-permute-start.6 = (bf16[256,256]{1,0:T(8,128)(2,1)S(1)}, bf16[256,256]{1,0:T(8,128)(2,1)S(1)}, u32[]{:S(2)}, u32[]{:S(2)}) collective-permute-start(bf16[256,256]{1,0:T(8,128)(2,1)S(1)} %constant_dynamic-update-slice_fusion.refs_1_), channel_id=1, source_target_pairs={{0,4},{1,5},{2,6},{3,7},{4,8},{5,9},{6,10},{7,11},{8,12},{9,13},{1... | collective-permute-start | bytes 393224 | tf_op jit(solution)/shard_map/ppermute | solution.py:362
  11.4 6.8 %collective-permute-start.11 = (bf16[128,640]{1,0:T(8,128)(2,1)S(1)}, bf16[128,640]{1,0:T(8,128)(2,1)S(1)}, u32[]{:S(2)}, u32[]{:S(2)}) collective-permute-start(bf16[128,640]{1,0:T(8,128)(2,1)S(1)} %get-tuple-element.71), channel_id=1, source_target_pairs={{0,3},{1,2},{2,1},{3,0},{4,7},{5,6},{6,5},{7,4},{8,11},{9,10},{10,... | collective-permute-start | bytes 491528 | tf_op jit(solution)/shard_map/ppermute | solution.py:340
  13.1 7.4 %collective-permute-start.9 = (bf16[128,640]{1,0:T(8,128)(2,1)S(1)}, bf16[128,640]{1,0:T(8,128)(2,1)S(1)}, u32[]{:S(2)}, u32[]{:S(2)}) collective-permute-start(bf16[128,640]{1,0:T(8,128)(2,1)S(1)} %get-tuple-element.72), channel_id=1, source_target_pairs={{0,1},{1,0},{2,3},{3,2},{4,5},{5,4},{6,7},{7,6},{8,9},{9,8},{10,11... | collective-permute-start | bytes 491528 | tf_op jit(solution)/shard_map/ppermute | solution.py:340
  13.1 8.5 %collective-permute-start.10 = (bf16[128,640]{1,0:T(8,128)(2,1)S(1)}, bf16[128,640]{1,0:T(8,128)(2,1)S(1)}, u32[]{:S(2)}, u32[]{:S(2)}) collective-permute-start(bf16[128,640]{1,0:T(8,128)(2,1)S(1)} %get-tuple-element.74), channel_id=1, source_target_pairs={{0,2},{1,3},{2,0},{3,1},{4,6},{5,7},{6,4},{7,5},{8,10},{9,11},{10,... | collective-permute-start | bytes 491528 | tf_op jit(solution)/shard_map/ppermute | solution.py:340
  13.8 8.4 %collective-permute-start.2 = (bf16[256,256]{1,0:T(8,128)(2,1)S(1)}, bf16[256,256]{1,0:T(8,128)(2,1)S(1)}, u32[]{:S(2)}, u32[]{:S(2)}) collective-permute-start(bf16[256,256]{1,0:T(8,128)(2,1)S(1)} %collective-permute-done.1.refs_0_), channel_id=1, source_target_pairs={{4,8},{5,9},{6,10},{7,11},{8,12},{9,13},{10,14},{11,15},{20,24},{2... | collective-permute-start | bytes 393224 | tf_op jit(solution)/shard_map/ppermute | solution.py:362
  16.2 6.6 %collective-permute-start.7 = (bf16[256,256]{1,0:T(8,128)(2,1)S(1)}, bf16[256,256]{1,0:T(8,128)(2,1)S(1)}, u32[]{:S(2)}, u32[]{:S(2)}) collective-permute-start(bf16[256,256]{1,0:T(8,128)(2,1)S(1)} %collective-permute-done.6.refs_1_), channel_id=1, source_target_pairs={{4,8},{5,9},{6,10},{7,11},{8,12},{9,13},{10,14},{11,15},{20,24},{2... | collective-permute-start | bytes 393224 | tf_op jit(solution)/shard_map/ppermute | solution.py:362
  18.2 9.2 %collective-permute-start.14 = (bf16[128,640]{1,0:T(8,128)(2,1)S(1)}, bf16[128,640]{1,0:T(8,128)(2,1)S(1)}, u32[]{:S(2)}, u32[]{:S(2)}) collective-permute-start(bf16[128,640]{1,0:T(8,128)(2,1)S(1)} %get-tuple-element.67), channel_id=1, source_target_pairs={{0,3},{1,2},{2,1},{3,0},{4,7},{5,6},{6,5},{7,4},{8,11},{9,10},{10,... | collective-permute-start | bytes 491528 | tf_op jit(solution)/shard_map/ppermute | solution.py:340
  20.4 7.0 %collective-permute-start.12 = (bf16[128,640]{1,0:T(8,128)(2,1)S(1)}, bf16[128,640]{1,0:T(8,128)(2,1)S(1)}, u32[]{:S(2)}, u32[]{:S(2)}) collective-permute-start(bf16[128,640]{1,0:T(8,128)(2,1)S(1)} %get-tuple-element.68), channel_id=1, source_target_pairs={{0,1},{1,0},{2,3},{3,2},{4,5},{5,4},{6,7},{7,6},{8,9},{9,8},{10,11... | collective-permute-start | bytes 491528 | tf_op jit(solution)/shard_map/ppermute | solution.py:340
  21.6 7.1 %collective-permute-start.13 = (bf16[128,640]{1,0:T(8,128)(2,1)S(1)}, bf16[128,640]{1,0:T(8,128)(2,1)S(1)}, u32[]{:S(2)}, u32[]{:S(2)}) collective-permute-start(bf16[128,640]{1,0:T(8,128)(2,1)S(1)} %get-tuple-element.70), channel_id=1, source_target_pairs={{0,2},{1,3},{2,0},{3,1},{4,6},{5,7},{6,4},{7,5},{8,10},{9,11},{10,... | collective-permute-start | bytes 491528 | tf_op jit(solution)/shard_map/ppermute | solution.py:340
  22.2 6.9 %collective-permute-start.3 = (bf16[256,256]{1,0:T(8,128)(2,1)S(1)}, bf16[256,256]{1,0:T(8,128)(2,1)S(1)}, u32[]{:S(2)}, u32[]{:S(2)}) collective-permute-start(bf16[256,256]{1,0:T(8,128)(2,1)S(1)} %collective-permute-done.2.refs_0_), channel_id=1, source_target_pairs={{8,12},{9,13},{10,14},{11,15},{24,28},{25,29},{26,30},{27,31}} | collective-permute-start | bytes 393224 | tf_op jit(solution)/shard_map/ppermute | solution.py:362
  22.8 6.2 %collective-permute-start.8 = (bf16[256,256]{1,0:T(8,128)(2,1)S(1)}, bf16[256,256]{1,0:T(8,128)(2,1)S(1)}, u32[]{:S(2)}, u32[]{:S(2)}) collective-permute-start(bf16[256,256]{1,0:T(8,128)(2,1)S(1)} %collective-permute-done.7.refs_1_), channel_id=1, source_target_pairs={{8,12},{9,13},{10,14},{11,15},{24,28},{25,29},{26,30},{27,31}} | collective-permute-start | bytes 393224 | tf_op jit(solution)/shard_map/ppermute | solution.py:362
  29.1 12.4 %collective-permute-start.15 = (bf16[512,256]{1,0:T(8,128)(2,1)S(1)}, bf16[512,256]{1,0:T(8,128)(2,1)S(1)}, u32[]{:S(2)}, u32[]{:S(2)}) collective-permute-start(bf16[512,256]{1,0:T(8,128)(2,1)S(1)} %get-tuple-element.42), channel_id=1, source_target_pairs={{8,0},{9,1},{10,2},{11,3},{24,16},{25,17},{26,18},{27,19}} | collective-permute-start | bytes 786440 | tf_op jit(solution)/shard_map/ppermute | solution.py:393
  33.2 19.2 %collective-permute-start.16 = (bf16[512,256]{1,0:T(8,128)(2,1)S(1)}, bf16[512,256]{1,0:T(8,128)(2,1)S(1)}, u32[]{:S(2)}, u32[]{:S(2)}) collective-permute-start(bf16[512,256]{1,0:T(8,128)(2,1)S(1)} %get-tuple-element.44), channel_id=1, source_target_pairs={{4,0},{5,1},{6,2},{7,3},{8,4},{9,5},{10,6},{11,7},{20,16},{21,17},... | collective-permute-start | bytes 786440 | tf_op jit(solution)/shard_map/ppermute | solution.py:393
  38.6 19.3 %collective-permute-start.17 = (bf16[512,256]{1,0:T(8,128)(2,1)S(1)}, bf16[512,256]{1,0:T(8,128)(2,1)S(1)}, u32[]{:S(2)}, u32[]{:S(2)}) collective-permute-start(bf16[512,256]{1,0:T(8,128)(2,1)S(1)} %get-tuple-element.60), channel_id=1, source_target_pairs={{12,0},{13,1},{14,2},{15,3},{28,16},{29,17},{30,18},{31,19}} | collective-permute-start | bytes 786440 | tf_op jit(solution)/shard_map/ppermute | solution.py:393
  39.6 18.3 %collective-permute-start.22 = (bf16[512,256]{1,0:T(8,128)(2,1)S(1)}, bf16[512,256]{1,0:T(8,128)(2,1)S(1)}, u32[]{:S(2)}, u32[]{:S(2)}) collective-permute-start(bf16[512,256]{1,0:T(8,128)(2,1)S(1)} %get-tuple-element.66), channel_id=1, source_target_pairs={{12,8},{13,9},{14,10},{15,11},{28,24},{29,25},{30,26},{31,27}} | collective-permute-start | bytes 786440 | tf_op jit(solution)/shard_map/ppermute | solution.py:393
  40.3 18.5 %collective-permute-start.21 = (bf16[512,256]{1,0:T(8,128)(2,1)S(1)}, bf16[512,256]{1,0:T(8,128)(2,1)S(1)}, u32[]{:S(2)}, u32[]{:S(2)}) collective-permute-start(bf16[512,256]{1,0:T(8,128)(2,1)S(1)} %get-tuple-element.65), channel_id=1, source_target_pairs={{12,4},{13,5},{14,6},{15,7},{28,20},{29,21},{30,22},{31,23}} | collective-permute-start | bytes 786440 | tf_op jit(solution)/shard_map/ppermute | solution.py:393
  52.6 14.8 %collective-permute-start.19 = (bf16[128,640]{1,0:T(8,128)(2,1)S(1)}, bf16[128,640]{1,0:T(8,128)(2,1)S(1)}, u32[]{:S(2)}, u32[]{:S(2)}) collective-permute-start(bf16[128,640]{1,0:T(8,128)(2,1)S(1)} %get-tuple-element.62), channel_id=1, source_target_pairs={{0,2},{1,3},{2,0},{3,1},{4,6},{5,7},{6,4},{7,5},{8,10},{9,11},{10,... | collective-permute-start | bytes 491528 | tf_op jit(solution)/shard_map/ppermute | solution.py:340
  53.4 13.9 %collective-permute-start.20 = (bf16[128,640]{1,0:T(8,128)(2,1)S(1)}, bf16[128,640]{1,0:T(8,128)(2,1)S(1)}, u32[]{:S(2)}, u32[]{:S(2)}) collective-permute-start(bf16[128,640]{1,0:T(8,128)(2,1)S(1)} %get-tuple-element.63), channel_id=1, source_target_pairs={{0,3},{1,2},{2,1},{3,0},{4,7},{5,6},{6,5},{7,4},{8,11},{9,10},{10,... | collective-permute-start | bytes 491528 | tf_op jit(solution)/shard_map/ppermute | solution.py:340
  57.9 9.5 %collective-permute-start.18 = (bf16[128,640]{1,0:T(8,128)(2,1)S(1)}, bf16[128,640]{1,0:T(8,128)(2,1)S(1)}, u32[]{:S(2)}, u32[]{:S(2)}) collective-permute-start(bf16[128,640]{1,0:T(8,128)(2,1)S(1)} %get-tuple-element.61), channel_id=1, source_target_pairs={{0,1},{1,0},{2,3},{3,2},{4,5},{5,4},{6,7},{7,6},{8,9},{9,8},{10,11... | collective-permute-start | bytes 491528 | tf_op jit(solution)/shard_map/ppermute | solution.py:340
  59.0 7.1 %collective-permute-start.25 = (bf16[128,256]{1,0:T(8,128)(2,1)S(1)}, bf16[128,256]{1,0:T(8,128)(2,1)S(1)}, u32[]{:S(2)}, u32[]{:S(2)}) collective-permute-start(bf16[128,256]{1,0:T(8,128)(2,1)S(1)} %get-tuple-element.75), channel_id=1, source_target_pairs={{0,3},{1,2},{2,1},{3,0},{4,7},{5,6},{6,5},{7,4},{8,11},{9,10},{10,... | collective-permute-start | bytes 196616 | tf_op jit(solution)/shard_map/ppermute | solution.py:340
  62.4 4.8 %collective-permute-start.24 = (bf16[128,256]{1,0:T(8,128)(2,1)S(1)}, bf16[128,256]{1,0:T(8,128)(2,1)S(1)}, u32[]{:S(2)}, u32[]{:S(2)}) collective-permute-start(bf16[128,256]{1,0:T(8,128)(2,1)S(1)} %get-tuple-element.76), channel_id=1, source_target_pairs={{0,2},{1,3},{2,0},{3,1},{4,6},{5,7},{6,4},{7,5},{8,10},{9,11},{10,... | collective-permute-start | bytes 196616 | tf_op jit(solution)/shard_map/ppermute | solution.py:340
  66.1 1.3 %collective-permute-start.23 = (bf16[128,256]{1,0:T(8,128)(2,1)S(1)}, bf16[128,256]{1,0:T(8,128)(2,1)S(1)}, u32[]{:S(2)}, u32[]{:S(2)}) collective-permute-start(bf16[128,256]{1,0:T(8,128)(2,1)S(1)} %get-tuple-element.77), channel_id=1, source_target_pairs={{0,1},{1,0},{2,3},{3,2},{4,5},{5,4},{6,7},{7,6},{8,9},{9,8},{10,11... | collective-permute-start | bytes 196616 | tf_op jit(solution)/shard_map/ppermute | solution.py:340

commit v7 on v6

--- a/solution.py
+++ b/solution.py
@@ -372,7 +372,7 @@
         for offset in reversed(range(start + 1)):
             kv = chain[offset]
             if top_plane and offset == 0:
-                kv = (after(kv[0], *arrived[: planes - 2]), kv[1])
+                kv = (after(kv[0], arrived[0]), kv[1])
             if offset == planes - 2 and not top_plane:
                 kv = (after(kv[0], *chain[-1]), kv[1])
             results = backward_call(
@@ -401,7 +401,7 @@
     for part in arrived:
         total = total + part.astype(jnp.float32)
     total = total.astype(jnp.bfloat16)
-    dq = [dq[0], after(dq[1], arrived[planes - 2])] + list(dq[2:])
+    dq = [dq[0], after(dq[1], *arrived[1 : planes - 1])] + list(dq[2:])
     dq_back = [swap(dq[d], d) for d in range(KVH)]
     dkv_back = [swap(total[d * tokens : (d + 1) * tokens], d) for d in range(KVH)]
     return tuple(place_call(dq_back, dkv_back))

time: 69.2 us -> 68.3 us (0.987)
    ppermute x15, waiting for transfers between devices: 7.3 us -> 5.95 us  [swap(): return lax.ppermute(array, 'seq', [(i, i ^ d) for i in range(devices)])]
    ppermute x5, waiting for transfers between devices: 11.8 us -> 12.7 us  [gradients(): arrived.append(lax.ppermute(results[0], 'seq', pairs))]
where the time goes in v7:
time: 68.3 us; the launch traced here: 68 us
  starting transfers between devices  34.4 us (50%)
  waiting for transfers between devices  18.7 us (27%)
  Pallas kernels  12.5 us (18%)
  local copies, waits for them, and re-layouts  1.17 us (2%)
  between operations  1.02 us (1%)
    ppermute x15, starting transfers between devices, swap(): return lax.ppermute(array, 'seq', [(i, i ^ d) for i in range(devices)])  17.1 us
    ppermute x5, waiting for transfers between devices, gradients(): arrived.append(lax.ppermute(results[0], 'seq', pairs))  12.7 us
    pallas_call x12, Pallas kernels, local_call(): pl.pallas_call(placed, in_specs=[vmem] * len(operands), out_specs=[vmem]...  12.5 us
    ppermute x6, starting transfers between devices, per_device(): lax.ppermute(half, 'seq', pairs)  12.1 us
    ppermute x15, waiting for transfers between devices, swap(): return lax.ppermute(array, 'seq', [(i, i ^ d) for i in range(devices)])  5.95 us
    ppermute x5, starting transfers between devices, gradients(): arrived.append(lax.ppermute(results[0], 'seq', pairs))  5.24 us
  transfers between devices with their start and end apart: 26, of which 8 were waited for; matrix products, arithmetic and copies ran while one was open for 1% of the time, Pallas kernels for 17%

profile of v7, /device:TPU:9, one launch (start us, length us, event | category | flops | bytes accessed | tf_op | source)
XLA Modules:
  0.0 68.0 jit_solution(9236575279582886642)
XLA Ops:
  0.7 1.0 %constant_dynamic-slice_fusion.4 = (bf16[128,128]{1,0:T(8,128)(2,1)S(1)}, bf16[128,128]{1,0:T(8,128)(2,1)S(1)}, bf16[128,128]{1,0:T(8,128)(2,1)S(1)}, bf16[128,1...) fusion(bf16[128,512]{1,0:T(8,128)(2,1)} %param.6, ...), kind=kLoop, calls=%fused_computation.11 | loop fusion | bytes 524304 | tf_op jit(solution)/shard_map/dynamic_slice | solution.py:343
  1.7 1.3 %collective-permute-start.4 = (bf16[128,256]{1,0:T(8,128)(2,1)S(1)}, bf16[128,256]{1,0:T(8,128)(2,1)S(1)}, u32[]{:S(2)}, u32[]{:S(2)}) collective-permute-start(bf16[128,256]{1,0:T(8,128)(2,1)S(1)} %pad_maximum_fusion.2), channel_id=1, source_target_pairs={{0,2},{1,3},{2,0},{3,1},{4,6},{5,7},{6,4},{7,5},{8,10},{9,11},{10,... | collective-permute-start | bytes 196616 | tf_op jit(solution)/shard_map/ppermute | solution.py:340
  3.0 1.0 %collective-permute-start = (bf16[128,256]{1,0:T(8,128)(2,1)S(1)}, bf16[128,256]{1,0:T(8,128)(2,1)S(1)}, u32[]{:S(2)}, u32[]{:S(2)}) collective-permute-start(bf16[128,256]{1,0:T(8,128)(2,1)S(1)} %pad_maximum_fusion.1), channel_id=1, source_target_pairs={{0,1},{1,0},{2,3},{3,2},{4,5},{5,4},{6,7},{7,6},{8,9},{9,8},{10,11... | collective-permute-start | bytes 196616 | tf_op jit(solution)/shard_map/ppermute | solution.py:340
  4.1 0.2 collective-permute-start.5
  4.3 0.1 constant_dynamic-slice_fusion.6
  4.3 0.6 collective-permute-done
  5.0 3.2 %collective-permute-start.1 = (bf16[256,256]{1,0:T(8,128)(2,1)S(1)}, bf16[256,256]{1,0:T(8,128)(2,1)S(1)}, u32[]{:S(2)}, u32[]{:S(2)}) collective-permute-start(bf16[256,256]{1,0:T(8,128)(2,1)S(1)} %pad_maximum_fusion.refs_0_), channel_id=1, source_target_pairs={{0,4},{1,5},{2,6},{3,7},{4,8},{5,9},{6,10},{7,11},{8,12},{9,13},{1... | collective-permute-start | bytes 393224 | tf_op jit(solution)/shard_map/ppermute | solution.py:362
  8.2 0.0 collective-permute-done.4
  8.2 0.0 collective-permute-done.5
  8.2 3.2 %collective-permute-start.6 = (bf16[256,256]{1,0:T(8,128)(2,1)S(1)}, bf16[256,256]{1,0:T(8,128)(2,1)S(1)}, u32[]{:S(2)}, u32[]{:S(2)}) collective-permute-start(bf16[256,256]{1,0:T(8,128)(2,1)S(1)} %constant_dynamic-update-slice_fusion.refs_1_), channel_id=1, source_target_pairs={{0,4},{1,5},{2,6},{3,7},{4,8},{5,9},{6,10},{7,11},{8,12},{9,13},{1... | collective-permute-start | bytes 393224 | tf_op jit(solution)/shard_map/ppermute | solution.py:362
  11.4 1.6 %collective-permute-start.11 = (bf16[128,640]{1,0:T(8,128)(2,1)S(1)}, bf16[128,640]{1,0:T(8,128)(2,1)S(1)}, u32[]{:S(2)}, u32[]{:S(2)}) collective-permute-start(bf16[128,640]{1,0:T(8,128)(2,1)S(1)} %get-tuple-element.71), channel_id=1, source_target_pairs={{0,3},{1,2},{2,1},{3,0},{4,7},{5,6},{6,5},{7,4},{8,11},{9,10},{10,... | collective-permute-start | bytes 491528 | tf_op jit(solution)/shard_map/ppermute | solution.py:340
  13.1 0.0 collective-permute-start.9
  13.1 0.7 %collective-permute-start.10 = (bf16[128,640]{1,0:T(8,128)(2,1)S(1)}, bf16[128,640]{1,0:T(8,128)(2,1)S(1)}, u32[]{:S(2)}, u32[]{:S(2)}) collective-permute-start(bf16[128,640]{1,0:T(8,128)(2,1)S(1)} %get-tuple-element.74), channel_id=1, source_target_pairs={{0,2},{1,3},{2,0},{3,1},{4,6},{5,7},{6,4},{7,5},{8,10},{9,11},{10,... | collective-permute-start | bytes 491528 | tf_op jit(solution)/shard_map/ppermute | solution.py:340
  13.8 0.0 collective-permute-done.1.refs_0_
  13.8 2.4 %collective-permute-start.2 = (bf16[256,256]{1,0:T(8,128)(2,1)S(1)}, bf16[256,256]{1,0:T(8,128)(2,1)S(1)}, u32[]{:S(2)}, u32[]{:S(2)}) collective-permute-start(bf16[256,256]{1,0:T(8,128)(2,1)S(1)} %collective-permute-done.1.refs_0_), channel_id=1, source_target_pairs={{4,8},{5,9},{6,10},{7,11},{8,12},{9,13},{10,14},{11,15},{20,24},{2... | collective-permute-start | bytes 393224 | tf_op jit(solution)/shard_map/ppermute | solution.py:362
  16.2 0.0 collective-permute-done.6.refs_1_
  16.2 1.9 %collective-permute-start.7 = (bf16[256,256]{1,0:T(8,128)(2,1)S(1)}, bf16[256,256]{1,0:T(8,128)(2,1)S(1)}, u32[]{:S(2)}, u32[]{:S(2)}) collective-permute-start(bf16[256,256]{1,0:T(8,128)(2,1)S(1)} %collective-permute-done.6.refs_1_), channel_id=1, source_target_pairs={{4,8},{5,9},{6,10},{7,11},{8,12},{9,13},{10,14},{11,15},{20,24},{2... | collective-permute-start | bytes 393224 | tf_op jit(solution)/shard_map/ppermute | solution.py:362
  18.1 0.1 constant_dynamic-slice_fusion
  18.2 0.0 collective-permute-done.11.refs_5_
  18.2 2.2 %collective-permute-start.14 = (bf16[128,640]{1,0:T(8,128)(2,1)S(1)}, bf16[128,640]{1,0:T(8,128)(2,1)S(1)}, u32[]{:S(2)}, u32[]{:S(2)}) collective-permute-start(bf16[128,640]{1,0:T(8,128)(2,1)S(1)} %get-tuple-element.67), channel_id=1, source_target_pairs={{0,3},{1,2},{2,1},{3,0},{4,7},{5,6},{6,5},{7,4},{8,11},{9,10},{10,... | collective-permute-start | bytes 491528 | tf_op jit(solution)/shard_map/ppermute | solution.py:340
  20.4 0.0 collective-permute-done.9.refs_3_
  20.4 0.0 collective-permute-start.12
  20.4 1.1 %collective-permute-done.10.refs_4_ = bf16[128,640]{1,0:T(8,128)(2,1)S(1)} collective-permute-done((bf16[128,640]{1,0:T(8,128)(2,1)S(1)}, bf16[128,640]{1,0:T(8,128)(2,1)S(1)}, u32[]{:S(2)}, u32[]{:S(2)}) %collective-permute-start.10) | collective-permute-done | bytes 163872 | tf_op jit(solution)/shard_map/ppermute | solution.py:340
  21.6 0.6 collective-permute-start.13
  22.2 0.0 collective-permute-done.2.refs_0_
  22.2 0.7 collective-permute-start.3
  22.8 0.0 collective-permute-done.7.refs_1_
  22.8 0.7 collective-permute-start.8
  23.5 2.0 %shard_map.67 = (f32[5,8,512]{2,1,0:T(8,128)S(1)}, f32[5,136,512]{2,1,0:T(8,128)S(1)}) custom-call(bf16[256,256]{1,0:T(8,128)(2,1)S(1)} %pad_maximum_fusion.refs_0_, bf16[256,256]{1,0:T(8,128)(2,1)S(1)} %constant_dynamic-update-slice_fusion.refs_1_, bf16[128,640]{1,0:T(8,128)(2,1)S(1)} %get-tuple-element.73.refs_2_, ...), custom_call_target="tpu_custom_call" | custom-call | flops 134217728 | tf_op jit(solution)/shard_map/pallas_call | solution.py:247
  25.5 1.9 %shard_map.68 = (f32[5,8,512]{2,1,0:T(8,128)S(1)}, f32[5,136,512]{2,1,0:T(8,128)S(1)}) custom-call(bf16[256,256]{1,0:T(8,128)(2,1)S(1)} %collective-permute-done.1.refs_0_, bf16[256,256]{1,0:T(8,128)(2,1)S(1)} %collective-permute-done.6.refs_1_, bf16[128,640]{1,0:T(8,128)(2,1)S(1)} %get-tuple-element.73.refs_2_, ...), custom_call_target="tpu_custom_call" | custom-call | flops 134217728 | tf_op jit(solution)/shard_map/pallas_call | solution.py:247
  27.4 0.0 collective-permute-done.14.refs_9_
  27.4 0.0 collective-permute-done.12.refs_7_
  27.4 1.3 %collective-permute-done.13.refs_8_ = bf16[128,640]{1,0:T(8,128)(2,1)S(1)} collective-permute-done((bf16[128,640]{1,0:T(8,128)(2,1)S(1)}, bf16[128,640]{1,0:T(8,128)(2,1)S(1)}, u32[]{:S(2)}, u32[]{:S(2)}) %collective-permute-start.13) | collective-permute-done | bytes 163872 | tf_op jit(solution)/shard_map/ppermute | solution.py:340
  28.7 0.3 shard_map.69
  29.1 0.0 collective-permute-done.3.refs_0_
  29.1 0.0 collective-permute-done.8.refs_1_
  29.1 0.7 collective-permute-start.15
  29.8 3.4 %shard_map.71 = (bf16[512,256]{1,0:T(8,128)(2,1)S(1)}, f32[5,128,512]{2,1,0:T(8,128)S(1)}) custom-call(bf16[256,256]{1,0:T(8,128)(2,1)S(1)} %collective-permute-done.1.refs_0_, bf16[256,256]{1,0:T(8,128)(2,1)S(1)} %collective-permute-done.6.refs_1_, bf16[128,640]{1,0:T(8,128)(2,1)S(1)} %get-tuple-element.73.refs_2_, ...), custom_call_target="tpu_custom_call" | custom-call | flops 335544320 | tf_op jit(solution)/shard_map/pallas_call | solution.py:247
  33.2 3.4 %shard_map.72 = (f32[512,256]{1,0:T(8,128)S(1)}, bf16[128,640]{1,0:T(8,128)(2,1)S(1)}, bf16[128,640]{1,0:T(8,128)(2,1)S(1)}, bf16[128,640]{1,0:T(8,128)(2,1)S(1)}, bf16[128,640]{1,0:T(8,128)(2,1)S(1)}) custom-call(bf16[256,256]{1,0:T(8,128)(2,1)S(1)} %pad_maximum_fusion.refs_0_, bf16[256,256]{1,0:T(8,128)(2,1)S(1)} %constant_dynamic-update-slice_fusion.refs_1_, ...), custom_call_target="tpu_custom_call" | custom-call | flops 335544320 | tf_op jit(solution)/shard_map/pallas_call | solution.py:247
  36.6 1.9 %collective-permute-start.16 = (bf16[512,256]{1,0:T(8,128)(2,1)S(1)}, bf16[512,256]{1,0:T(8,128)(2,1)S(1)}, u32[]{:S(2)}, u32[]{:S(2)}) collective-permute-start(bf16[512,256]{1,0:T(8,128)(2,1)S(1)} %get-tuple-element.59), channel_id=1, source_target_pairs={{4,0},{5,1},{6,2},{7,3},{8,4},{9,5},{10,6},{11,7},{20,16},{21,17},... | collective-permute-start | bytes 786440 | tf_op jit(solution)/shard_map/ppermute | solution.py:393
  38.6 0.7 collective-permute-start.17
  39.3 0.2 shard_map.75
  39.6 0.7 collective-permute-start.22
  40.3 1.3 %collective-permute-start.21 = (bf16[512,256]{1,0:T(8,128)(2,1)S(1)}, bf16[512,256]{1,0:T(8,128)(2,1)S(1)}, u32[]{:S(2)}, u32[]{:S(2)}) collective-permute-start(bf16[512,256]{1,0:T(8,128)(2,1)S(1)} %get-tuple-element.65), channel_id=1, source_target_pairs={{12,4},{13,5},{14,6},{15,7},{28,20},{29,21},{30,22},{31,23}} | collective-permute-start | bytes 786440 | tf_op jit(solution)/shard_map/ppermute | solution.py:393
  41.6 0.0 collective-permute-done.15
  41.6 0.1 shard_map.77
  41.7 0.9 %collective-permute-start.19 = (bf16[128,640]{1,0:T(8,128)(2,1)S(1)}, bf16[128,640]{1,0:T(8,128)(2,1)S(1)}, u32[]{:S(2)}, u32[]{:S(2)}) collective-permute-start(bf16[128,640]{1,0:T(8,128)(2,1)S(1)} %get-tuple-element.62), channel_id=1, source_target_pairs={{0,2},{1,3},{2,0},{3,1},{4,6},{5,7},{6,4},{7,5},{8,10},{9,11},{10,... | collective-permute-start | bytes 491528 | tf_op jit(solution)/shard_map/ppermute | solution.py:340
  42.6 10.7 %collective-permute-done.16 = bf16[512,256]{1,0:T(8,128)(2,1)S(1)} collective-permute-done((bf16[512,256]{1,0:T(8,128)(2,1)S(1)}, bf16[512,256]{1,0:T(8,128)(2,1)S(1)}, u32[]{:S(2)}, u32[]{:S(2)}) %collective-permute-start.16) | collective-permute-done | bytes 262176 | tf_op jit(solution)/shard_map/ppermute | solution.py:393
  53.3 3.4 %collective-permute-start.20 = (bf16[128,640]{1,0:T(8,128)(2,1)S(1)}, bf16[128,640]{1,0:T(8,128)(2,1)S(1)}, u32[]{:S(2)}, u32[]{:S(2)}) collective-permute-start(bf16[128,640]{1,0:T(8,128)(2,1)S(1)} %get-tuple-element.63), channel_id=1, source_target_pairs={{0,3},{1,2},{2,1},{3,0},{4,7},{5,6},{6,5},{7,4},{8,11},{9,10},{10,... | collective-permute-start | bytes 491528 | tf_op jit(solution)/shard_map/ppermute | solution.py:340
  56.7 0.0 collective-permute-done.17
  56.7 0.0 collective-permute-start.18
  56.7 0.0 collective-permute-done.22
  56.7 2.0 %collective-permute-done.21 = bf16[512,256]{1,0:T(8,128)(2,1)S(1)} collective-permute-done((bf16[512,256]{1,0:T(8,128)(2,1)S(1)}, bf16[512,256]{1,0:T(8,128)(2,1)S(1)}, u32[]{:S(2)}, u32[]{:S(2)}) %collective-permute-start.21) | collective-permute-done | bytes 262176 | tf_op jit(solution)/shard_map/ppermute | solution.py:393
  58.8 0.2 add_convert_fusion
  59.0 3.4 %collective-permute-start.25 = (bf16[128,256]{1,0:T(8,128)(2,1)S(1)}, bf16[128,256]{1,0:T(8,128)(2,1)S(1)}, u32[]{:S(2)}, u32[]{:S(2)}) collective-permute-start(bf16[128,256]{1,0:T(8,128)(2,1)S(1)} %get-tuple-element.75), channel_id=1, source_target_pairs={{0,3},{1,2},{2,1},{3,0},{4,7},{5,6},{6,5},{7,4},{8,11},{9,10},{10,... | collective-permute-start | bytes 196616 | tf_op jit(solution)/shard_map/ppermute | solution.py:340
  62.4 0.6 collective-permute-start.24
  63.0 2.0 %collective-permute-done.25.refs_7_ = bf16[128,256]{1,0:T(8,128)(2,1)S(1)} collective-permute-done((bf16[128,256]{1,0:T(8,128)(2,1)S(1)}, bf16[128,256]{1,0:T(8,128)(2,1)S(1)}, u32[]{:S(2)}, u32[]{:S(2)}) %collective-permute-start.25) | collective-permute-done | bytes 65568 | tf_op jit(solution)/shard_map/ppermute | solution.py:340
  65.0 1.1 %collective-permute-start.23 = (bf16[128,256]{1,0:T(8,128)(2,1)S(1)}, bf16[128,256]{1,0:T(8,128)(2,1)S(1)}, u32[]{:S(2)}, u32[]{:S(2)}) collective-permute-start(bf16[128,256]{1,0:T(8,128)(2,1)S(1)} %get-tuple-element.77), channel_id=1, source_target_pairs={{0,1},{1,0},{2,3},{3,2},{4,5},{5,4},{6,7},{7,6},{8,9},{9,8},{10,11... | collective-permute-start | bytes 196616 | tf_op jit(solution)/shard_map/ppermute | solution.py:340
  66.1 0.4 collective-permute-done.24.refs_6_
  66.5 0.5 collective-permute-done.23.refs_5_
  67.0 0.0 collective-permute-done.19.refs_2_
  67.0 0.0 collective-permute-done.20.refs_3_
  67.0 0.0 collective-permute-done.18.refs_1_
  67.0 1.0 %shard_map.78 = (bf16[128,2560]{1,0:T(8,128)(2,1)}, bf16[128,512]{1,0:T(8,128)(2,1)}, bf16[128,512]{1,0:T(8,128)(2,1)}) custom-call(bf16[128,640]{1,0:T(8,128)(2,1)S(1)} %get-tuple-element.57.refs_0_, bf16[128,640]{1,0:T(8,128)(2,1)S(1)} %collective-permute-done.18.refs_1_, bf16[128,640]{1,0:T(8,128)(2,1)S(1)} %collective-permute-done.19.refs_2_, ...), custom_call_target="tpu_custom_call" | custom-call | tf_op jit(solution)/shard_map/pallas_call | solution.py:247
  (15 shorter events, 0.2 us)
Async XLA Ops:
  0.6 3.6 %copy-start = (bf16[128,2560]{1,0:T(8,128)(2,1)S(1)}, bf16[128,2560]{1,0:T(8,128)(2,1)}, u32[]{:S(2)}) copy-start(bf16[128,2560]{1,0:T(8,128)(2,1)} %param.4) | copy-start | bytes 1966084
  0.7 17.4 %copy-start.1 = (bf16[128,2560]{1,0:T(8,128)(2,1)S(1)}, bf16[128,2560]{1,0:T(8,128)(2,1)}, u32[]{:S(2)}) copy-start(bf16[128,2560]{1,0:T(8,128)(2,1)} %param.7) | copy-start | bytes 1966084
  1.7 6.5 %collective-permute-start.4 = (bf16[128,256]{1,0:T(8,128)(2,1)S(1)}, bf16[128,256]{1,0:T(8,128)(2,1)S(1)}, u32[]{:S(2)}, u32[]{:S(2)}) collective-permute-start(bf16[128,256]{1,0:T(8,128)(2,1)S(1)} %pad_maximum_fusion.2), channel_id=1, source_target_pairs={{0,2},{1,3},{2,0},{3,1},{4,6},{5,7},{6,4},{7,5},{8,10},{9,11},{10,... | collective-permute-start | bytes 196616 | tf_op jit(solution)/shard_map/ppermute | solution.py:340
  3.0 1.9 %collective-permute-start = (bf16[128,256]{1,0:T(8,128)(2,1)S(1)}, bf16[128,256]{1,0:T(8,128)(2,1)S(1)}, u32[]{:S(2)}, u32[]{:S(2)}) collective-permute-start(bf16[128,256]{1,0:T(8,128)(2,1)S(1)} %pad_maximum_fusion.1), channel_id=1, source_target_pairs={{0,1},{1,0},{2,3},{3,2},{4,5},{5,4},{6,7},{7,6},{8,9},{9,8},{10,11... | collective-permute-start | bytes 196616 | tf_op jit(solution)/shard_map/ppermute | solution.py:340
  4.1 4.1 %collective-permute-start.5 = (bf16[128,256]{1,0:T(8,128)(2,1)S(1)}, bf16[128,256]{1,0:T(8,128)(2,1)S(1)}, u32[]{:S(2)}, u32[]{:S(2)}) collective-permute-start(bf16[128,256]{1,0:T(8,128)(2,1)S(1)} %pad_maximum_fusion.3), channel_id=1, source_target_pairs={{0,3},{1,2},{2,1},{3,0},{4,7},{5,6},{6,5},{7,4},{8,11},{9,10},{10,... | collective-permute-start | bytes 196616 | tf_op jit(solution)/shard_map/ppermute | solution.py:340
  5.0 8.8 %collective-permute-start.1 = (bf16[256,256]{1,0:T(8,128)(2,1)S(1)}, bf16[256,256]{1,0:T(8,128)(2,1)S(1)}, u32[]{:S(2)}, u32[]{:S(2)}) collective-permute-start(bf16[256,256]{1,0:T(8,128)(2,1)S(1)} %pad_maximum_fusion.refs_0_), channel_id=1, source_target_pairs={{0,4},{1,5},{2,6},{3,7},{4,8},{5,9},{6,10},{7,11},{8,12},{9,13},{1... | collective-permute-start | bytes 393224 | tf_op jit(solution)/shard_map/ppermute | solution.py:362
  8.2 8.0 %collective-permute-start.6 = (bf16[256,256]{1,0:T(8,128)(2,1)S(1)}, bf16[256,256]{1,0:T(8,128)(2,1)S(1)}, u32[]{:S(2)}, u32[]{:S(2)}) collective-permute-start(bf16[256,256]{1,0:T(8,128)(2,1)S(1)} %constant_dynamic-update-slice_fusion.refs_1_), channel_id=1, source_target_pairs={{0,4},{1,5},{2,6},{3,7},{4,8},{5,9},{6,10},{7,11},{8,12},{9,13},{1... | collective-permute-start | bytes 393224 | tf_op jit(solution)/shard_map/ppermute | solution.py:362
  11.4 6.8 %collective-permute-start.11 = (bf16[128,640]{1,0:T(8,128)(2,1)S(1)}, bf16[128,640]{1,0:T(8,128)(2,1)S(1)}, u32[]{:S(2)}, u32[]{:S(2)}) collective-permute-start(bf16[128,640]{1,0:T(8,128)(2,1)S(1)} %get-tuple-element.71), channel_id=1, source_target_pairs={{0,3},{1,2},{2,1},{3,0},{4,7},{5,6},{6,5},{7,4},{8,11},{9,10},{10,... | collective-permute-start | bytes 491528 | tf_op jit(solution)/shard_map/ppermute | solution.py:340
  13.1 7.4 %collective-permute-start.9 = (bf16[128,640]{1,0:T(8,128)(2,1)S(1)}, bf16[128,640]{1,0:T(8,128)(2,1)S(1)}, u32[]{:S(2)}, u32[]{:S(2)}) collective-permute-start(bf16[128,640]{1,0:T(8,128)(2,1)S(1)} %get-tuple-element.72), channel_id=1, source_target_pairs={{0,1},{1,0},{2,3},{3,2},{4,5},{5,4},{6,7},{7,6},{8,9},{9,8},{10,11... | collective-permute-start | bytes 491528 | tf_op jit(solution)/shard_map/ppermute | solution.py:340
  13.1 8.5 %collective-permute-start.10 = (bf16[128,640]{1,0:T(8,128)(2,1)S(1)}, bf16[128,640]{1,0:T(8,128)(2,1)S(1)}, u32[]{:S(2)}, u32[]{:S(2)}) collective-permute-start(bf16[128,640]{1,0:T(8,128)(2,1)S(1)} %get-tuple-element.74), channel_id=1, source_target_pairs={{0,2},{1,3},{2,0},{3,1},{4,6},{5,7},{6,4},{7,5},{8,10},{9,11},{10,... | collective-permute-start | bytes 491528 | tf_op jit(solution)/shard_map/ppermute | solution.py:340
  13.8 8.4 %collective-permute-start.2 = (bf16[256,256]{1,0:T(8,128)(2,1)S(1)}, bf16[256,256]{1,0:T(8,128)(2,1)S(1)}, u32[]{:S(2)}, u32[]{:S(2)}) collective-permute-start(bf16[256,256]{1,0:T(8,128)(2,1)S(1)} %collective-permute-done.1.refs_0_), channel_id=1, source_target_pairs={{4,8},{5,9},{6,10},{7,11},{8,12},{9,13},{10,14},{11,15},{20,24},{2... | collective-permute-start | bytes 393224 | tf_op jit(solution)/shard_map/ppermute | solution.py:362
  16.2 6.6 %collective-permute-start.7 = (bf16[256,256]{1,0:T(8,128)(2,1)S(1)}, bf16[256,256]{1,0:T(8,128)(2,1)S(1)}, u32[]{:S(2)}, u32[]{:S(2)}) collective-permute-start(bf16[256,256]{1,0:T(8,128)(2,1)S(1)} %collective-permute-done.6.refs_1_), channel_id=1, source_target_pairs={{4,8},{5,9},{6,10},{7,11},{8,12},{9,13},{10,14},{11,15},{20,24},{2... | collective-permute-start | bytes 393224 | tf_op jit(solution)/shard_map/ppermute | solution.py:362
  18.2 9.2 %collective-permute-start.14 = (bf16[128,640]{1,0:T(8,128)(2,1)S(1)}, bf16[128,640]{1,0:T(8,128)(2,1)S(1)}, u32[]{:S(2)}, u32[]{:S(2)}) collective-permute-start(bf16[128,640]{1,0:T(8,128)(2,1)S(1)} %get-tuple-element.67), channel_id=1, source_target_pairs={{0,3},{1,2},{2,1},{3,0},{4,7},{5,6},{6,5},{7,4},{8,11},{9,10},{10,... | collective-permute-start | bytes 491528 | tf_op jit(solution)/shard_map/ppermute | solution.py:340
  20.4 7.0 %collective-permute-start.12 = (bf16[128,640]{1,0:T(8,128)(2,1)S(1)}, bf16[128,640]{1,0:T(8,128)(2,1)S(1)}, u32[]{:S(2)}, u32[]{:S(2)}) collective-permute-start(bf16[128,640]{1,0:T(8,128)(2,1)S(1)} %get-tuple-element.68), channel_id=1, source_target_pairs={{0,1},{1,0},{2,3},{3,2},{4,5},{5,4},{6,7},{7,6},{8,9},{9,8},{10,11... | collective-permute-start | bytes 491528 | tf_op jit(solution)/shard_map/ppermute | solution.py:340
  21.6 7.1 %collective-permute-start.13 = (bf16[128,640]{1,0:T(8,128)(2,1)S(1)}, bf16[128,640]{1,0:T(8,128)(2,1)S(1)}, u32[]{:S(2)}, u32[]{:S(2)}) collective-permute-start(bf16[128,640]{1,0:T(8,128)(2,1)S(1)} %get-tuple-element.70), channel_id=1, source_target_pairs={{0,2},{1,3},{2,0},{3,1},{4,6},{5,7},{6,4},{7,5},{8,10},{9,11},{10,... | collective-permute-start | bytes 491528 | tf_op jit(solution)/shard_map/ppermute | solution.py:340
  22.2 6.9 %collective-permute-start.3 = (bf16[256,256]{1,0:T(8,128)(2,1)S(1)}, bf16[256,256]{1,0:T(8,128)(2,1)S(1)}, u32[]{:S(2)}, u32[]{:S(2)}) collective-permute-start(bf16[256,256]{1,0:T(8,128)(2,1)S(1)} %collective-permute-done.2.refs_0_), channel_id=1, source_target_pairs={{8,12},{9,13},{10,14},{11,15},{24,28},{25,29},{26,30},{27,31}} | collective-permute-start | bytes 393224 | tf_op jit(solution)/shard_map/ppermute | solution.py:362
  22.8 6.2 %collective-permute-start.8 = (bf16[256,256]{1,0:T(8,128)(2,1)S(1)}, bf16[256,256]{1,0:T(8,128)(2,1)S(1)}, u32[]{:S(2)}, u32[]{:S(2)}) collective-permute-start(bf16[256,256]{1,0:T(8,128)(2,1)S(1)} %collective-permute-done.7.refs_1_), channel_id=1, source_target_pairs={{8,12},{9,13},{10,14},{11,15},{24,28},{25,29},{26,30},{27,31}} | collective-permute-start | bytes 393224 | tf_op jit(solution)/shard_map/ppermute | solution.py:362
  29.1 12.4 %collective-permute-start.15 = (bf16[512,256]{1,0:T(8,128)(2,1)S(1)}, bf16[512,256]{1,0:T(8,128)(2,1)S(1)}, u32[]{:S(2)}, u32[]{:S(2)}) collective-permute-start(bf16[512,256]{1,0:T(8,128)(2,1)S(1)} %get-tuple-element.42), channel_id=1, source_target_pairs={{8,0},{9,1},{10,2},{11,3},{24,16},{25,17},{26,18},{27,19}} | collective-permute-start | bytes 786440 | tf_op jit(solution)/shard_map/ppermute | solution.py:393
  36.6 16.7 %collective-permute-start.16 = (bf16[512,256]{1,0:T(8,128)(2,1)S(1)}, bf16[512,256]{1,0:T(8,128)(2,1)S(1)}, u32[]{:S(2)}, u32[]{:S(2)}) collective-permute-start(bf16[512,256]{1,0:T(8,128)(2,1)S(1)} %get-tuple-element.59), channel_id=1, source_target_pairs={{4,0},{5,1},{6,2},{7,3},{8,4},{9,5},{10,6},{11,7},{20,16},{21,17},... | collective-permute-start | bytes 786440 | tf_op jit(solution)/shard_map/ppermute | solution.py:393
  38.6 18.1 %collective-permute-start.17 = (bf16[512,256]{1,0:T(8,128)(2,1)S(1)}, bf16[512,256]{1,0:T(8,128)(2,1)S(1)}, u32[]{:S(2)}, u32[]{:S(2)}) collective-permute-start(bf16[512,256]{1,0:T(8,128)(2,1)S(1)} %get-tuple-element.60), channel_id=1, source_target_pairs={{12,0},{13,1},{14,2},{15,3},{28,16},{29,17},{30,18},{31,19}} | collective-permute-start | bytes 786440 | tf_op jit(solution)/shard_map/ppermute | solution.py:393
  39.6 17.1 %collective-permute-start.22 = (bf16[512,256]{1,0:T(8,128)(2,1)S(1)}, bf16[512,256]{1,0:T(8,128)(2,1)S(1)}, u32[]{:S(2)}, u32[]{:S(2)}) collective-permute-start(bf16[512,256]{1,0:T(8,128)(2,1)S(1)} %get-tuple-element.66), channel_id=1, source_target_pairs={{12,8},{13,9},{14,10},{15,11},{28,24},{29,25},{30,26},{31,27}} | collective-permute-start | bytes 786440 | tf_op jit(solution)/shard_map/ppermute | solution.py:393
  40.3 18.5 %collective-permute-start.21 = (bf16[512,256]{1,0:T(8,128)(2,1)S(1)}, bf16[512,256]{1,0:T(8,128)(2,1)S(1)}, u32[]{:S(2)}, u32[]{:S(2)}) collective-permute-start(bf16[512,256]{1,0:T(8,128)(2,1)S(1)} %get-tuple-element.65), channel_id=1, source_target_pairs={{12,4},{13,5},{14,6},{15,7},{28,20},{29,21},{30,22},{31,23}} | collective-permute-start | bytes 786440 | tf_op jit(solution)/shard_map/ppermute | solution.py:393
  41.7 25.3 %collective-permute-start.19 = (bf16[128,640]{1,0:T(8,128)(2,1)S(1)}, bf16[128,640]{1,0:T(8,128)(2,1)S(1)}, u32[]{:S(2)}, u32[]{:S(2)}) collective-permute-start(bf16[128,640]{1,0:T(8,128)(2,1)S(1)} %get-tuple-element.62), channel_id=1, source_target_pairs={{0,2},{1,3},{2,0},{3,1},{4,6},{5,7},{6,4},{7,5},{8,10},{9,11},{10,... | collective-permute-start | bytes 491528 | tf_op jit(solution)/shard_map/ppermute | solution.py:340
  53.3 13.7 %collective-permute-start.20 = (bf16[128,640]{1,0:T(8,128)(2,1)S(1)}, bf16[128,640]{1,0:T(8,128)(2,1)S(1)}, u32[]{:S(2)}, u32[]{:S(2)}) collective-permute-start(bf16[128,640]{1,0:T(8,128)(2,1)S(1)} %get-tuple-element.63), channel_id=1, source_target_pairs={{0,3},{1,2},{2,1},{3,0},{4,7},{5,6},{6,5},{7,4},{8,11},{9,10},{10,... | collective-permute-start | bytes 491528 | tf_op jit(solution)/shard_map/ppermute | solution.py:340
  56.7 10.3 %collective-permute-start.18 = (bf16[128,640]{1,0:T(8,128)(2,1)S(1)}, bf16[128,640]{1,0:T(8,128)(2,1)S(1)}, u32[]{:S(2)}, u32[]{:S(2)}) collective-permute-start(bf16[128,640]{1,0:T(8,128)(2,1)S(1)} %get-tuple-element.61), channel_id=1, source_target_pairs={{0,1},{1,0},{2,3},{3,2},{4,5},{5,4},{6,7},{7,6},{8,9},{9,8},{10,11... | collective-permute-start | bytes 491528 | tf_op jit(solution)/shard_map/ppermute | solution.py:340
  59.0 6.0 %collective-permute-start.25 = (bf16[128,256]{1,0:T(8,128)(2,1)S(1)}, bf16[128,256]{1,0:T(8,128)(2,1)S(1)}, u32[]{:S(2)}, u32[]{:S(2)}) collective-permute-start(bf16[128,256]{1,0:T(8,128)(2,1)S(1)} %get-tuple-element.75), channel_id=1, source_target_pairs={{0,3},{1,2},{2,1},{3,0},{4,7},{5,6},{6,5},{7,4},{8,11},{9,10},{10,... | collective-permute-start | bytes 196616 | tf_op jit(solution)/shard_map/ppermute | solution.py:340
  62.4 4.1 %collective-permute-start.24 = (bf16[128,256]{1,0:T(8,128)(2,1)S(1)}, bf16[128,256]{1,0:T(8,128)(2,1)S(1)}, u32[]{:S(2)}, u32[]{:S(2)}) collective-permute-start(bf16[128,256]{1,0:T(8,128)(2,1)S(1)} %get-tuple-element.76), channel_id=1, source_target_pairs={{0,2},{1,3},{2,0},{3,1},{4,6},{5,7},{6,4},{7,5},{8,10},{9,11},{10,... | collective-permute-start | bytes 196616 | tf_op jit(solution)/shard_map/ppermute | solution.py:340
  65.0 2.0 %collective-permute-start.23 = (bf16[128,256]{1,0:T(8,128)(2,1)S(1)}, bf16[128,256]{1,0:T(8,128)(2,1)S(1)}, u32[]{:S(2)}, u32[]{:S(2)}) collective-permute-start(bf16[128,256]{1,0:T(8,128)(2,1)S(1)} %get-tuple-element.77), channel_id=1, source_target_pairs={{0,1},{1,0},{2,3},{3,2},{4,5},{5,4},{6,7},{7,6},{8,9},{9,8},{10,11... | collective-permute-start | bytes 196616 | tf_op jit(solution)/shard_map/ppermute | solution.py:340
